TPU v7x, 32 devices: a whole 2x2x4 slice. The times are simulated.
32 devices in a mesh: wl: 4 (over y, x), cell: 8 (over z, core).
Axes of the slice: x: 2, y: 2, z: 4, core: 2. Of those that a mesh axis runs over, the one named last changes fastest.
Arguments:
- interfaces: float32 [8, 3, 2, 128, 128], replicated, may hold values from -0.10606602 to 1.006066
- cell_profile: int32 [64], P('cell'), may hold values from 0 to 3
- cell_section: int32 [64], P('cell'), may hold values from 0 to 7
- mode_loss: float32 [4, 128], replicated, may hold values from 0.985 to 1
- phase: float32 [4, 4, 128], P(None, 'wl'), may hold values from -3.140625 to 3.140625
- mode_field: float32 [4, 128, 4096], P(None, None, 'wl'), may hold values from -0.5 to 0.5
- target: float32 [4, 2, 128, 128], P('wl'), may hold values from -0.5 to 0.5
Outputs:
- reflection: float32 [4, 2, 128, 128], P('wl', None, 'cell')
- gradient: float32 [64, 4096], P('cell', 'wl')
All inputs are finite; a program needn't handle non-finite values.
Results may differ from a plain program's by a relative error of at most 0.0003.
Values sent between devices are 32-bit elements; how exact they have to be, the bound alone decides.
No kernel may reach another device: no remote copies, remote signals or barrier semaphores. Data moves between devices by JAX's collectives and lax.ppermute only.
A program may use at most 128 MiB of HBM per device.

v0:
```python
import jax
import jax.numpy as jnp
from jax import lax
from jax.experimental import pallas as pl
from jax.experimental.pallas import tpu as pltpu
from jax.sharding import PartitionSpec as P

F32 = jnp.float32
BF16 = jnp.bfloat16
MIB = 1024 * 1024
SHIFT = 8
REFL, TRANS, BACK = 0, 1, 2


def split(x):
    hi = x.astype(BF16)
    lo = (x - hi.astype(F32)).astype(BF16)
    return hi, lo


def whole(pair):
    return pair[0].astype(F32) + pair[1].astype(F32)


def expand(h):
    m = h.shape[0]
    return jnp.concatenate([h, jnp.concatenate([-h[:, m:], h[:, :m]], axis=1)], axis=0)


def right(pair):
    return expand(pair[0]), expand(pair[1])


def dot(a, b):
    return jnp.dot(a, b, preferred_element_type=F32)


def mul(left, weights):
    hi, lo = left
    m = hi.shape[0]
    both = dot(jnp.concatenate([hi, lo], axis=0), weights[0])
    return both[:m] + both[m:] + dot(hi, weights[1])


def get(ref, *at):
    return ref[(*at, 0)], ref[(*at, 1)]


def keep(ref, pair, *at):
    ref[(*at, 0)], ref[(*at, 1)] = pair


def unit(m):
    row = lax.broadcasted_iota(jnp.int32, (m, 2 * m), 0)
    col = lax.broadcasted_iota(jnp.int32, (m, 2 * m), 1)
    return jnp.where(row == col, 1.0, 0.0).astype(F32)


def merge(former, latter):
    r1, t1, b1 = former
    r2, t2, b2 = latter
    t1w = right(t1)
    z = mul(b1, right(r2))
    back = mul(b1, right(b2))
    trans = mul(t2, t1w)
    refl = whole(r1) + mul(split(z), t1w)
    return split(refl), split(trans), split(back)


def merge_end(former, latter):
    r1, t1, b1 = former
    t1w = right(t1)
    z = mul(b1, right(latter[0]))
    trans = mul(latter[1], t1w)
    return split(whole(r1) + mul(split(z), t1w)), split(trans)


def triple(ref, *at):
    return tuple(get(ref, *at, kind) for kind in range(3))


def keep_triple(ref, values, *at):
    for kind in range(3):
        keep(ref, values[kind], *at, kind)


def split_triple(ref, *at):
    return tuple(split(ref[(*at, kind)]) for kind in range(3))


def propagation(loss_ref, phase_ref, row_ref, col_ref):
    m = loss_ref.shape[1]
    amp = loss_ref[...]
    angle = phase_ref[...]
    for part, values in enumerate((amp * jnp.cos(angle), amp * jnp.sin(angle))):
        for q in range(loss_ref.shape[0]):
            wide = jnp.broadcast_to(values[q : q + 1], (m, m))
            row_ref[q, part] = wide[:8]
            col_ref[q, part] = wide.T


def trans_leaf(lib_ref, col_ref, code):
    q, s = code >> SHIFT, code & ((1 << SHIFT) - 1)
    re, im = lib_ref[s, TRANS, 0], lib_ref[s, TRANS, 1]
    cr, ci = col_ref[q, 0], col_ref[q, 1]
    return split(jnp.concatenate([cr * re - ci * im, cr * im + ci * re], axis=1))


def back_leaf(lib_ref, row_ref, code):
    q, s = code >> SHIFT, code & ((1 << SHIFT) - 1)
    re, im = lib_ref[s, BACK, 0], lib_ref[s, BACK, 1]
    rr, ri = row_ref[q, 0][:1], row_ref[q, 1][:1]
    return split(jnp.concatenate([re * rr - im * ri, re * ri + im * rr], axis=1))


def refl_leaf(lib_ref, code):
    s = code & ((1 << SHIFT) - 1)
    return split(jnp.concatenate([lib_ref[s, REFL, 0], lib_ref[s, REFL, 1]], axis=1))


def leaf(lib_ref, row_ref, col_ref, code):
    return (
        refl_leaf(lib_ref, code),
        trans_leaf(lib_ref, col_ref, code),
        back_leaf(lib_ref, row_ref, code),
    )


def own_kernel(code_ref, lib_ref, loss_ref, phase_ref, nodes_ref, own_ref, row_ref, col_ref):
    cells = code_ref.shape[0]
    propagation(loss_ref, phase_ref, row_ref, col_ref)
    pairs = []
    for j in range(cells // 2):
        pairs.append(
            merge(
                leaf(lib_ref, row_ref, col_ref, code_ref[2 * j]),
                leaf(lib_ref, row_ref, col_ref, code_ref[2 * j + 1]),
            )
        )
        keep_triple(nodes_ref, pairs[j], j)
    fours = []
    for j in range(cells // 4):
        fours.append(merge(pairs[2 * j], pairs[2 * j + 1]))
        keep_triple(nodes_ref, fours[j], cells // 2 + j)
    top = merge(*fours)
    for kind in range(3):
        own_ref[kind] = whole(top[kind])


def scan_kernel(
    code_ref, lib_ref, loss_ref, phase_ref, nodes_ref, own_ref,
    grown_ref, back_ref, trans_ref,
    row_ref, col_ref,
):
    cells = code_ref.shape[0]
    m = loss_ref.shape[1]
    propagation(loss_ref, phase_ref, row_ref, col_ref)

    def cell(i):
        return leaf(lib_ref, row_ref, col_ref, code_ref[i])

    def put(i, values):
        keep(trans_ref, values[TRANS], i)
        keep(back_ref, values[BACK], i)
        return values

    def grow(i, refl, before):
        keep(grown_ref, split(whole(before) + mul(refl, right(before))), i)

    def trans_of(i):
        return trans_leaf(lib_ref, col_ref, code_ref[i])

    suffix4 = put(4, triple(nodes_ref, 5))
    before2 = get(nodes_ref, 0, TRANS)
    before4 = get(nodes_ref, 4, TRANS)
    suffix2 = put(2, merge(triple(nodes_ref, 1), suffix4))
    suffix3 = put(3, merge(cell(3), suffix4))
    before3 = split(mul(trans_of(2), right(before2)))
    grow(3, suffix3[REFL], before3)
    grow(2, suffix2[REFL], before2)
    grow(4, suffix4[REFL], before4)
    suffix1 = put(1, merge(cell(1), suffix2))
    before6 = split(mul(get(nodes_ref, 2, TRANS), right(before4)))
    suffix6 = put(6, triple(nodes_ref, 3))
    suffix5 = put(5, merge(cell(5), suffix6))
    grow(6, suffix6[REFL], before6)
    before5 = split(mul(trans_of(4), right(before4)))
    before7 = split(mul(trans_of(6), right(before6)))
    grow(5, suffix5[REFL], before5)
    suffix7 = put(7, cell(7))
    grow(7, suffix7[REFL], before7)
    grow(1, suffix1[REFL], trans_of(0))
    keep(grown_ref, split(unit(m) + own_ref[REFL]), 0)
    keep(trans_ref, split(own_ref[TRANS]), 0)
    keep(back_ref, split(own_ref[BACK]), 0)


def far_kernel(
    me_ref, code_ref, lib_ref, loss_ref, phase_ref, own_ref, out_ref,
    row_ref, col_ref, pairs_ref, fours_ref, acc_ref,
):
    blocks, cells = code_ref.shape
    m = loss_ref.shape[1]
    chips = blocks // 2
    chip = me_ref[0] >> 1
    core = me_ref[0] & 1
    right_count = chips - 1 - chip
    right_end = 2 * chip + 2 + (core + 1) * right_count
    left_end = (core + 1) * chip
    out_ref[0:3] = own_ref[...]
    propagation(loss_ref, phase_ref, row_ref, col_ref)
    eye = split(unit(m))
    none = (jnp.zeros_like(eye[0]), jnp.zeros_like(eye[0]))
    for side in range(2):
        keep_triple(acc_ref, (none, eye, eye), side)

    def place(i):
        on_right = i < right_count
        return jnp.where(on_right, right_end - 1 - i, left_end - 1 - (i - right_count)), on_right

    def pair_step(i, _):
        k, _ = place(i)
        for j in range(cells // 2):
            keep_triple(
                pairs_ref,
                merge(
                    leaf(lib_ref, row_ref, col_ref, code_ref[k, 2 * j]),
                    leaf(lib_ref, row_ref, col_ref, code_ref[k, 2 * j + 1]),
                ),
                i,
                j,
            )
        return 0

    lax.fori_loop(0, chips - 1, pair_step, 0)
    for i in range(chips - 1):
        for j in range(cells // 4):
            keep_triple(
                fours_ref, merge(triple(pairs_ref, i, 2 * j), triple(pairs_ref, i, 2 * j + 1)), i, j
            )
    for i in range(chips - 1):
        keep_triple(pairs_ref, merge(triple(fours_ref, i, 0), triple(fours_ref, i, 1)), i, 0)
    for i in range(chips - 1):
        side = jnp.where(i < right_count, 1, 0)
        first = (i == 0) | (i == right_count)

        @pl.when(first)
        def _():
            acc_ref[side] = pairs_ref[i, 0]

        @pl.when(jnp.logical_not(first))
        def _():
            keep_triple(acc_ref, merge(triple(pairs_ref, i, 0), triple(acc_ref, side)), side)

    for side in range(2):
        for kind in range(3):
            out_ref[3 + 3 * side + kind] = whole(get(acc_ref, side, kind))


OWN, LEFT, RIGHT = 0, 3, 6


def last_kernel(
    me_ref, target_ref, mine_ref, theirs_ref, grown_ref, back_ref, trans_ref,
    first_ref, second_ref, reflection_ref,
    s_ref, q_ref, left_ref,
):
    cells = grown_ref.shape[0]
    m = target_ref.shape[1]
    h = m // 2
    core = me_ref[0] & 1

    def part(ref, start):
        return tuple(split(ref[start + kind]) for kind in range(3))

    def join(zero_ref, one_ref):
        far = merge(part(zero_ref, LEFT), part(one_ref, LEFT))
        end = merge_end(part(zero_ref, RIGHT), part(one_ref, RIGHT))
        return far, end

    @pl.when(core == 0)
    def _():
        far, end = join(mine_ref, theirs_ref)
        s, q = merge_end(part(theirs_ref, OWN), end)
        keep(s_ref, s)
        keep(q_ref, q)
        for kind in range(3):
            left_ref[kind] = whole(far[kind])

    @pl.when(core == 1)
    def _():
        far, end = join(theirs_ref, mine_ref)
        far = merge(far, part(theirs_ref, OWN))
        keep(s_ref, end[0])
        keep(q_ref, end[1])
        for kind in range(3):
            left_ref[kind] = whole(far[kind])

    s, q = get(s_ref), get(q_ref)
    p = split(left_ref[TRANS])
    pw = right(p)
    block = right(get(trans_ref, 0))
    q_block = split(mul(q, block))
    s_block = split(mul(s, block))
    total = mul(q_block, pw)
    here = right(split(mine_ref[OWN + REFL] + mul(get(back_ref, 0), right(s_block))))
    rows = reflection_ref.shape[1]
    at = pl.ds(pl.multiple_of(me_ref[0] * rows, rows), rows)
    mine = mul(split(mul(split(left_ref[BACK, at, :]), here)), pw) + left_ref[REFL, at, :]
    reflection_ref[0] = mine[:, :m]
    reflection_ref[1] = mine[:, m:]
    miss = jnp.concatenate(
        [(total[:, :m] - target_ref[0]).T, (total[:, m:] - target_ref[1]).T], axis=1
    )
    ahead = split(mul(split(miss), right(q)))
    x1 = right(split(mul(p, right(ahead))))
    x2 = right(split(mul(s_block, x1)))
    row = lax.broadcasted_iota(jnp.int32, (h, m), 0)
    lane = lax.broadcasted_iota(jnp.int32, (h, m), 1)
    use_top = (lane >= h) | (row > lane)
    eye = lax.broadcasted_iota(jnp.int32, (m, m), 0) == lax.broadcasted_iota(jnp.int32, (m, m), 1)
    group = cells // 2
    for half, ref in enumerate((first_ref, second_ref)):
        ref[group * h :] = jnp.zeros_like(ref[group * h :])
        for j in range(group):
            i = half * group + j
            y = mul(get(grown_ref, i), x1) + mul(get(back_ref, i), x2)
            ys = split(jnp.concatenate([y[:, :m], -y[:, m:]], axis=1))
            th, tl = get(trans_ref, i)
            th = jnp.concatenate([th[:, :m], th[:, m:]], axis=0)
            tl = jnp.concatenate([tl[:, :m], tl[:, m:]], axis=0)
            c = mul(ys, (th, tl))
            both = c + c.T
            low = pltpu.roll(both[h:], h, 1)
            ref[j * h : (j + 1) * h] = jnp.where(use_top, both[:h], low)
            ref[group * h + j : group * h + j + 1] = jnp.sum(
                jnp.where(eye, c, 0.0), axis=0, keepdims=True
            )


def field_kernel(field_ref, hi_ref, lo_ref):
    for q in range(field_ref.shape[0]):
        hi_ref[q], lo_ref[q] = split(field_ref[q])


def project_kernel(prof_ref, hi_ref, lo_ref, a0_ref, a1_ref, b0_ref, b1_ref, out_ref):
    m = hi_ref.shape[1]
    h = m // 2
    group = prof_ref.shape[0] // 2
    row = lax.broadcasted_iota(jnp.int32, (h, m), 0)
    lane = lax.broadcasted_iota(jnp.int32, (h, m), 1)
    eye = lax.broadcasted_iota(jnp.int32, (m, m), 0) == lax.broadcasted_iota(jnp.int32, (m, m), 1)
    for half, (mine_ref, theirs_ref) in enumerate(((a0_ref, a1_ref), (b0_ref, b1_ref))):
        for j in range(group):
            i = half * group + j
            at = slice(j * h, (j + 1) * h)
            packed = mine_ref[at] + theirs_ref[at]
            at = slice(group * h + j, group * h + j + 1)
            diag = mine_ref[at] + theirs_ref[at]
            top = jnp.where((lane >= h) | (row > lane), packed, 0.0)
            low = pltpu.roll(jnp.where((lane < h) & (row < lane), packed, 0.0), h, 1)
            c = jnp.concatenate([top, low], axis=0) + jnp.where(eye, diag, 0.0)
            ch, cl = split(c)
            q = prof_ref[i]
            fh, fl = hi_ref[q], lo_ref[q]
            w = dot(jnp.concatenate([ch, cl], axis=1), jnp.concatenate([fh, fh], axis=0))
            w = w + dot(ch, fl)
            out_ref[i : i + 1] = jnp.sum(
                (fh.astype(F32) + fl.astype(F32)) * w, axis=0, keepdims=True
            )


def call(kernel, name, kinds, outs, scratch, limit, products, *args):
    def spec(kind):
        return pl.BlockSpec(memory_space=pltpu.SMEM if kind == "s" else pltpu.VMEM)

    several = isinstance(outs, list)
    return pl.pallas_call(
        kernel,
        out_shape=outs,
        in_specs=[spec(kind) for kind in kinds],
        out_specs=[spec("v")] * len(outs) if several else spec("v"),
        scratch_shapes=scratch,
        compiler_params=pltpu.CompilerParams(vmem_limit_bytes=limit * MIB),
        cost_estimate=pl.CostEstimate(
            flops=products * 6 * 8 * 128**3, bytes_accessed=4 * MIB, transcendentals=0
        ),
        name=name,
    )(*args)


def body(interfaces, cell_profile, cell_section, mode_loss, phase, mode_field, target):
    cells = cell_profile.shape[0]
    profiles, m = mode_loss.shape
    blocks = lax.axis_size("cell")
    waves = lax.axis_size("wl")
    pixels = mode_field.shape[2]
    chips = blocks // 2
    angle = phase.reshape(profiles, m)
    wanted = target.reshape(2, m, m)
    me = lax.axis_index("cell").astype(jnp.int32).reshape(1)

    def pairs(*lead):
        return (*lead, 2, m, 2 * m)

    def f32(*shape):
        return jax.ShapeDtypeStruct(shape, F32)

    def bf16(*shape):
        return jax.ShapeDtypeStruct(shape, BF16)

    props = [pltpu.VMEM((profiles, 2, 8, m), F32), pltpu.VMEM((profiles, 2, m, m), F32)]
    codes = (cell_profile << SHIFT) | cell_section
    all_codes = lax.all_to_all(jnp.broadcast_to(codes[None], (blocks, cells)), "cell", 0, 0)
    nodes, own = call(
        own_kernel, "own_tree", "svvv", [bf16(*pairs(6, 3)), f32(3, m, 2 * m)], props, 16, 28,
        codes, interfaces, mode_loss, angle,
    )
    mine = call(
        far_kernel, "far_trees", "ssvvvv", f32(9, m, 2 * m),
        props
        + [
            pltpu.VMEM(pairs(chips - 1, cells // 2, 3), BF16),
            pltpu.VMEM(pairs(chips - 1, cells // 4, 3), BF16),
            pltpu.VMEM(pairs(2, 3), BF16),
        ],
        8 + 3 * blocks, 32 * (chips - 1),
        me, all_codes, interfaces, mode_loss, angle, own,
    )
    theirs = lax.ppermute(mine, "cell", [(i, i ^ 1) for i in range(blocks)])
    grown, back, trans = call(
        scan_kernel, "own_scan", "svvvvv", [bf16(*pairs(cells))] * 3, props, 20, 27,
        codes, interfaces, mode_loss, angle, nodes, own,
    )
    half = f32(cells // 2 * (m // 2) + 8, m)
    first, second, reflection = call(
        last_kernel, "couplings", "svvvvvv", [half, half, f32(2, m // blocks, m)],
        [pltpu.VMEM(pairs(), BF16)] * 2 + [pltpu.VMEM((3, m, 2 * m), F32)], 24, 40,
        me, wanted, mine, theirs, grown, back, trans,
    )

    steps = []
    bit = 1
    while bit < waves:
        steps.append(bit)
        bit *= 2
    parts = [first, second]
    other = [jnp.zeros_like(part) for part in parts]
    for number in range(len(steps)):
        if number:
            parts = [a + b for a, b in zip(parts, other)]
        other = [
            lax.ppermute(part, "wl", [(i, i ^ order[number]) for i in range(waves)])
            for part, order in zip(parts, (steps, steps[::-1]))
        ]
    field = bf16(profiles, m, pixels)
    fields = call(field_kernel, "field_parts", "v", [field, field], [], 12, 1, mode_field)
    gradient = call(
        project_kernel, "project", "svvvvvv", f32(cells, pixels), [], 16, 8,
        cell_profile, *fields, parts[0], other[0], parts[1], other[1],
    )
    return reflection[None], gradient


def solution(mesh):
    in_specs = (
        P(),
        P("cell"),
        P("cell"),
        P(),
        P(None, "wl", None),
        P(None, None, "wl"),
        P("wl", None, None, None),
    )
    out_specs = (P("wl", None, "cell", None), P("cell", "wl"))
    return jax.shard_map(body, mesh=mesh, in_specs=in_specs, out_specs=out_specs, check_vma=False)
```

profile of v0, /device:TPU:0, one launch (start us, length us, event | category | flops | bytes accessed | tf_op | source)
XLA Modules:
  0.0 47.1 jit_solution(12812276887940876018)
XLA Ops:
  0.6 0.7 %shift-left_or_fusion.code_ref = s32[8]{0:T(128)S(1)} fusion(s32[8]{0:T(128)} %param.9, s32[8]{0:T(128)} %prof_ref.1), kind=kLoop, calls=%fused_computation | loop fusion | flops 16 | bytes 96 | tf_op jit(solution)/shard_map/or | solution.py:413
  1.3 0.6 %broadcast_in_dim.4 = s32[8,1,8]{2,1,0:T(1,128)} broadcast(s32[8]{0:T(128)S(1)} %shift-left_or_fusion.code_ref), dimensions={2} | broadcast | bytes 288 | tf_op jit(solution)/shard_map/broadcast_in_dim | solution.py:414
  1.9 6.3 %all-to-all-start = ((s32[8,1,8]{2,1,0:T(1,128)}), s32[8,1,8]{2,1,0:T(1,128)S(1)}, u32[]{:S(2)}, u32[]{:S(2)}) async-start(s32[8,1,8]{2,1,0:T(1,128)} %broadcast_in_dim.4), calls=%async_computation | async-start | bytes 8192 | tf_op jit(solution)/shard_map/all_to_all | solution.py:414
  8.2 1.9 %copy-done.1 = f32[8,3,2,128,128]{4,3,2,1,0:T(8,128)S(1)} copy-done((f32[8,3,2,128,128]{4,3,2,1,0:T(8,128)S(1)}, f32[8,3,2,128,128]{4,3,2,1,0:T(8,128)}, u32[]{:S(2)}) %copy-start.1) | copy-done | bytes 3145752
  10.1 0.7 %copy-done.4 = f32[4,128]{1,0:T(4,128)S(1)} copy-done((f32[4,128]{1,0:T(4,128)S(1)}, f32[4,128]{1,0:T(4,128)}, u32[]{:S(2)}) %copy-start.4) | copy-done | bytes 2072
  10.8 0.7 %copy-done.6 = f32[4,1,128]{2,1,0:T(1,128)S(1)} copy-done((f32[4,1,128]{2,1,0:T(1,128)S(1)}, f32[4,1,128]{2,1,0:T(1,128)}, u32[]{:S(2)}) %copy-start.6) | copy-done | bytes 2072
  11.5 2.7 %own_tree.1 = (bf16[6,3,2,128,256]{4,3,2,1,0:T(8,128)(2,1)S(1)}, f32[3,128,256]{2,1,0:T(8,128)S(1)}) custom-call(s32[8]{0:T(128)S(1)} %shift-left_or_fusion.code_ref, f32[8,3,2,128,128]{4,3,2,1,0:T(8,128)S(1)} %copy-done.1, f32[4,128]{1,0:T(4,128)S(1)} %copy-done.4, f32[4,128]{1,0:T(4,128)S(1)} %bitcast.7), custom_call_target="tpu_custom_call" | custom-call | flops 2818572288 | bytes 4194304 | tf_op jit(solution)/shard_map/own_tree/pallas_call | solution.py:378
  14.2 0.0 copy-start.9
  14.2 1.4 %copy-done.9 = bf16[6,3,2,128,256]{4,3,2,1,0:T(8,128)(2,1)} copy-done((bf16[6,3,2,128,256]{4,3,2,1,0:T(8,128)(2,1)}, bf16[6,3,2,128,256]{4,3,2,1,0:T(8,128)(2,1)S(1)}, u32[]{:S(2)}) %copy-start.9) | copy-done | bytes 2359320
  15.6 0.0 all-to-all-done
  15.6 0.0 copy-done.2
  15.6 0.0 copy-done.5
  15.6 0.0 copy-done.7
  15.7 0.0 copy-start.10
  15.7 7.6 %far_trees.1.mine_ref = f32[9,128,256]{2,1,0:T(8,128)S(1)} custom-call(s32[1]{0:T(128)} %bitcast.me_ref, s32[8,8]{1,0:T(8,128)S(1)} %bitcast.5, f32[8,3,2,128,128]{4,3,2,1,0:T(8,128)S(1)} %copy-done.2, f32[4,128]{1,0:T(4,128)S(1)} %copy-done.5, f32[4,128]{1,0:T(4,128)S(1)} %bitcast.8, f32[3,128,256]{2,1,0:T(8,128)S(1)} %get-tuple-element.12.own_ref), custom_call_target="tpu_custom_call" | custom-call | flops 9663676416 | bytes 4194304 | tf_op jit(solution)/shard_map/far_trees/pallas_call | solution.py:378
  23.3 0.6 %collective-permute-start = (f32[9,128,256]{2,1,0:T(8,128)S(1)}, f32[9,128,256]{2,1,0:T(8,128)S(1)}, u32[]{:S(2)}, u32[]{:S(2)}) collective-permute-start(f32[9,128,256]{2,1,0:T(8,128)S(1)} %far_trees.1.mine_ref), channel_id=1, source_target_pairs={{0,1},{1,0},{2,3},{3,2},{4,5},{5,4},{6,7},{7,6},{8,9},{9,8},{10,11... | collective-permute-start | bytes 3538952 | tf_op jit(solution)/shard_map/ppermute | solution.py:430
  23.8 0.0 copy-done.10
  23.8 2.7 %own_scan.1 = (bf16[8,2,128,256]{3,2,1,0:T(8,128)(2,1)S(1)}, bf16[8,2,128,256]{3,2,1,0:T(8,128)(2,1)S(1)}, bf16[8,2,128,256]{3,2,1,0:T(8,128)(2,1)S(1)}) custom-call(s32[8]{0:T(128)S(1)} %shift-left_or_fusion.code_ref, f32[8,3,2,128,128]{4,3,2,1,0:T(8,128)S(1)} %copy-done.2, f32[4,128]{1,0:T(4,128)S(1)} %copy-done.5, f32[4,128]{1,0:T(4,128)S(1)} %bitcast.9, ...), custom_call_target="tpu_custom_call" | custom-call | flops 2717908992 | bytes 4194304 | tf_op jit(solution)/shard_map/own_scan/pallas_call | solution.py:378
  26.5 0.0 collective-permute-done.theirs_ref
  26.6 0.0 copy-start
  26.6 5.9 %couplings.1 = (f32[264,128]{1,0:T(8,128)S(1)}, f32[264,128]{1,0:T(8,128)S(1)}, f32[2,16,128]{2,1,0:T(8,128)}) custom-call(s32[1]{0:T(128)} %bitcast.me_ref, f32[2,128,128]{2,1,0:T(8,128)S(1)} %bitcast.6, f32[9,128,256]{2,1,0:T(8,128)S(1)} %far_trees.1.mine_ref, f32[9,128,256]{2,1,0:T(8,128)S(1)} %collective-permute-done.theirs_ref, ...), custom_call_target="tpu_custom_call" | custom-call | flops 4026531840 | bytes 4194304 | tf_op jit(solution)/shard_map/couplings/pallas_call | solution.py:378
  32.4 0.0 copy-start.8
  32.4 1.6 %collective-permute-start.3 = (f32[264,128]{1,0:T(8,128)S(1)}, f32[264,128]{1,0:T(8,128)S(1)}, u32[]{:S(2)}, u32[]{:S(2)}) collective-permute-start(f32[264,128]{1,0:T(8,128)S(1)} %get-tuple-element.21), channel_id=1, source_target_pairs={{0,16},{8,24},{16,0},{24,8},{1,17},{9,25},{17,1},{25,9},{2,18},{10... | collective-permute-start | bytes 405512 | tf_op jit(solution)/shard_map/ppermute | solution.py:453
  34.0 1.5 %collective-permute-start.1 = (f32[264,128]{1,0:T(8,128)S(1)}, f32[264,128]{1,0:T(8,128)S(1)}, u32[]{:S(2)}, u32[]{:S(2)}) collective-permute-start(f32[264,128]{1,0:T(8,128)S(1)} %get-tuple-element.20), channel_id=1, source_target_pairs={{0,8},{8,0},{16,24},{24,16},{1,9},{9,1},{17,25},{25,17},{2,10},{10... | collective-permute-start | bytes 405512 | tf_op jit(solution)/shard_map/ppermute | solution.py:453
  35.5 2.4 %collective-permute-done.3 = f32[264,128]{1,0:T(8,128)S(1)} collective-permute-done((f32[264,128]{1,0:T(8,128)S(1)}, f32[264,128]{1,0:T(8,128)S(1)}, u32[]{:S(2)}, u32[]{:S(2)}) %collective-permute-start.3) | collective-permute-done | bytes 135200 | tf_op jit(solution)/shard_map/ppermute | solution.py:453
  37.9 1.6 %collective-permute-start.4 = (f32[264,128]{1,0:T(8,128)S(1)}, f32[264,128]{1,0:T(8,128)S(1)}, u32[]{:S(2)}, u32[]{:S(2)}) collective-permute-start(f32[264,128]{1,0:T(8,128)S(1)} %add.7.b0_ref), channel_id=1, source_target_pairs={{0,8},{8,0},{16,24},{24,16},{1,9},{9,1},{17,25},{25,17},{2,10},{10... | collective-permute-start | bytes 405512 | tf_op jit(solution)/shard_map/ppermute | solution.py:453
  39.5 0.0 collective-permute-done.1
  39.5 1.6 %collective-permute-start.2 = (f32[264,128]{1,0:T(8,128)S(1)}, f32[264,128]{1,0:T(8,128)S(1)}, u32[]{:S(2)}, u32[]{:S(2)}) collective-permute-start(f32[264,128]{1,0:T(8,128)S(1)} %add.6.a0_ref), channel_id=1, source_target_pairs={{0,16},{8,24},{16,0},{24,8},{1,17},{9,25},{17,1},{25,9},{2,18},{10... | collective-permute-start | bytes 405512 | tf_op jit(solution)/shard_map/ppermute | solution.py:453
  41.1 0.4 field_parts.1
  41.5 1.5 %collective-permute-done.4.b1_ref = f32[264,128]{1,0:T(8,128)S(1)} collective-permute-done((f32[264,128]{1,0:T(8,128)S(1)}, f32[264,128]{1,0:T(8,128)S(1)}, u32[]{:S(2)}, u32[]{:S(2)}) %collective-permute-start.4) | collective-permute-done | bytes 135200 | tf_op jit(solution)/shard_map/ppermute | solution.py:453
  43.0 1.6 %collective-permute-done.2.a1_ref = f32[264,128]{1,0:T(8,128)S(1)} collective-permute-done((f32[264,128]{1,0:T(8,128)S(1)}, f32[264,128]{1,0:T(8,128)S(1)}, u32[]{:S(2)}, u32[]{:S(2)}) %collective-permute-start.2) | collective-permute-done | bytes 135200 | tf_op jit(solution)/shard_map/ppermute | solution.py:453
  44.6 2.5 %project.1 = f32[8,1024]{1,0:T(8,128)} custom-call(s32[8]{0:T(128)S(1)} %copy-done.8, bf16[4,128,1024]{2,1,0:T(8,128)(2,1)S(1)} %get-tuple-element.18.hi_ref, bf16[4,128,1024]{2,1,0:T(8,128)(2,1)S(1)} %get-tuple-element.19.lo_ref, f32[264,128]{1,0:T(8,128)S(1)} %add.6.a0_ref, f32[264,128]{1,0:T(8,128)S(1)} %collective-permute-done.2.a1_ref, ...), custom_call_target="tpu_custom_call" | custom-call | flops 805306368 | bytes 4194304 | tf_op jit(solution)/shard_map/project/pallas_call | solution.py:378
  (12 shorter events, 0.1 us)
Async XLA Ops:
  1.9 13.7 %all-to-all-start = ((s32[8,1,8]{2,1,0:T(1,128)}), s32[8,1,8]{2,1,0:T(1,128)S(1)}, u32[]{:S(2)}, u32[]{:S(2)}) async-start(s32[8,1,8]{2,1,0:T(1,128)} %broadcast_in_dim.4), calls=%async_computation | async-start | bytes 8192 | tf_op jit(solution)/shard_map/all_to_all | solution.py:414
  8.2 1.9 %copy-start.1 = (f32[8,3,2,128,128]{4,3,2,1,0:T(8,128)S(1)}, f32[8,3,2,128,128]{4,3,2,1,0:T(8,128)}, u32[]{:S(2)}) copy-start(f32[8,3,2,128,128]{4,3,2,1,0:T(8,128)} %lib_ref.5) | copy-start | bytes 9437188
  10.1 0.7 %copy-start.4 = (f32[4,128]{1,0:T(4,128)S(1)}, f32[4,128]{1,0:T(4,128)}, u32[]{:S(2)}) copy-start(f32[4,128]{1,0:T(4,128)} %loss_ref.5) | copy-start | bytes 6148
  10.8 0.7 %copy-start.6 = (f32[4,1,128]{2,1,0:T(1,128)S(1)}, f32[4,1,128]{2,1,0:T(1,128)}, u32[]{:S(2)}) copy-start(f32[4,1,128]{2,1,0:T(1,128)} %param.11) | copy-start | bytes 6148
  11.5 4.2 %copy-start.2 = (f32[8,3,2,128,128]{4,3,2,1,0:T(8,128)S(1)}, f32[8,3,2,128,128]{4,3,2,1,0:T(8,128)}, u32[]{:S(2)}) copy-start(f32[8,3,2,128,128]{4,3,2,1,0:T(8,128)} %lib_ref.5) | copy-start | bytes 9437188
  11.5 4.2 %copy-start.5 = (f32[4,128]{1,0:T(4,128)S(1)}, f32[4,128]{1,0:T(4,128)}, u32[]{:S(2)}) copy-start(f32[4,128]{1,0:T(4,128)} %loss_ref.5) | copy-start | bytes 6148
  11.5 4.2 %copy-start.7 = (f32[4,1,128]{2,1,0:T(1,128)S(1)}, f32[4,1,128]{2,1,0:T(1,128)}, u32[]{:S(2)}) copy-start(f32[4,1,128]{2,1,0:T(1,128)} %param.11) | copy-start | bytes 6148
  14.2 1.4 %copy-start.9 = (bf16[6,3,2,128,256]{4,3,2,1,0:T(8,128)(2,1)}, bf16[6,3,2,128,256]{4,3,2,1,0:T(8,128)(2,1)S(1)}, u32[]{:S(2)}) copy-start(bf16[6,3,2,128,256]{4,3,2,1,0:T(8,128)(2,1)S(1)} %get-tuple-element.13.nodes_ref) | copy-start | bytes 7077892
  15.7 8.2 %copy-start.10 = (bf16[6,3,2,128,256]{4,3,2,1,0:T(8,128)(2,1)S(1)}, bf16[6,3,2,128,256]{4,3,2,1,0:T(8,128)(2,1)}, u32[]{:S(2)}) copy-start(bf16[6,3,2,128,256]{4,3,2,1,0:T(8,128)(2,1)} %copy-done.9) | copy-start | bytes 7077892
  23.3 3.3 %collective-permute-start = (f32[9,128,256]{2,1,0:T(8,128)S(1)}, f32[9,128,256]{2,1,0:T(8,128)S(1)}, u32[]{:S(2)}, u32[]{:S(2)}) collective-permute-start(f32[9,128,256]{2,1,0:T(8,128)S(1)} %far_trees.1.mine_ref), channel_id=1, source_target_pairs={{0,1},{1,0},{2,3},{3,2},{4,5},{5,4},{6,7},{7,6},{8,9},{9,8},{10,11... | collective-permute-start | bytes 3538952 | tf_op jit(solution)/shard_map/ppermute | solution.py:430
  23.8 2.7 %copy-start.3 = (f32[1,2,128,128]{3,2,1,0:T(8,128)S(1)}, f32[1,2,128,128]{3,2,1,0:T(8,128)}, u32[]{:S(2)}) copy-start(f32[1,2,128,128]{3,2,1,0:T(8,128)} %param.13) | copy-start | bytes 393220
  26.6 14.5 %copy-start = (f32[4,128,1024]{2,1,0:T(8,128)S(1)}, f32[4,128,1024]{2,1,0:T(8,128)}, u32[]{:S(2)}) copy-start(f32[4,128,1024]{2,1,0:T(8,128)} %field_ref.1) | copy-start | bytes 6291460
  32.4 12.1 %copy-start.8 = (s32[8]{0:T(128)S(1)}, s32[8]{0:T(128)}, u32[]{:S(2)}) copy-start(s32[8]{0:T(128)} %prof_ref.1) | copy-start | bytes 100
  32.4 5.4 %collective-permute-start.3 = (f32[264,128]{1,0:T(8,128)S(1)}, f32[264,128]{1,0:T(8,128)S(1)}, u32[]{:S(2)}, u32[]{:S(2)}) collective-permute-start(f32[264,128]{1,0:T(8,128)S(1)} %get-tuple-element.21), channel_id=1, source_target_pairs={{0,16},{8,24},{16,0},{24,8},{1,17},{9,25},{17,1},{25,9},{2,18},{10... | collective-permute-start | bytes 405512 | tf_op jit(solution)/shard_map/ppermute | solution.py:453
  34.0 5.4 %collective-permute-start.1 = (f32[264,128]{1,0:T(8,128)S(1)}, f32[264,128]{1,0:T(8,128)S(1)}, u32[]{:S(2)}, u32[]{:S(2)}) collective-permute-start(f32[264,128]{1,0:T(8,128)S(1)} %get-tuple-element.20), channel_id=1, source_target_pairs={{0,8},{8,0},{16,24},{24,16},{1,9},{9,1},{17,25},{25,17},{2,10},{10... | collective-permute-start | bytes 405512 | tf_op jit(solution)/shard_map/ppermute | solution.py:453
  37.9 5.1 %collective-permute-start.4 = (f32[264,128]{1,0:T(8,128)S(1)}, f32[264,128]{1,0:T(8,128)S(1)}, u32[]{:S(2)}, u32[]{:S(2)}) collective-permute-start(f32[264,128]{1,0:T(8,128)S(1)} %add.7.b0_ref), channel_id=1, source_target_pairs={{0,8},{8,0},{16,24},{24,16},{1,9},{9,1},{17,25},{25,17},{2,10},{10... | collective-permute-start | bytes 405512 | tf_op jit(solution)/shard_map/ppermute | solution.py:453
  39.5 5.1 %collective-permute-start.2 = (f32[264,128]{1,0:T(8,128)S(1)}, f32[264,128]{1,0:T(8,128)S(1)}, u32[]{:S(2)}, u32[]{:S(2)}) collective-permute-start(f32[264,128]{1,0:T(8,128)S(1)} %add.6.a0_ref), channel_id=1, source_target_pairs={{0,16},{8,24},{16,0},{24,8},{1,17},{9,25},{17,1},{25,9},{2,18},{10... | collective-permute-start | bytes 405512 | tf_op jit(solution)/shard_map/ppermute | solution.py:453
where the time goes:
time: 47.3 us; the launch traced here: 47.1 us
  Pallas kernels  21.7 us (46%)
  starting transfers between devices  13.1 us (28%)
  waiting for transfers between devices  5.48 us (12%)
  local copies, waits for them, and re-layouts  5.3 us (11%)
  between operations  0.74 us (2%)
  other arithmetic  0.72 us (2%)
    pallas_call x6, Pallas kernels, call(): pl.pallas_call(kernel, out_shape=outs, in_specs=[spec(kind) for kind in k...  21.7 us
    all_to_all x1, starting transfers between devices, body(): lax.all_to_all(jnp.broadcast_to(codes[None], (blocks, cells)), 'cell', 0, 0)  6.33 us
    ppermute x4, starting transfers between devices, body(): lax.ppermute(part, 'wl', [(i, i ^ order[number]) for i in range(waves)])  6.21 us
    ppermute x4, waiting for transfers between devices, body(): lax.ppermute(part, 'wl', [(i, i ^ order[number]) for i in range(waves)])  5.47 us
    unnamed x22, local copies, waits for them, and re-layouts  4.71 us
  transfers between devices with their start and end apart: 6, of which 3 were waited for; matrix products, arithmetic and copies ran while one was open for 0% of the time, Pallas kernels for 12%

commit v1 on v0

--- a/solution.py
+++ b/solution.py
@@ -1,3 +1,4 @@
+import functools
 import jax
 import jax.numpy as jnp
 from jax import lax
@@ -67,14 +68,6 @@
     return split(refl), split(trans), split(back)
 
 
-def merge_end(former, latter):
-    r1, t1, b1 = former
-    t1w = right(t1)
-    z = mul(b1, right(latter[0]))
-    trans = mul(latter[1], t1w)
-    return split(whole(r1) + mul(split(z), t1w)), split(trans)
-
-
 def triple(ref, *at):
     return tuple(get(ref, *at, kind) for kind in range(3))
 
@@ -82,10 +75,6 @@
 def keep_triple(ref, values, *at):
     for kind in range(3):
         keep(ref, values[kind], *at, kind)
-
-
-def split_triple(ref, *at):
-    return tuple(split(ref[(*at, kind)]) for kind in range(3))
 
 
 def propagation(loss_ref, phase_ref, row_ref, col_ref):
@@ -148,24 +137,23 @@
 
 
 def scan_kernel(
-    code_ref, lib_ref, loss_ref, phase_ref, nodes_ref, own_ref,
-    grown_ref, back_ref, trans_ref,
-    row_ref, col_ref,
+    code_ref, lib_ref, row_ref, col_ref, nodes_ref, own_ref, grown_ref, back_ref, trans_ref
 ):
-    cells = code_ref.shape[0]
-    m = loss_ref.shape[1]
-    propagation(loss_ref, phase_ref, row_ref, col_ref)
+    m = own_ref.shape[1]
 
     def cell(i):
         return leaf(lib_ref, row_ref, col_ref, code_ref[i])
 
+    def store(ref, i, pair):
+        ref[0, i], ref[1, i] = pair
+
     def put(i, values):
-        keep(trans_ref, values[TRANS], i)
-        keep(back_ref, values[BACK], i)
+        store(trans_ref, i, values[TRANS])
+        store(back_ref, i, values[BACK])
         return values
 
     def grow(i, refl, before):
-        keep(grown_ref, split(whole(before) + mul(refl, right(before))), i)
+        store(grown_ref, i, split(whole(before) + mul(refl, right(before))))
 
     def trans_of(i):
         return trans_leaf(lib_ref, col_ref, code_ref[i])
@@ -190,25 +178,28 @@
     suffix7 = put(7, cell(7))
     grow(7, suffix7[REFL], before7)
     grow(1, suffix1[REFL], trans_of(0))
-    keep(grown_ref, split(unit(m) + own_ref[REFL]), 0)
-    keep(trans_ref, split(own_ref[TRANS]), 0)
-    keep(back_ref, split(own_ref[BACK]), 0)
-
-
-def far_kernel(
-    me_ref, code_ref, lib_ref, loss_ref, phase_ref, own_ref, out_ref,
-    row_ref, col_ref, pairs_ref, fours_ref, acc_ref,
-):
+    store(grown_ref, 0, split(unit(m) + own_ref[REFL]))
+    store(trans_ref, 0, split(own_ref[TRANS]))
+    store(back_ref, 0, split(own_ref[BACK]))
+
+
+def far_kernel(*refs):
+    me_ref, *code_refs = refs[:-9]
+    lib_ref, row_ref, col_ref, own_ref, out_ref, code_ref, pairs_ref, fours_ref, acc_ref = refs[-9:]
     blocks, cells = code_ref.shape
-    m = loss_ref.shape[1]
+    m = own_ref.shape[1]
     chips = blocks // 2
-    chip = me_ref[0] >> 1
-    core = me_ref[0] & 1
+    me = me_ref[0]
+    chip = me >> 1
+    core = me & 1
     right_count = chips - 1 - chip
     right_end = 2 * chip + 2 + (core + 1) * right_count
     left_end = (core + 1) * chip
     out_ref[0:3] = own_ref[...]
-    propagation(loss_ref, phase_ref, row_ref, col_ref)
+    for r, ref in enumerate(code_refs):
+        k = lax.rem(me + 1 + r, blocks)
+        for i in range(cells):
+            code_ref[k, i] = ref[i]
     eye = split(unit(m))
     none = (jnp.zeros_like(eye[0]), jnp.zeros_like(eye[0]))
     for side in range(2):
@@ -216,10 +207,10 @@
 
     def place(i):
         on_right = i < right_count
-        return jnp.where(on_right, right_end - 1 - i, left_end - 1 - (i - right_count)), on_right
+        return jnp.where(on_right, right_end - 1 - i, left_end - 1 - (i - right_count))
 
     def pair_step(i, _):
-        k, _ = place(i)
+        k = place(i)
         for j in range(cells // 2):
             keep_triple(
                 pairs_ref,
@@ -260,82 +251,96 @@
 OWN, LEFT, RIGHT = 0, 3, 6
 
 
-def last_kernel(
-    me_ref, target_ref, mine_ref, theirs_ref, grown_ref, back_ref, trans_ref,
-    first_ref, second_ref, reflection_ref,
-    s_ref, q_ref, left_ref,
-):
-    cells = grown_ref.shape[0]
+def sides(me_ref, mine_ref, theirs_ref):
+    on_first = (me_ref[0] & 1) == 0
+
+    def first(index):
+        return jnp.where(on_first, mine_ref[index], theirs_ref[index])
+
+    def second(index):
+        return jnp.where(on_first, theirs_ref[index], mine_ref[index])
+
+    return on_first, first, second
+
+
+def chain_kernel(me_ref, target_ref, mine_ref, theirs_ref, x_ref):
     m = target_ref.shape[1]
-    h = m // 2
-    core = me_ref[0] & 1
-
-    def part(ref, start):
-        return tuple(split(ref[start + kind]) for kind in range(3))
-
-    def join(zero_ref, one_ref):
-        far = merge(part(zero_ref, LEFT), part(one_ref, LEFT))
-        end = merge_end(part(zero_ref, RIGHT), part(one_ref, RIGHT))
-        return far, end
-
-    @pl.when(core == 0)
-    def _():
-        far, end = join(mine_ref, theirs_ref)
-        s, q = merge_end(part(theirs_ref, OWN), end)
-        keep(s_ref, s)
-        keep(q_ref, q)
-        for kind in range(3):
-            left_ref[kind] = whole(far[kind])
-
-    @pl.when(core == 1)
-    def _():
-        far, end = join(theirs_ref, mine_ref)
-        far = merge(far, part(theirs_ref, OWN))
-        keep(s_ref, end[0])
-        keep(q_ref, end[1])
-        for kind in range(3):
-            left_ref[kind] = whole(far[kind])
-
-    s, q = get(s_ref), get(q_ref)
-    p = split(left_ref[TRANS])
-    pw = right(p)
-    block = right(get(trans_ref, 0))
-    q_block = split(mul(q, block))
-    s_block = split(mul(s, block))
-    total = mul(q_block, pw)
-    here = right(split(mine_ref[OWN + REFL] + mul(get(back_ref, 0), right(s_block))))
-    rows = reflection_ref.shape[1]
-    at = pl.ds(pl.multiple_of(me_ref[0] * rows, rows), rows)
-    mine = mul(split(mul(split(left_ref[BACK, at, :]), here)), pw) + left_ref[REFL, at, :]
-    reflection_ref[0] = mine[:, :m]
-    reflection_ref[1] = mine[:, m:]
+    on_first, first, second = sides(me_ref, mine_ref, theirs_ref)
+    own0_t = split(first(OWN + TRANS))
+    own1_t = split(second(OWN + TRANS))
+    own1_tw = right(own1_t)
+    far0_tw = right(split(first(RIGHT + TRANS)))
+    p_far = mul(split(second(LEFT + TRANS)), right(split(first(LEFT + TRANS))))
+    q_far = mul(split(second(RIGHT + TRANS)), far0_tw)
+    p_fars, q_fars = split(p_far), split(q_far)
+    z = mul(split(first(RIGHT + BACK)), right(split(second(RIGHT + REFL))))
+    p_here = mul(own0_t, right(p_fars))
+    q_here = mul(q_fars, own1_tw)
+    s_far = first(RIGHT + REFL) + mul(split(z), far0_tw)
+    total = mul(split(q_here), right(split(p_here)))
+    z = mul(split(second(OWN + BACK)), right(split(s_far)))
     miss = jnp.concatenate(
         [(total[:, :m] - target_ref[0]).T, (total[:, m:] - target_ref[1]).T], axis=1
     )
-    ahead = split(mul(split(miss), right(q)))
-    x1 = right(split(mul(p, right(ahead))))
-    x2 = right(split(mul(s_block, x1)))
+    s_here = second(OWN + REFL) + mul(split(z), own1_tw)
+    p = split(jnp.where(on_first, p_far, p_here))
+    q = split(jnp.where(on_first, q_here, q_far))
+    s = split(jnp.where(on_first, s_here, s_far))
+    ahead = mul(split(miss), right(q))
+    s_block = mul(s, right(split(mine_ref[OWN + TRANS])))
+    x1 = right(split(mul(p, right(split(ahead)))))
+    x_ref[0, 0], x_ref[0, 1] = x1
+    x_ref[1, 0], x_ref[1, 1] = right(split(mul(split(s_block), x1)))
+
+
+def reflect_kernel(me_ref, mine_ref, theirs_ref, out_ref, left_ref):
+    rows, m = out_ref.shape[1:]
+    _, first, second = sides(me_ref, mine_ref, theirs_ref)
+
+    def extend(former, refl):
+        z = mul(split(former(BACK)), right(split(refl)))
+        return former(REFL) + mul(split(z), right(split(former(TRANS))))
+
+    refl = extend(lambda kind: first(RIGHT + kind), second(RIGHT + REFL))
+    refl = extend(lambda kind: second(OWN + kind), refl)
+    refl = extend(lambda kind: first(OWN + kind), refl)
+    refl = extend(lambda kind: second(LEFT + kind), refl)
+    left_ref[0] = first(LEFT + REFL)
+    left_ref[1] = first(LEFT + BACK)
+    at = pl.ds(pl.multiple_of(me_ref[0] * rows, rows), rows)
+    z = mul(split(left_ref[1, at, :]), right(split(refl)))
+    mine = left_ref[0, at, :] + mul(split(z), right(split(first(LEFT + TRANS))))
+    out_ref[0] = mine[:, :m]
+    out_ref[1] = mine[:, m:]
+
+
+def coupling_kernel(half, x_ref, grown_ref, back_ref, trans_ref, out_ref):
+    group = grown_ref.shape[1] // 2
+    m = grown_ref.shape[2]
+    h = m // 2
+    cells = slice(half * group, (half + 1) * group)
+
+    def stack(ref):
+        return tuple(ref[part, cells].reshape(group * m, 2 * m) for part in range(2))
+
     row = lax.broadcasted_iota(jnp.int32, (h, m), 0)
     lane = lax.broadcasted_iota(jnp.int32, (h, m), 1)
     use_top = (lane >= h) | (row > lane)
     eye = lax.broadcasted_iota(jnp.int32, (m, m), 0) == lax.broadcasted_iota(jnp.int32, (m, m), 1)
-    group = cells // 2
-    for half, ref in enumerate((first_ref, second_ref)):
-        ref[group * h :] = jnp.zeros_like(ref[group * h :])
-        for j in range(group):
-            i = half * group + j
-            y = mul(get(grown_ref, i), x1) + mul(get(back_ref, i), x2)
-            ys = split(jnp.concatenate([y[:, :m], -y[:, m:]], axis=1))
-            th, tl = get(trans_ref, i)
-            th = jnp.concatenate([th[:, :m], th[:, m:]], axis=0)
-            tl = jnp.concatenate([tl[:, :m], tl[:, m:]], axis=0)
-            c = mul(ys, (th, tl))
-            both = c + c.T
-            low = pltpu.roll(both[h:], h, 1)
-            ref[j * h : (j + 1) * h] = jnp.where(use_top, both[:h], low)
-            ref[group * h + j : group * h + j + 1] = jnp.sum(
-                jnp.where(eye, c, 0.0), axis=0, keepdims=True
-            )
+    all_y = mul(stack(grown_ref), (x_ref[0, 0], x_ref[0, 1]))
+    all_y = all_y + mul(stack(back_ref), (x_ref[1, 0], x_ref[1, 1]))
+    out_ref[group * h :] = jnp.zeros_like(out_ref[group * h :])
+    for j in range(group):
+        y = all_y[j * m : (j + 1) * m]
+        ys = split(jnp.concatenate([y[:, :m], -y[:, m:]], axis=1))
+        t = [trans_ref[part, half * group + j] for part in range(2)]
+        c = mul(ys, [jnp.concatenate([a[:, :m], a[:, m:]], axis=0) for a in t])
+        both = c + c.T
+        low = pltpu.roll(both[h:], h, 1)
+        out_ref[j * h : (j + 1) * h] = jnp.where(use_top, both[:h], low)
+        out_ref[group * h + j : group * h + j + 1] = jnp.sum(
+            jnp.where(eye, c, 0.0), axis=0, keepdims=True
+        )
 
 
 def field_kernel(field_ref, hi_ref, lo_ref):
@@ -343,31 +348,33 @@
         hi_ref[q], lo_ref[q] = split(field_ref[q])
 
 
-def project_kernel(prof_ref, hi_ref, lo_ref, a0_ref, a1_ref, b0_ref, b1_ref, out_ref):
+def project_kernel(half, prof_ref, hi_ref, lo_ref, mine_ref, theirs_ref, *rest):
+    out_ref = rest[-1]
     m = hi_ref.shape[1]
     h = m // 2
     group = prof_ref.shape[0] // 2
+    if half:
+        out_ref[:group] = rest[0][...]
     row = lax.broadcasted_iota(jnp.int32, (h, m), 0)
     lane = lax.broadcasted_iota(jnp.int32, (h, m), 1)
     eye = lax.broadcasted_iota(jnp.int32, (m, m), 0) == lax.broadcasted_iota(jnp.int32, (m, m), 1)
-    for half, (mine_ref, theirs_ref) in enumerate(((a0_ref, a1_ref), (b0_ref, b1_ref))):
-        for j in range(group):
-            i = half * group + j
-            at = slice(j * h, (j + 1) * h)
-            packed = mine_ref[at] + theirs_ref[at]
-            at = slice(group * h + j, group * h + j + 1)
-            diag = mine_ref[at] + theirs_ref[at]
-            top = jnp.where((lane >= h) | (row > lane), packed, 0.0)
-            low = pltpu.roll(jnp.where((lane < h) & (row < lane), packed, 0.0), h, 1)
-            c = jnp.concatenate([top, low], axis=0) + jnp.where(eye, diag, 0.0)
-            ch, cl = split(c)
-            q = prof_ref[i]
-            fh, fl = hi_ref[q], lo_ref[q]
-            w = dot(jnp.concatenate([ch, cl], axis=1), jnp.concatenate([fh, fh], axis=0))
-            w = w + dot(ch, fl)
-            out_ref[i : i + 1] = jnp.sum(
-                (fh.astype(F32) + fl.astype(F32)) * w, axis=0, keepdims=True
-            )
+    for j in range(group):
+        at = slice(j * h, (j + 1) * h)
+        packed = mine_ref[at] + theirs_ref[at]
+        at = slice(group * h + j, group * h + j + 1)
+        diag = mine_ref[at] + theirs_ref[at]
+        top = jnp.where((lane >= h) | (row > lane), packed, 0.0)
+        low = pltpu.roll(jnp.where((lane < h) & (row < lane), packed, 0.0), h, 1)
+        c = jnp.concatenate([top, low], axis=0) + jnp.where(eye, diag, 0.0)
+        ch, cl = split(c)
+        q = prof_ref[half * group + j]
+        fh, fl = hi_ref[q], lo_ref[q]
+        w = dot(jnp.concatenate([ch, cl], axis=1), jnp.concatenate([fh, fh], axis=0))
+        w = w + dot(ch, fl)
+        i = half * group + j
+        out_ref[i : i + 1] = jnp.sum(
+            (fh.astype(F32) + fl.astype(F32)) * w, axis=0, keepdims=True
+        )
 
 
 def call(kernel, name, kinds, outs, scratch, limit, products, *args):
@@ -409,34 +416,49 @@
     def bf16(*shape):
         return jax.ShapeDtypeStruct(shape, BF16)
 
-    props = [pltpu.VMEM((profiles, 2, 8, m), F32), pltpu.VMEM((profiles, 2, m, m), F32)]
+    tables = [f32(profiles, 2, 8, m), f32(profiles, 2, m, m)]
     codes = (cell_profile << SHIFT) | cell_section
-    all_codes = lax.all_to_all(jnp.broadcast_to(codes[None], (blocks, cells)), "cell", 0, 0)
-    nodes, own = call(
-        own_kernel, "own_tree", "svvv", [bf16(*pairs(6, 3)), f32(3, m, 2 * m)], props, 16, 28,
+    others = [
+        lax.ppermute(codes, "cell", [((i + r) % blocks, i) for i in range(blocks)])
+        for r in range(1, blocks)
+    ]
+    nodes, own, row_table, col_table = call(
+        own_kernel, "own_tree", "svvv", [bf16(*pairs(6, 3)), f32(3, m, 2 * m), *tables], [], 16, 28,
         codes, interfaces, mode_loss, angle,
     )
     mine = call(
-        far_kernel, "far_trees", "ssvvvv", f32(9, m, 2 * m),
-        props
-        + [
+        far_kernel, "far_trees", "s" * blocks + "vvvv", f32(9, m, 2 * m),
+        [
+            pltpu.SMEM((blocks, cells), jnp.int32),
             pltpu.VMEM(pairs(chips - 1, cells // 2, 3), BF16),
             pltpu.VMEM(pairs(chips - 1, cells // 4, 3), BF16),
             pltpu.VMEM(pairs(2, 3), BF16),
         ],
         8 + 3 * blocks, 32 * (chips - 1),
-        me, all_codes, interfaces, mode_loss, angle, own,
+        me, *others, interfaces, row_table, col_table, own,
     )
     theirs = lax.ppermute(mine, "cell", [(i, i ^ 1) for i in range(blocks)])
+    parts_shape = bf16(2, cells, m, 2 * m)
     grown, back, trans = call(
-        scan_kernel, "own_scan", "svvvvv", [bf16(*pairs(cells))] * 3, props, 20, 27,
-        codes, interfaces, mode_loss, angle, nodes, own,
-    )
-    half = f32(cells // 2 * (m // 2) + 8, m)
-    first, second, reflection = call(
-        last_kernel, "couplings", "svvvvvv", [half, half, f32(2, m // blocks, m)],
-        [pltpu.VMEM(pairs(), BF16)] * 2 + [pltpu.VMEM((3, m, 2 * m), F32)], 24, 40,
-        me, wanted, mine, theirs, grown, back, trans,
+        scan_kernel, "own_scan", "svvvvv", [parts_shape] * 3, [], 20, 27,
+        codes, interfaces, row_table, col_table, nodes, own,
+    )
+    x = call(
+        chain_kernel, "chain", "svvv", bf16(2, 2, 2 * m, 2 * m), [], 16, 20,
+        me, wanted, mine, theirs,
+    )
+    parts = [
+        call(
+            functools.partial(coupling_kernel, half), "couplings", "vvvv",
+            f32(cells // 2 * (m // 2) + 8, m), [], 16, 10,
+            x, grown, back, trans,
+        )
+        for half in range(2)
+    ]
+    reflection = call(
+        reflect_kernel, "reflection", "svv", f32(2, m // blocks, m),
+        [pltpu.VMEM((2, m, 2 * m), F32)], 16, 10,
+        me, mine, theirs,
     )
 
     steps = []
@@ -444,7 +466,6 @@
     while bit < waves:
         steps.append(bit)
         bit *= 2
-    parts = [first, second]
     other = [jnp.zeros_like(part) for part in parts]
     for number in range(len(steps)):
         if number:
@@ -456,8 +477,12 @@
     field = bf16(profiles, m, pixels)
     fields = call(field_kernel, "field_parts", "v", [field, field], [], 12, 1, mode_field)
     gradient = call(
-        project_kernel, "project", "svvvvvv", f32(cells, pixels), [], 16, 8,
-        cell_profile, *fields, parts[0], other[0], parts[1], other[1],
+        functools.partial(project_kernel, 0), "project", "svvvv", f32(cells // 2, pixels), [], 16, 4,
+        cell_profile, *fields, parts[0], other[0],
+    )
+    gradient = call(
+        functools.partial(project_kernel, 1), "project", "svvvvv", f32(cells, pixels), [], 16, 4,
+        cell_profile, *fields, parts[1], other[1], gradient,
     )
     return reflection[None], gradient
 

time: 47.3 us -> 49.3 us (1.042)
  starting transfers between devices: 13.1 us -> 16.5 us
  local copies, waits for them, and re-layouts: 5.3 us -> 3.27 us
  Pallas kernels: 21.7 us -> 23.3 us
  waiting for transfers between devices: 5.48 us -> 4.51 us
    ppermute x0 -> x7, starting transfers between devices: none -> 10.8 us  [body(): lax.ppermute(codes, 'cell', [((i + r) % blocks, i) for i in range(blocks)])]
    all_to_all x1 -> x0, starting transfers between devices: 6.33 us -> none  [body(): lax.all_to_all(jnp.broadcast_to(codes[None], (blocks, cells)), 'cell', 0, 0)]
    ppermute x4, waiting for transfers between devices: 5.47 us -> 3.21 us  [body(): lax.ppermute(part, 'wl', [(i, i ^ order[number]) for i in range(waves)])]
    pallas_call x6 -> x10, Pallas kernels: 21.7 us -> 23.3 us  [call(): pl.pallas_call(kernel, out_shape=outs, in_specs=[spec(kind) for kind in k...]
    unnamed x22 -> x14, local copies, waits for them, and re-layouts: 4.71 us -> 3.27 us
    ppermute x4, starting transfers between devices: 6.21 us -> 4.9 us  [body(): lax.ppermute(part, 'wl', [(i, i ^ order[number]) for i in range(waves)])]
    ppermute x0 -> x7, waiting for transfers between devices: none -> 1.3 us  [body(): lax.ppermute(codes, 'cell', [((i + r) % blocks, i) for i in range(blocks)])]
    broadcast_in_dim x1 -> x0, local copies, waits for them, and re-layouts: 0.6 us -> none  [body(): jnp.broadcast_to(codes[None], (blocks, cells))]
  transfers between devices with their start and end apart: 6 -> 12, of which waited for: 3 -> 5; matrix products, arithmetic and copies ran while one was open for 0% -> 0% of each run, Pallas kernels for 12% -> 23%
where the time goes in v1:
time: 49.3 us; the launch traced here: 49.1 us
  Pallas kernels  23.3 us (47%)
  starting transfers between devices  16.5 us (33%)
  waiting for transfers between devices  4.51 us (9%)
  local copies, waits for them, and re-layouts  3.27 us (7%)
  between operations  0.75 us (2%)
  other arithmetic  0.71 us (1%)
    pallas_call x10, Pallas kernels, call(): pl.pallas_call(kernel, out_shape=outs, in_specs=[spec(kind) for kind in k...  23.3 us
    ppermute x7, starting transfers between devices, body(): lax.ppermute(codes, 'cell', [((i + r) % blocks, i) for i in range(blocks)])  10.8 us
    ppermute x4, starting transfers between devices, body(): lax.ppermute(part, 'wl', [(i, i ^ order[number]) for i in range(waves)])  4.9 us
    unnamed x14, local copies, waits for them, and re-layouts  3.27 us
    ppermute x4, waiting for transfers between devices, body(): lax.ppermute(part, 'wl', [(i, i ^ order[number]) for i in range(waves)])  3.21 us
    ppermute x7, waiting for transfers between devices, body(): lax.ppermute(codes, 'cell', [((i + r) % blocks, i) for i in range(blocks)])  1.3 us
  transfers between devices with their start and end apart: 12, of which 5 were waited for; matrix products, arithmetic and copies ran while one was open for 0% of the time, Pallas kernels for 23%

profile of v1, /device:TPU:0, one launch (start us, length us, event | category | flops | bytes accessed | tf_op | source)
XLA Modules:
  0.0 49.1 jit_solution(16154870355430588521)
XLA Ops:
  0.6 0.7 %shift-left_or_fusion.code_ref = s32[8]{0:T(128)S(1)} fusion(s32[8]{0:T(128)} %param.9, s32[8]{0:T(128)} %prof_ref.3), kind=kLoop, calls=%fused_computation | loop fusion | flops 16 | bytes 96 | tf_op jit(solution)/shard_map/or | solution.py:420
  1.3 0.5 collective-permute-start.6
  1.8 2.6 %collective-permute-start.5 = (s32[8]{0:T(128)S(1)}, s32[8]{0:T(128)S(1)}, u32[]{:S(2)}, u32[]{:S(2)}) collective-permute-start(s32[8]{0:T(128)S(1)} %shift-left_or_fusion.code_ref), channel_id=1, source_target_pairs={{6,0},{7,1},{0,2},{1,3},{2,4},{3,5},{4,6},{5,7},{14,8},{15,9},{8,1... | collective-permute-start | bytes 104 | tf_op jit(solution)/shard_map/ppermute | solution.py:422
  4.4 2.6 %collective-permute-start.4 = (s32[8]{0:T(128)S(1)}, s32[8]{0:T(128)S(1)}, u32[]{:S(2)}, u32[]{:S(2)}) collective-permute-start(s32[8]{0:T(128)S(1)} %shift-left_or_fusion.code_ref), channel_id=1, source_target_pairs={{5,0},{6,1},{7,2},{0,3},{1,4},{2,5},{3,6},{4,7},{13,8},{14,9},{15,... | collective-permute-start | bytes 104 | tf_op jit(solution)/shard_map/ppermute | solution.py:422
  6.9 1.2 %collective-permute-start.3 = (s32[8]{0:T(128)S(1)}, s32[8]{0:T(128)S(1)}, u32[]{:S(2)}, u32[]{:S(2)}) collective-permute-start(s32[8]{0:T(128)S(1)} %shift-left_or_fusion.code_ref), channel_id=1, source_target_pairs={{4,0},{5,1},{6,2},{7,3},{0,4},{1,5},{2,6},{3,7},{12,8},{13,9},{14,... | collective-permute-start | bytes 104 | tf_op jit(solution)/shard_map/ppermute | solution.py:422
  8.2 1.2 %collective-permute-start.2 = (s32[8]{0:T(128)S(1)}, s32[8]{0:T(128)S(1)}, u32[]{:S(2)}, u32[]{:S(2)}) collective-permute-start(s32[8]{0:T(128)S(1)} %shift-left_or_fusion.code_ref), channel_id=1, source_target_pairs={{3,0},{4,1},{5,2},{6,3},{7,4},{0,5},{1,6},{2,7},{11,8},{12,9},{13,... | collective-permute-start | bytes 104 | tf_op jit(solution)/shard_map/ppermute | solution.py:422
  9.3 1.9 %copy-done.2 = f32[8,3,2,128,128]{4,3,2,1,0:T(8,128)S(1)} copy-done((f32[8,3,2,128,128]{4,3,2,1,0:T(8,128)S(1)}, f32[8,3,2,128,128]{4,3,2,1,0:T(8,128)}, u32[]{:S(2)}) %copy-start.2) | copy-done | bytes 3145752
  11.2 0.7 %copy-done.5 = f32[4,128]{1,0:T(4,128)S(1)} copy-done((f32[4,128]{1,0:T(4,128)S(1)}, f32[4,128]{1,0:T(4,128)}, u32[]{:S(2)}) %copy-start.5) | copy-done | bytes 2072
  11.9 0.7 %copy-done.6 = f32[4,1,128]{2,1,0:T(1,128)S(1)} copy-done((f32[4,1,128]{2,1,0:T(1,128)S(1)}, f32[4,1,128]{2,1,0:T(1,128)}, u32[]{:S(2)}) %copy-start.6) | copy-done | bytes 2072
  12.6 2.8 %own_tree.1 = (bf16[6,3,2,128,256]{4,3,2,1,0:T(8,128)(2,1)S(1)}, f32[3,128,256]{2,1,0:T(8,128)S(1)}, f32[4,2,8,128]{3,2,1,0:T(8,128)S(1)}, f32[4,2,128,128]{3,2,1,0:T(8,128)S(1)}) custom-call(s32[8]{0:T(128)S(1)} %shift-left_or_fusion.code_ref, f32[8,3,2,128,128]{4,3,2,1,0:T(8,128)S(1)} %copy-done.2, f32[4,128]{1,0:T(4,128)S(1)} %copy-done.5, ...), custom_call_target="tpu_custom_call" | custom-call | flops 2818572288 | bytes 4194304 | tf_op jit(solution)/shard_map/own_tree/pallas_call | solution.py:385
  15.3 1.4 %collective-permute-start.1 = (s32[8]{0:T(128)S(1)}, s32[8]{0:T(128)S(1)}, u32[]{:S(2)}, u32[]{:S(2)}) collective-permute-start(s32[8]{0:T(128)S(1)} %shift-left_or_fusion.code_ref), channel_id=1, source_target_pairs={{2,0},{3,1},{4,2},{5,3},{6,4},{7,5},{0,6},{1,7},{10,8},{11,9},{12,... | collective-permute-start | bytes 104 | tf_op jit(solution)/shard_map/ppermute | solution.py:422
  16.8 1.4 %collective-permute-start = (s32[8]{0:T(128)S(1)}, s32[8]{0:T(128)S(1)}, u32[]{:S(2)}, u32[]{:S(2)}) collective-permute-start(s32[8]{0:T(128)S(1)} %shift-left_or_fusion.code_ref), channel_id=1, source_target_pairs={{1,0},{2,1},{3,2},{4,3},{5,4},{6,5},{7,6},{0,7},{9,8},{10,9},{11,1... | collective-permute-start | bytes 104 | tf_op jit(solution)/shard_map/ppermute | solution.py:422
  18.2 0.7 %collective-permute-done.1.refs_2_ = s32[8]{0:T(128)S(1)} collective-permute-done((s32[8]{0:T(128)S(1)}, s32[8]{0:T(128)S(1)}, u32[]{:S(2)}, u32[]{:S(2)}) %collective-permute-start.1) | collective-permute-done | bytes 64 | tf_op jit(solution)/shard_map/ppermute | solution.py:422
  18.9 0.5 %collective-permute-done.refs_1_ = s32[8]{0:T(128)S(1)} collective-permute-done((s32[8]{0:T(128)S(1)}, s32[8]{0:T(128)S(1)}, u32[]{:S(2)}, u32[]{:S(2)}) %collective-permute-start) | collective-permute-done | bytes 64 | tf_op jit(solution)/shard_map/ppermute | solution.py:422
  19.5 7.4 %far_trees.1.mine_ref = f32[9,128,256]{2,1,0:T(8,128)S(1)} custom-call(s32[1]{0:T(128)} %bitcast.refs_0_.me_ref, s32[8]{0:T(128)S(1)} %collective-permute-done.refs_1_, s32[8]{0:T(128)S(1)} %collective-permute-done.1.refs_2_, s32[8]{0:T(128)S(1)} %collective-permute-done.2.refs_3_, s32[8]{0:T(128)S(1)} %collective-permute-done.3.refs_4_, ...), custom_call_target="tpu_custom_call" | custom-call | flops 9663676416 | bytes 4194304 | tf_op jit(solution)/shard_map/far_trees/pallas_call | solution.py:385
  26.9 0.8 %collective-permute-start.7 = (f32[9,128,256]{2,1,0:T(8,128)S(1)}, f32[9,128,256]{2,1,0:T(8,128)S(1)}, u32[]{:S(2)}, u32[]{:S(2)}) collective-permute-start(f32[9,128,256]{2,1,0:T(8,128)S(1)} %far_trees.1.mine_ref), channel_id=1, source_target_pairs={{0,1},{1,0},{2,3},{3,2},{4,5},{5,4},{6,7},{7,6},{8,9},{9,8},{10,11... | collective-permute-start | bytes 3538952 | tf_op jit(solution)/shard_map/ppermute | solution.py:440
  27.7 2.5 %own_scan.1 = (bf16[2,8,128,256]{3,2,1,0:T(8,128)(2,1)S(1)}, bf16[2,8,128,256]{3,2,1,0:T(8,128)(2,1)S(1)}, bf16[2,8,128,256]{3,2,1,0:T(8,128)(2,1)S(1)}) custom-call(s32[8]{0:T(128)S(1)} %shift-left_or_fusion.code_ref, f32[8,3,2,128,128]{4,3,2,1,0:T(8,128)S(1)} %copy-done.3, f32[4,2,8,128]{3,2,1,0:T(8,128)S(1)} %get-tuple-element.11.refs_9_.row_ref, ...), custom_call_target="tpu_custom_call" | custom-call | flops 2717908992 | bytes 4194304 | tf_op jit(solution)/shard_map/own_scan/pallas_call | solution.py:385
  30.2 1.5 %chain.1.x_ref = bf16[2,2,256,256]{3,2,1,0:T(8,128)(2,1)S(1)} custom-call(s32[1]{0:T(128)} %bitcast.refs_0_.me_ref, f32[2,128,128]{2,1,0:T(8,128)S(1)} %bitcast.4, f32[9,128,256]{2,1,0:T(8,128)S(1)} %far_trees.1.mine_ref, f32[9,128,256]{2,1,0:T(8,128)S(1)} %collective-permute-done.7.theirs_ref), custom_call_target="tpu_custom_call" | custom-call | flops 2013265920 | bytes 4194304 | tf_op jit(solution)/shard_map/chain/pallas_call | solution.py:385
  31.7 1.3 %couplings.3 = f32[264,128]{1,0:T(8,128)S(1)} custom-call(bf16[2,2,256,256]{3,2,1,0:T(8,128)(2,1)S(1)} %chain.1.x_ref, bf16[2,8,128,256]{3,2,1,0:T(8,128)(2,1)S(1)} %get-tuple-element.17.grown_ref, bf16[2,8,128,256]{3,2,1,0:T(8,128)(2,1)S(1)} %get-tuple-element.18.back_ref, bf16[2,8,128,256]{3,2,1,0:T(8,128)(2,1)S(1)} %get-tuple-element.19.trans_ref), custom_call_target="tpu_custom_call" | custom-call | flops 1006632960 | bytes 4194304 | tf_op jit(solution)/shard_map/couplings/pallas_call | solution.py:385
  33.1 0.0 copy-start
  33.1 1.6 %collective-permute-start.10 = (f32[264,128]{1,0:T(8,128)S(1)}, f32[264,128]{1,0:T(8,128)S(1)}, u32[]{:S(2)}, u32[]{:S(2)}) collective-permute-start(f32[264,128]{1,0:T(8,128)S(1)} %couplings.3), channel_id=1, source_target_pairs={{0,8},{8,0},{16,24},{24,16},{1,9},{9,1},{17,25},{25,17},{2,10},{10... | collective-permute-start | bytes 405512 | tf_op jit(solution)/shard_map/ppermute | solution.py:474
  34.7 1.3 %couplings.2 = f32[264,128]{1,0:T(8,128)S(1)} custom-call(bf16[2,2,256,256]{3,2,1,0:T(8,128)(2,1)S(1)} %chain.1.x_ref, bf16[2,8,128,256]{3,2,1,0:T(8,128)(2,1)S(1)} %get-tuple-element.17.grown_ref, bf16[2,8,128,256]{3,2,1,0:T(8,128)(2,1)S(1)} %get-tuple-element.18.back_ref, bf16[2,8,128,256]{3,2,1,0:T(8,128)(2,1)S(1)} %get-tuple-element.19.trans_ref), custom_call_target="tpu_custom_call" | custom-call | flops 1006632960 | bytes 4194304 | tf_op jit(solution)/shard_map/couplings/pallas_call | solution.py:385
  36.0 1.6 %collective-permute-start.8 = (f32[264,128]{1,0:T(8,128)S(1)}, f32[264,128]{1,0:T(8,128)S(1)}, u32[]{:S(2)}, u32[]{:S(2)}) collective-permute-start(f32[264,128]{1,0:T(8,128)S(1)} %couplings.2), channel_id=1, source_target_pairs={{0,16},{8,24},{16,0},{24,8},{1,17},{9,25},{17,1},{25,9},{2,18},{10... | collective-permute-start | bytes 405512 | tf_op jit(solution)/shard_map/ppermute | solution.py:474
  37.6 1.4 %collective-permute-done.10 = f32[264,128]{1,0:T(8,128)S(1)} collective-permute-done((f32[264,128]{1,0:T(8,128)S(1)}, f32[264,128]{1,0:T(8,128)S(1)}, u32[]{:S(2)}, u32[]{:S(2)}) %collective-permute-start.10) | collective-permute-done | bytes 135200 | tf_op jit(solution)/shard_map/ppermute | solution.py:474
  39.0 1.6 %collective-permute-start.11 = (f32[264,128]{1,0:T(8,128)S(1)}, f32[264,128]{1,0:T(8,128)S(1)}, u32[]{:S(2)}, u32[]{:S(2)}) collective-permute-start(f32[264,128]{1,0:T(8,128)S(1)} %add.7.mine_ref), channel_id=1, source_target_pairs={{0,16},{8,24},{16,0},{24,8},{1,17},{9,25},{17,1},{25,9},{2,18},{10... | collective-permute-start | bytes 405512 | tf_op jit(solution)/shard_map/ppermute | solution.py:474
  40.6 1.4 %collective-permute-done.8 = f32[264,128]{1,0:T(8,128)S(1)} collective-permute-done((f32[264,128]{1,0:T(8,128)S(1)}, f32[264,128]{1,0:T(8,128)S(1)}, u32[]{:S(2)}, u32[]{:S(2)}) %collective-permute-start.8) | collective-permute-done | bytes 135200 | tf_op jit(solution)/shard_map/ppermute | solution.py:474
  42.0 0.2 collective-permute-start.9
  42.2 0.4 field_parts.1
  42.6 2.7 %reflection.1 = f32[2,16,128]{2,1,0:T(8,128)} custom-call(s32[1]{0:T(128)} %bitcast.refs_0_.me_ref, f32[9,128,256]{2,1,0:T(8,128)S(1)} %far_trees.1.mine_ref, f32[9,128,256]{2,1,0:T(8,128)S(1)} %collective-permute-done.7.theirs_ref), custom_call_target="tpu_custom_call" | custom-call | flops 1006632960 | bytes 4194304 | tf_op jit(solution)/shard_map/reflection/pallas_call | solution.py:385
  45.3 1.4 %project.2.rest_0_ = f32[4,1024]{1,0:T(4,128)S(1)} custom-call(s32[8]{0:T(128)S(1)} %copy-done.1, bf16[4,128,1024]{2,1,0:T(8,128)(2,1)S(1)} %get-tuple-element.14.hi_ref, bf16[4,128,1024]{2,1,0:T(8,128)(2,1)S(1)} %get-tuple-element.15.lo_ref, f32[264,128]{1,0:T(8,128)S(1)} %add.7.mine_ref, f32[264,128]{1,0:T(8,128)S(1)} %collective-permute-done.11.theirs_ref), custom_call_target="tpu_custom_call" | custom-call | flops 402653184 | bytes 4194304 | tf_op jit(solution)/shard_map/project/pallas_call | solution.py:385
  46.7 0.4 collective-permute-done.9.theirs_ref
  47.1 2.0 %project.3 = f32[8,1024]{1,0:T(8,128)} custom-call(s32[8]{0:T(128)S(1)} %copy-done.1, bf16[4,128,1024]{2,1,0:T(8,128)(2,1)S(1)} %get-tuple-element.14.hi_ref, bf16[4,128,1024]{2,1,0:T(8,128)(2,1)S(1)} %get-tuple-element.15.lo_ref, f32[264,128]{1,0:T(8,128)S(1)} %add.6.mine_ref, f32[264,128]{1,0:T(8,128)S(1)} %collective-permute-done.9.theirs_ref, ...), custom_call_target="tpu_custom_call" | custom-call | flops 402653184 | bytes 4194304 | tf_op jit(solution)/shard_map/project/pallas_call | solution.py:385
  (19 shorter events, 0.1 us)
Async XLA Ops:
  1.3 14.0 %collective-permute-start.6 = (s32[8]{0:T(128)S(1)}, s32[8]{0:T(128)S(1)}, u32[]{:S(2)}, u32[]{:S(2)}) collective-permute-start(s32[8]{0:T(128)S(1)} %shift-left_or_fusion.code_ref), channel_id=1, source_target_pairs={{7,0},{0,1},{1,2},{2,3},{3,4},{4,5},{5,6},{6,7},{15,8},{8,9},{9,10... | collective-permute-start | bytes 104 | tf_op jit(solution)/shard_map/ppermute | solution.py:422
  1.8 15.0 %collective-permute-start.5 = (s32[8]{0:T(128)S(1)}, s32[8]{0:T(128)S(1)}, u32[]{:S(2)}, u32[]{:S(2)}) collective-permute-start(s32[8]{0:T(128)S(1)} %shift-left_or_fusion.code_ref), channel_id=1, source_target_pairs={{6,0},{7,1},{0,2},{1,3},{2,4},{3,5},{4,6},{5,7},{14,8},{15,9},{8,1... | collective-permute-start | bytes 104 | tf_op jit(solution)/shard_map/ppermute | solution.py:422
  4.4 13.8 %collective-permute-start.4 = (s32[8]{0:T(128)S(1)}, s32[8]{0:T(128)S(1)}, u32[]{:S(2)}, u32[]{:S(2)}) collective-permute-start(s32[8]{0:T(128)S(1)} %shift-left_or_fusion.code_ref), channel_id=1, source_target_pairs={{5,0},{6,1},{7,2},{0,3},{1,4},{2,5},{3,6},{4,7},{13,8},{14,9},{15,... | collective-permute-start | bytes 104 | tf_op jit(solution)/shard_map/ppermute | solution.py:422
  6.9 11.3 %collective-permute-start.3 = (s32[8]{0:T(128)S(1)}, s32[8]{0:T(128)S(1)}, u32[]{:S(2)}, u32[]{:S(2)}) collective-permute-start(s32[8]{0:T(128)S(1)} %shift-left_or_fusion.code_ref), channel_id=1, source_target_pairs={{4,0},{5,1},{6,2},{7,3},{0,4},{1,5},{2,6},{3,7},{12,8},{13,9},{14,... | collective-permute-start | bytes 104 | tf_op jit(solution)/shard_map/ppermute | solution.py:422
  8.2 10.0 %collective-permute-start.2 = (s32[8]{0:T(128)S(1)}, s32[8]{0:T(128)S(1)}, u32[]{:S(2)}, u32[]{:S(2)}) collective-permute-start(s32[8]{0:T(128)S(1)} %shift-left_or_fusion.code_ref), channel_id=1, source_target_pairs={{3,0},{4,1},{5,2},{6,3},{7,4},{0,5},{1,6},{2,7},{11,8},{12,9},{13,... | collective-permute-start | bytes 104 | tf_op jit(solution)/shard_map/ppermute | solution.py:422
  9.3 1.9 %copy-start.2 = (f32[8,3,2,128,128]{4,3,2,1,0:T(8,128)S(1)}, f32[8,3,2,128,128]{4,3,2,1,0:T(8,128)}, u32[]{:S(2)}) copy-start(f32[8,3,2,128,128]{4,3,2,1,0:T(8,128)} %lib_ref.3) | copy-start | bytes 9437188
  11.2 0.7 %copy-start.5 = (f32[4,128]{1,0:T(4,128)S(1)}, f32[4,128]{1,0:T(4,128)}, u32[]{:S(2)}) copy-start(f32[4,128]{1,0:T(4,128)} %loss_ref.1) | copy-start | bytes 6148
  11.9 0.7 %copy-start.6 = (f32[4,1,128]{2,1,0:T(1,128)S(1)}, f32[4,1,128]{2,1,0:T(1,128)}, u32[]{:S(2)}) copy-start(f32[4,1,128]{2,1,0:T(1,128)} %param.11) | copy-start | bytes 6148
  12.6 6.9 %copy-start.3 = (f32[8,3,2,128,128]{4,3,2,1,0:T(8,128)S(1)}, f32[8,3,2,128,128]{4,3,2,1,0:T(8,128)}, u32[]{:S(2)}) copy-start(f32[8,3,2,128,128]{4,3,2,1,0:T(8,128)} %lib_ref.3) | copy-start | bytes 9437188
  15.3 3.6 %collective-permute-start.1 = (s32[8]{0:T(128)S(1)}, s32[8]{0:T(128)S(1)}, u32[]{:S(2)}, u32[]{:S(2)}) collective-permute-start(s32[8]{0:T(128)S(1)} %shift-left_or_fusion.code_ref), channel_id=1, source_target_pairs={{2,0},{3,1},{4,2},{5,3},{6,4},{7,5},{0,6},{1,7},{10,8},{11,9},{12,... | collective-permute-start | bytes 104 | tf_op jit(solution)/shard_map/ppermute | solution.py:422
  16.8 2.7 %collective-permute-start = (s32[8]{0:T(128)S(1)}, s32[8]{0:T(128)S(1)}, u32[]{:S(2)}, u32[]{:S(2)}) collective-permute-start(s32[8]{0:T(128)S(1)} %shift-left_or_fusion.code_ref), channel_id=1, source_target_pairs={{1,0},{2,1},{3,2},{4,3},{5,4},{6,5},{7,6},{0,7},{9,8},{10,9},{11,1... | collective-permute-start | bytes 104 | tf_op jit(solution)/shard_map/ppermute | solution.py:422
  26.9 3.3 %collective-permute-start.7 = (f32[9,128,256]{2,1,0:T(8,128)S(1)}, f32[9,128,256]{2,1,0:T(8,128)S(1)}, u32[]{:S(2)}, u32[]{:S(2)}) collective-permute-start(f32[9,128,256]{2,1,0:T(8,128)S(1)} %far_trees.1.mine_ref), channel_id=1, source_target_pairs={{0,1},{1,0},{2,3},{3,2},{4,5},{5,4},{6,7},{7,6},{8,9},{9,8},{10,11... | collective-permute-start | bytes 3538952 | tf_op jit(solution)/shard_map/ppermute | solution.py:440
  27.7 2.5 %copy-start.4 = (f32[1,2,128,128]{3,2,1,0:T(8,128)S(1)}, f32[1,2,128,128]{3,2,1,0:T(8,128)}, u32[]{:S(2)}) copy-start(f32[1,2,128,128]{3,2,1,0:T(8,128)} %param.13) | copy-start | bytes 393220
  33.1 9.1 %copy-start = (f32[4,128,1024]{2,1,0:T(8,128)S(1)}, f32[4,128,1024]{2,1,0:T(8,128)}, u32[]{:S(2)}) copy-start(f32[4,128,1024]{2,1,0:T(8,128)} %field_ref.1) | copy-start | bytes 6291460
  33.1 5.9 %collective-permute-start.10 = (f32[264,128]{1,0:T(8,128)S(1)}, f32[264,128]{1,0:T(8,128)S(1)}, u32[]{:S(2)}, u32[]{:S(2)}) collective-permute-start(f32[264,128]{1,0:T(8,128)S(1)} %couplings.3), channel_id=1, source_target_pairs={{0,8},{8,0},{16,24},{24,16},{1,9},{9,1},{17,25},{25,17},{2,10},{10... | collective-permute-start | bytes 405512 | tf_op jit(solution)/shard_map/ppermute | solution.py:474
  36.0 6.0 %collective-permute-start.8 = (f32[264,128]{1,0:T(8,128)S(1)}, f32[264,128]{1,0:T(8,128)S(1)}, u32[]{:S(2)}, u32[]{:S(2)}) collective-permute-start(f32[264,128]{1,0:T(8,128)S(1)} %couplings.2), channel_id=1, source_target_pairs={{0,16},{8,24},{16,0},{24,8},{1,17},{9,25},{17,1},{25,9},{2,18},{10... | collective-permute-start | bytes 405512 | tf_op jit(solution)/shard_map/ppermute | solution.py:474
  39.0 6.3 %collective-permute-start.11 = (f32[264,128]{1,0:T(8,128)S(1)}, f32[264,128]{1,0:T(8,128)S(1)}, u32[]{:S(2)}, u32[]{:S(2)}) collective-permute-start(f32[264,128]{1,0:T(8,128)S(1)} %add.7.mine_ref), channel_id=1, source_target_pairs={{0,16},{8,24},{16,0},{24,8},{1,17},{9,25},{17,1},{25,9},{2,18},{10... | collective-permute-start | bytes 405512 | tf_op jit(solution)/shard_map/ppermute | solution.py:474
  42.0 5.1 %collective-permute-start.9 = (f32[264,128]{1,0:T(8,128)S(1)}, f32[264,128]{1,0:T(8,128)S(1)}, u32[]{:S(2)}, u32[]{:S(2)}) collective-permute-start(f32[264,128]{1,0:T(8,128)S(1)} %add.6.mine_ref), channel_id=1, source_target_pairs={{0,8},{8,0},{16,24},{24,16},{1,9},{9,1},{17,25},{25,17},{2,10},{10... | collective-permute-start | bytes 405512 | tf_op jit(solution)/shard_map/ppermute | solution.py:474
  42.6 2.7 %copy-start.1 = (s32[8]{0:T(128)S(1)}, s32[8]{0:T(128)}, u32[]{:S(2)}) copy-start(s32[8]{0:T(128)} %prof_ref.3) | copy-start | bytes 100

commit v2 on v1

--- a/solution.py
+++ b/solution.py
@@ -10,7 +10,9 @@
 BF16 = jnp.bfloat16
 MIB = 1024 * 1024
 SHIFT = 8
+LOW = (1 << SHIFT) - 1
 REFL, TRANS, BACK = 0, 1, 2
+FEWER = 3
 
 
 def split(x):
@@ -77,33 +79,31 @@
         keep(ref, values[kind], *at, kind)
 
 
-def propagation(loss_ref, phase_ref, row_ref, col_ref):
-    m = loss_ref.shape[1]
-    amp = loss_ref[...]
-    angle = phase_ref[...]
-    for part, values in enumerate((amp * jnp.cos(angle), amp * jnp.sin(angle))):
-        for q in range(loss_ref.shape[0]):
-            wide = jnp.broadcast_to(values[q : q + 1], (m, m))
+def spread(factor_refs, row_ref, col_ref):
+    for part, ref in enumerate(factor_refs):
+        profiles, m = ref.shape
+        for q in range(profiles):
+            wide = jnp.broadcast_to(ref[q : q + 1], (m, m))
             row_ref[q, part] = wide[:8]
             col_ref[q, part] = wide.T
 
 
 def trans_leaf(lib_ref, col_ref, code):
-    q, s = code >> SHIFT, code & ((1 << SHIFT) - 1)
+    q, s = code >> SHIFT, code & LOW
     re, im = lib_ref[s, TRANS, 0], lib_ref[s, TRANS, 1]
     cr, ci = col_ref[q, 0], col_ref[q, 1]
     return split(jnp.concatenate([cr * re - ci * im, cr * im + ci * re], axis=1))
 
 
 def back_leaf(lib_ref, row_ref, code):
-    q, s = code >> SHIFT, code & ((1 << SHIFT) - 1)
+    q, s = code >> SHIFT, code & LOW
     re, im = lib_ref[s, BACK, 0], lib_ref[s, BACK, 1]
     rr, ri = row_ref[q, 0][:1], row_ref[q, 1][:1]
     return split(jnp.concatenate([re * rr - im * ri, re * ri + im * rr], axis=1))
 
 
 def refl_leaf(lib_ref, code):
-    s = code & ((1 << SHIFT) - 1)
+    s = code & LOW
     return split(jnp.concatenate([lib_ref[s, REFL, 0], lib_ref[s, REFL, 1]], axis=1))
 
 
@@ -115,17 +115,18 @@
     )
 
 
-def own_kernel(code_ref, lib_ref, loss_ref, phase_ref, nodes_ref, own_ref, row_ref, col_ref):
-    cells = code_ref.shape[0]
-    propagation(loss_ref, phase_ref, row_ref, col_ref)
+def own_kernel(
+    me_ref, code_ref, lib_ref, real_ref, imag_ref, nodes_ref, own_ref, row_ref, col_ref
+):
+    cells = code_ref.shape[1]
+    spread((real_ref, imag_ref), row_ref, col_ref)
+
+    def cell(i):
+        return leaf(lib_ref, row_ref, col_ref, code_ref[me_ref[0], i])
+
     pairs = []
     for j in range(cells // 2):
-        pairs.append(
-            merge(
-                leaf(lib_ref, row_ref, col_ref, code_ref[2 * j]),
-                leaf(lib_ref, row_ref, col_ref, code_ref[2 * j + 1]),
-            )
-        )
+        pairs.append(merge(cell(2 * j), cell(2 * j + 1)))
         keep_triple(nodes_ref, pairs[j], j)
     fours = []
     for j in range(cells // 4):
@@ -137,12 +138,16 @@
 
 
 def scan_kernel(
-    code_ref, lib_ref, row_ref, col_ref, nodes_ref, own_ref, grown_ref, back_ref, trans_ref
+    me_ref, code_ref, lib_ref, row_ref, col_ref, nodes_ref, own_ref,
+    grown_ref, back_ref, trans_ref,
 ):
     m = own_ref.shape[1]
 
+    def code(i):
+        return code_ref[me_ref[0], i]
+
     def cell(i):
-        return leaf(lib_ref, row_ref, col_ref, code_ref[i])
+        return leaf(lib_ref, row_ref, col_ref, code(i))
 
     def store(ref, i, pair):
         ref[0, i], ref[1, i] = pair
@@ -156,7 +161,7 @@
         store(grown_ref, i, split(whole(before) + mul(refl, right(before))))
 
     def trans_of(i):
-        return trans_leaf(lib_ref, col_ref, code_ref[i])
+        return trans_leaf(lib_ref, col_ref, code(i))
 
     suffix4 = put(4, triple(nodes_ref, 5))
     before2 = get(nodes_ref, 0, TRANS)
@@ -183,23 +188,18 @@
     store(back_ref, 0, split(own_ref[BACK]))
 
 
-def far_kernel(*refs):
-    me_ref, *code_refs = refs[:-9]
-    lib_ref, row_ref, col_ref, own_ref, out_ref, code_ref, pairs_ref, fours_ref, acc_ref = refs[-9:]
+def far_kernel(
+    me_ref, code_ref, lib_ref, row_ref, col_ref, own_ref, out_ref, pairs_ref, fours_ref, acc_ref
+):
     blocks, cells = code_ref.shape
     m = own_ref.shape[1]
     chips = blocks // 2
-    me = me_ref[0]
-    chip = me >> 1
-    core = me & 1
+    chip = me_ref[0] >> 1
+    core = me_ref[0] & 1
     right_count = chips - 1 - chip
     right_end = 2 * chip + 2 + (core + 1) * right_count
     left_end = (core + 1) * chip
     out_ref[0:3] = own_ref[...]
-    for r, ref in enumerate(code_refs):
-        k = lax.rem(me + 1 + r, blocks)
-        for i in range(cells):
-            code_ref[k, i] = ref[i]
     eye = split(unit(m))
     none = (jnp.zeros_like(eye[0]), jnp.zeros_like(eye[0]))
     for side in range(2):
@@ -263,7 +263,7 @@
     return on_first, first, second
 
 
-def chain_kernel(me_ref, target_ref, mine_ref, theirs_ref, x_ref):
+def chain_kernel(me_ref, target_ref, mine_ref, theirs_ref, x_ref, part_ref):
     m = target_ref.shape[1]
     on_first, first, second = sides(me_ref, mine_ref, theirs_ref)
     own0_t = split(first(OWN + TRANS))
@@ -283,6 +283,8 @@
         [(total[:, :m] - target_ref[0]).T, (total[:, m:] - target_ref[1]).T], axis=1
     )
     s_here = second(OWN + REFL) + mul(split(z), own1_tw)
+    part_ref[0] = s_here
+    part_ref[1] = p_far
     p = split(jnp.where(on_first, p_far, p_here))
     q = split(jnp.where(on_first, q_here, q_far))
     s = split(jnp.where(on_first, s_here, s_far))
@@ -293,32 +295,28 @@
     x_ref[1, 0], x_ref[1, 1] = right(split(mul(split(s_block), x1)))
 
 
-def reflect_kernel(me_ref, mine_ref, theirs_ref, out_ref, left_ref):
+def reflect_kernel(me_ref, mine_ref, theirs_ref, part_ref, out_ref, left_ref):
     rows, m = out_ref.shape[1:]
     _, first, second = sides(me_ref, mine_ref, theirs_ref)
-
-    def extend(former, refl):
-        z = mul(split(former(BACK)), right(split(refl)))
-        return former(REFL) + mul(split(z), right(split(former(TRANS))))
-
-    refl = extend(lambda kind: first(RIGHT + kind), second(RIGHT + REFL))
-    refl = extend(lambda kind: second(OWN + kind), refl)
-    refl = extend(lambda kind: first(OWN + kind), refl)
-    refl = extend(lambda kind: second(LEFT + kind), refl)
     left_ref[0] = first(LEFT + REFL)
     left_ref[1] = first(LEFT + BACK)
     at = pl.ds(pl.multiple_of(me_ref[0] * rows, rows), rows)
-    z = mul(split(left_ref[1, at, :]), right(split(refl)))
-    mine = left_ref[0, at, :] + mul(split(z), right(split(first(LEFT + TRANS))))
+    back = split(left_ref[1, at, :])
+    z = mul(split(first(OWN + BACK)), right(split(part_ref[0])))
+    refl = first(OWN + REFL) + mul(split(z), right(split(first(OWN + TRANS))))
+    z = mul(back, right(split(second(LEFT + REFL))))
+    left = left_ref[0, at, :] + mul(split(z), right(split(first(LEFT + TRANS))))
+    back = mul(back, right(split(second(LEFT + BACK))))
+    z = mul(split(back), right(split(refl)))
+    mine = left + mul(split(z), right(split(part_ref[1])))
     out_ref[0] = mine[:, :m]
     out_ref[1] = mine[:, m:]
 
 
-def coupling_kernel(half, x_ref, grown_ref, back_ref, trans_ref, out_ref):
-    group = grown_ref.shape[1] // 2
+def coupling_kernel(start, group, x_ref, grown_ref, back_ref, trans_ref, out_ref):
     m = grown_ref.shape[2]
     h = m // 2
-    cells = slice(half * group, (half + 1) * group)
+    cells = slice(start, start + group)
 
     def stack(ref):
         return tuple(ref[part, cells].reshape(group * m, 2 * m) for part in range(2))
@@ -333,7 +331,7 @@
     for j in range(group):
         y = all_y[j * m : (j + 1) * m]
         ys = split(jnp.concatenate([y[:, :m], -y[:, m:]], axis=1))
-        t = [trans_ref[part, half * group + j] for part in range(2)]
+        t = [trans_ref[part, start + j] for part in range(2)]
         c = mul(ys, [jnp.concatenate([a[:, :m], a[:, m:]], axis=0) for a in t])
         both = c + c.T
         low = pltpu.roll(both[h:], h, 1)
@@ -348,13 +346,12 @@
         hi_ref[q], lo_ref[q] = split(field_ref[q])
 
 
-def project_kernel(half, prof_ref, hi_ref, lo_ref, mine_ref, theirs_ref, *rest):
+def project_kernel(start, group, prof_ref, hi_ref, lo_ref, mine_ref, theirs_ref, *rest):
     out_ref = rest[-1]
     m = hi_ref.shape[1]
     h = m // 2
-    group = prof_ref.shape[0] // 2
-    if half:
-        out_ref[:group] = rest[0][...]
+    if start:
+        out_ref[:start] = rest[0][...]
     row = lax.broadcasted_iota(jnp.int32, (h, m), 0)
     lane = lax.broadcasted_iota(jnp.int32, (h, m), 1)
     eye = lax.broadcasted_iota(jnp.int32, (m, m), 0) == lax.broadcasted_iota(jnp.int32, (m, m), 1)
@@ -367,11 +364,11 @@
         low = pltpu.roll(jnp.where((lane < h) & (row < lane), packed, 0.0), h, 1)
         c = jnp.concatenate([top, low], axis=0) + jnp.where(eye, diag, 0.0)
         ch, cl = split(c)
-        q = prof_ref[half * group + j]
+        q = prof_ref[start + j]
         fh, fl = hi_ref[q], lo_ref[q]
         w = dot(jnp.concatenate([ch, cl], axis=1), jnp.concatenate([fh, fh], axis=0))
         w = w + dot(ch, fl)
-        i = half * group + j
+        i = start + j
         out_ref[i : i + 1] = jnp.sum(
             (fh.astype(F32) + fl.astype(F32)) * w, axis=0, keepdims=True
         )
@@ -404,6 +401,7 @@
     pixels = mode_field.shape[2]
     chips = blocks // 2
     angle = phase.reshape(profiles, m)
+    factors = (mode_loss * jnp.cos(angle), mode_loss * jnp.sin(angle))
     wanted = target.reshape(2, m, m)
     me = lax.axis_index("cell").astype(jnp.int32).reshape(1)
 
@@ -418,47 +416,36 @@
 
     tables = [f32(profiles, 2, 8, m), f32(profiles, 2, m, m)]
     codes = (cell_profile << SHIFT) | cell_section
-    others = [
-        lax.ppermute(codes, "cell", [((i + r) % blocks, i) for i in range(blocks)])
-        for r in range(1, blocks)
-    ]
+    codes = jnp.broadcast_to(codes[None], (blocks, cells))
+    all_codes = lax.all_to_all(codes, "cell", 0, 0)
     nodes, own, row_table, col_table = call(
-        own_kernel, "own_tree", "svvv", [bf16(*pairs(6, 3)), f32(3, m, 2 * m), *tables], [], 16, 28,
-        codes, interfaces, mode_loss, angle,
+        own_kernel, "own_tree", "ssvvv", [bf16(*pairs(6, 3)), f32(3, m, 2 * m), *tables], [], 12, 28,
+        me, all_codes, interfaces, *factors,
     )
     mine = call(
-        far_kernel, "far_trees", "s" * blocks + "vvvv", f32(9, m, 2 * m),
+        far_kernel, "far_trees", "ssvvvv", f32(9, m, 2 * m),
         [
-            pltpu.SMEM((blocks, cells), jnp.int32),
             pltpu.VMEM(pairs(chips - 1, cells // 2, 3), BF16),
             pltpu.VMEM(pairs(chips - 1, cells // 4, 3), BF16),
             pltpu.VMEM(pairs(2, 3), BF16),
         ],
-        8 + 3 * blocks, 32 * (chips - 1),
-        me, *others, interfaces, row_table, col_table, own,
+        8 + 3 * blocks // 2, 32 * (chips - 1),
+        me, all_codes, interfaces, row_table, col_table, own,
     )
     theirs = lax.ppermute(mine, "cell", [(i, i ^ 1) for i in range(blocks)])
     parts_shape = bf16(2, cells, m, 2 * m)
     grown, back, trans = call(
-        scan_kernel, "own_scan", "svvvvv", [parts_shape] * 3, [], 20, 27,
-        codes, interfaces, row_table, col_table, nodes, own,
-    )
-    x = call(
-        chain_kernel, "chain", "svvv", bf16(2, 2, 2 * m, 2 * m), [], 16, 20,
+        scan_kernel, "own_scan", "ssvvvvv", [parts_shape] * 3, [], 16, 27,
+        me, all_codes, interfaces, row_table, col_table, nodes, own,
+    )
+    x, part = call(
+        chain_kernel, "chain", "svvv", [bf16(2, 2, 2 * m, 2 * m), f32(2, m, 2 * m)], [], 12, 20,
         me, wanted, mine, theirs,
     )
-    parts = [
-        call(
-            functools.partial(coupling_kernel, half), "couplings", "vvvv",
-            f32(cells // 2 * (m // 2) + 8, m), [], 16, 10,
-            x, grown, back, trans,
-        )
-        for half in range(2)
-    ]
     reflection = call(
-        reflect_kernel, "reflection", "svv", f32(2, m // blocks, m),
-        [pltpu.VMEM((2, m, 2 * m), F32)], 16, 10,
-        me, mine, theirs,
+        reflect_kernel, "reflection", "svvv", f32(2, m // blocks, m),
+        [pltpu.VMEM((2, m, 2 * m), F32)], 12, 10,
+        me, mine, theirs, part,
     )
 
     steps = []
@@ -466,25 +453,40 @@
     while bit < waves:
         steps.append(bit)
         bit *= 2
-    other = [jnp.zeros_like(part) for part in parts]
-    for number in range(len(steps)):
-        if number:
-            parts = [a + b for a, b in zip(parts, other)]
-        other = [
-            lax.ppermute(part, "wl", [(i, i ^ order[number]) for i in range(waves)])
-            for part, order in zip(parts, (steps, steps[::-1]))
+    orders = (steps, steps[::-1])
+
+    def exchange(part, number):
+        pairs_of = [
+            (w * blocks + c, (w ^ orders[c & 1][number]) * blocks + c)
+            for w in range(waves)
+            for c in range(blocks)
         ]
+        return lax.ppermute(part, ("wl", "cell"), pairs_of)
+
     field = bf16(profiles, m, pixels)
     fields = call(field_kernel, "field_parts", "v", [field, field], [], 12, 1, mode_field)
-    gradient = call(
-        functools.partial(project_kernel, 0), "project", "svvvv", f32(cells // 2, pixels), [], 16, 4,
-        cell_profile, *fields, parts[0], other[0],
-    )
-    gradient = call(
-        functools.partial(project_kernel, 1), "project", "svvvvv", f32(cells, pixels), [], 16, 4,
-        cell_profile, *fields, parts[1], other[1], gradient,
-    )
-    return reflection[None], gradient
+    gradient = []
+    start = 0
+    for group in (cells - FEWER, FEWER):
+        packed = call(
+            functools.partial(coupling_kernel, start, group), "couplings", "vvvv",
+            f32(group * (m // 2) + 8, m), [], 12, 10,
+            x, grown, back, trans,
+        )
+        other = jnp.zeros_like(packed)
+        for number in range(len(steps)):
+            if number:
+                packed = packed + other
+            other = exchange(packed, number)
+        gradient = [
+            call(
+                functools.partial(project_kernel, start, group), "project",
+                "svvvv" + "v" * len(gradient), f32(start + group, pixels), [], 12, 4,
+                cell_profile, *fields, packed, other, *gradient,
+            )
+        ]
+        start += group
+    return reflection[None], gradient[0]
 
 
 def solution(mesh):

time: 49.3 us -> 46.6 us (0.945)
  starting transfers between devices: 16.5 us -> 11.7 us
  waiting for transfers between devices: 4.51 us -> 7.5 us
  Pallas kernels: 23.3 us -> 22.4 us
  local copies, waits for them, and re-layouts: 3.27 us -> 2.51 us
  other arithmetic: 0.71 us -> 1.45 us
    ppermute x11 -> x4, starting transfers between devices: 15.8 us -> 5.28 us  [exchange(): return lax.ppermute(part, ('wl', 'cell'), pairs_of)]
    all_to_all x0 -> x1, starting transfers between devices: none -> 6.33 us  [body(): all_codes = lax.all_to_all(codes, 'cell', 0, 0)]
    all_to_all x0 -> x1, waiting for transfers between devices: none -> 4.74 us  [body(): all_codes = lax.all_to_all(codes, 'cell', 0, 0)]
    ppermute x11 -> x4, waiting for transfers between devices: 4.51 us -> 2.63 us  [exchange(): return lax.ppermute(part, ('wl', 'cell'), pairs_of)]
    unnamed x14 -> x10, local copies, waits for them, and re-layouts: 3.27 us -> 1.91 us
    pallas_call x10, Pallas kernels: 23.3 us -> 22.4 us  [call(): pl.pallas_call(kernel, out_shape=outs, in_specs=[spec(kind) for kind in k...]
    mul x0 -> x1, other arithmetic: none -> 0.74 us  [body(): factors = (mode_loss * jnp.cos(angle), mode_loss * jnp.sin(angle))]
    ppermute x1, starting transfers between devices: 0.78 us -> 0.07 us  [body(): theirs = lax.ppermute(mine, 'cell', [(i, i ^ 1) for i in range(blocks)])]
  transfers between devices with their start and end apart: 12 -> 6, of which waited for: 5 -> 4; matrix products, arithmetic and copies ran while one was open for 0% -> 2% of each run, Pallas kernels for 23% -> 15%
where the time goes in v2:
time: 46.6 us; the launch traced here: 46.3 us
  Pallas kernels  22.4 us (48%)
  starting transfers between devices  11.7 us (25%)
  waiting for transfers between devices  7.5 us (16%)
  local copies, waits for them, and re-layouts  2.51 us (5%)
  other arithmetic  1.45 us (3%)
  between operations  0.76 us (2%)
    pallas_call x10, Pallas kernels, call(): pl.pallas_call(kernel, out_shape=outs, in_specs=[spec(kind) for kind in k...  22.4 us
    all_to_all x1, starting transfers between devices, body(): all_codes = lax.all_to_all(codes, 'cell', 0, 0)  6.33 us
    ppermute x4, starting transfers between devices, exchange(): return lax.ppermute(part, ('wl', 'cell'), pairs_of)  5.28 us
    all_to_all x1, waiting for transfers between devices, body(): all_codes = lax.all_to_all(codes, 'cell', 0, 0)  4.74 us
    ppermute x4, waiting for transfers between devices, exchange(): return lax.ppermute(part, ('wl', 'cell'), pairs_of)  2.63 us
    unnamed x10, local copies, waits for them, and re-layouts  1.91 us
  transfers between devices with their start and end apart: 6, of which 4 were waited for; matrix products, arithmetic and copies ran while one was open for 2% of the time, Pallas kernels for 15%

profile of v2, /device:TPU:0, one launch (start us, length us, event | category | flops | bytes accessed | tf_op | source)
XLA Modules:
  0.0 46.3 jit_solution(3592354702866655744)
XLA Ops:
  0.6 0.7 %shift-left_or_fusion = s32[8]{0:T(128)S(1)} fusion(s32[8]{0:T(128)} %param.9, s32[8]{0:T(128)} %prof_ref.3), kind=kLoop, calls=%fused_computation.2 | loop fusion | flops 16 | bytes 96 | tf_op jit(solution)/shard_map/or | solution.py:418
  1.3 0.6 %broadcast_in_dim.4 = s32[8,1,8]{2,1,0:T(1,128)} broadcast(s32[8]{0:T(128)S(1)} %shift-left_or_fusion), dimensions={2} | broadcast | bytes 288 | tf_op jit(solution)/shard_map/broadcast_in_dim | solution.py:419
  1.9 6.3 %all-to-all-start = ((s32[8,1,8]{2,1,0:T(1,128)}), s32[8,1,8]{2,1,0:T(1,128)S(1)}, u32[]{:S(2)}, u32[]{:S(2)}) async-start(s32[8,1,8]{2,1,0:T(1,128)} %broadcast_in_dim.4), calls=%async_computation | async-start | bytes 8192 | tf_op jit(solution)/shard_map/all_to_all | solution.py:420
  8.2 0.7 %bitcast_multiply_fusion = (f32[4,128]{1,0:T(4,128)S(1)}, f32[4,128]{1,0:T(4,128)S(1)}) fusion(f32[4,128]{1,0:T(4,128)} %param.10, f32[4,1,128]{2,0,1:T(4,128)} %bitcast.13), kind=kLoop, calls=%fused_computation | loop fusion | flops 1024 | bytes 8192 | tf_op jit(solution)/shard_map/mul | solution.py:404
  9.0 4.7 %all-to-all-done = s32[8,1,8]{2,1,0:T(1,128)S(1)} async-done(((s32[8,1,8]{2,1,0:T(1,128)}), s32[8,1,8]{2,1,0:T(1,128)S(1)}, u32[]{:S(2)}, u32[]{:S(2)}) %all-to-all-start) | async-done | bytes 288 | tf_op jit(solution)/shard_map/all_to_all | solution.py:420
  13.7 1.9 %copy-done.2 = f32[8,3,2,128,128]{4,3,2,1,0:T(8,128)S(1)} copy-done((f32[8,3,2,128,128]{4,3,2,1,0:T(8,128)S(1)}, f32[8,3,2,128,128]{4,3,2,1,0:T(8,128)}, u32[]{:S(2)}) %copy-start.2) | copy-done | bytes 3145752
  15.6 2.8 %own_tree.1 = (bf16[6,3,2,128,256]{4,3,2,1,0:T(8,128)(2,1)S(1)}, f32[3,128,256]{2,1,0:T(8,128)S(1)}, f32[4,2,8,128]{3,2,1,0:T(8,128)S(1)}, f32[4,2,128,128]{3,2,1,0:T(8,128)S(1)}) custom-call(s32[1]{0:T(128)} %bitcast.me_ref, s32[8,8]{1,0:T(8,128)S(1)} %bitcast.9, f32[8,3,2,128,128]{4,3,2,1,0:T(8,128)S(1)} %copy-done.2, ...), custom_call_target="tpu_custom_call" | custom-call | flops 2818572288 | bytes 4194304 | tf_op jit(solution)/shard_map/own_tree/pallas_call | solution.py:382
  18.4 0.0 copy-done.3
  18.4 7.7 %far_trees.1.mine_ref = f32[9,128,256]{2,1,0:T(8,128)S(1)} custom-call(s32[1]{0:T(128)} %bitcast.me_ref, s32[8,8]{1,0:T(8,128)S(1)} %bitcast.10, f32[8,3,2,128,128]{4,3,2,1,0:T(8,128)S(1)} %copy-done.3, f32[4,2,8,128]{3,2,1,0:T(8,128)S(1)} %get-tuple-element.13.row_ref, f32[4,2,128,128]{3,2,1,0:T(8,128)S(1)} %get-tuple-element.14.col_ref, ...), custom_call_target="tpu_custom_call" | custom-call | flops 9663676416 | bytes 4194304 | tf_op jit(solution)/shard_map/far_trees/pallas_call | solution.py:382
  26.1 0.1 collective-permute-start
  26.1 0.0 copy-start.4
  26.2 2.7 %own_scan.1 = (bf16[2,8,128,256]{3,2,1,0:T(8,128)(2,1)S(1)}, bf16[2,8,128,256]{3,2,1,0:T(8,128)(2,1)S(1)}, bf16[2,8,128,256]{3,2,1,0:T(8,128)(2,1)S(1)}) custom-call(s32[1]{0:T(128)} %bitcast.me_ref, s32[8,8]{1,0:T(8,128)S(1)} %bitcast.11, f32[8,3,2,128,128]{4,3,2,1,0:T(8,128)S(1)} %copy-done.3, f32[4,2,8,128]{3,2,1,0:T(8,128)S(1)} %get-tuple-element.13.row_ref, ...), custom_call_target="tpu_custom_call" | custom-call | flops 2717908992 | bytes 4194304 | tf_op jit(solution)/shard_map/own_scan/pallas_call | solution.py:382
  28.9 0.1 collective-permute-done.theirs_ref
  29.0 0.0 copy-done.4
  29.0 1.5 %chain.1 = (bf16[2,2,256,256]{3,2,1,0:T(8,128)(2,1)S(1)}, f32[2,128,256]{2,1,0:T(8,128)S(1)}) custom-call(s32[1]{0:T(128)} %bitcast.me_ref, f32[2,128,128]{2,1,0:T(8,128)S(1)} %bitcast.12, f32[9,128,256]{2,1,0:T(8,128)S(1)} %far_trees.1.mine_ref, f32[9,128,256]{2,1,0:T(8,128)S(1)} %collective-permute-done.theirs_ref), custom_call_target="tpu_custom_call" | custom-call | flops 2013265920 | bytes 4194304 | tf_op jit(solution)/shard_map/chain/pallas_call | solution.py:382
  30.5 1.5 %couplings.3 = f32[328,128]{1,0:T(8,128)S(1)} custom-call(bf16[2,2,256,256]{3,2,1,0:T(8,128)(2,1)S(1)} %get-tuple-element.19.x_ref, bf16[2,8,128,256]{3,2,1,0:T(8,128)(2,1)S(1)} %get-tuple-element.21.grown_ref, bf16[2,8,128,256]{3,2,1,0:T(8,128)(2,1)S(1)} %get-tuple-element.22.back_ref, bf16[2,8,128,256]{3,2,1,0:T(8,128)(2,1)S(1)} %get-tuple-element.23.trans_ref), custom_call_target="tpu_custom_call" | custom-call | flops 1006632960 | bytes 4194304 | tf_op jit(solution)/shard_map/couplings/pallas_call | solution.py:382
  32.0 0.0 copy-start
  32.1 1.6 %collective-permute-start.3 = (f32[328,128]{1,0:T(8,128)S(1)}, f32[328,128]{1,0:T(8,128)S(1)}, u32[]{:S(2)}, u32[]{:S(2)}) collective-permute-start(f32[328,128]{1,0:T(8,128)S(1)} %couplings.3), channel_id=1, source_target_pairs={{0,8},{1,17},{2,10},{3,19},{4,12},{5,21},{6,14},{7,23},{8,0},{9,25... | collective-permute-start | bytes 503816 | tf_op jit(solution)/shard_map/ppermute | solution.py:464
  33.6 1.1 %couplings.2 = f32[200,128]{1,0:T(8,128)S(1)} custom-call(bf16[2,2,256,256]{3,2,1,0:T(8,128)(2,1)S(1)} %get-tuple-element.19.x_ref, bf16[2,8,128,256]{3,2,1,0:T(8,128)(2,1)S(1)} %get-tuple-element.21.grown_ref, bf16[2,8,128,256]{3,2,1,0:T(8,128)(2,1)S(1)} %get-tuple-element.22.back_ref, bf16[2,8,128,256]{3,2,1,0:T(8,128)(2,1)S(1)} %get-tuple-element.23.trans_ref), custom_call_target="tpu_custom_call" | custom-call | flops 1006632960 | bytes 4194304 | tf_op jit(solution)/shard_map/couplings/pallas_call | solution.py:382
  34.7 0.6 %collective-permute-start.1 = (f32[200,128]{1,0:T(8,128)S(1)}, f32[200,128]{1,0:T(8,128)S(1)}, u32[]{:S(2)}, u32[]{:S(2)}) collective-permute-start(f32[200,128]{1,0:T(8,128)S(1)} %couplings.2), channel_id=1, source_target_pairs={{0,8},{1,17},{2,10},{3,19},{4,12},{5,21},{6,14},{7,23},{8,0},{9,25... | collective-permute-start | bytes 307208 | tf_op jit(solution)/shard_map/ppermute | solution.py:464
  35.3 2.2 %collective-permute-done.3 = f32[328,128]{1,0:T(8,128)S(1)} collective-permute-done((f32[328,128]{1,0:T(8,128)S(1)}, f32[328,128]{1,0:T(8,128)S(1)}, u32[]{:S(2)}, u32[]{:S(2)}) %collective-permute-start.3) | collective-permute-done | bytes 167968 | tf_op jit(solution)/shard_map/ppermute | solution.py:464
  37.5 1.6 %collective-permute-start.4 = (f32[328,128]{1,0:T(8,128)S(1)}, f32[328,128]{1,0:T(8,128)S(1)}, u32[]{:S(2)}, u32[]{:S(2)}) collective-permute-start(f32[328,128]{1,0:T(8,128)S(1)} %add.7.mine_ref), channel_id=1, source_target_pairs={{0,16},{1,9},{2,18},{3,11},{4,20},{5,13},{6,22},{7,15},{8,24},{9,1... | collective-permute-start | bytes 503816 | tf_op jit(solution)/shard_map/ppermute | solution.py:464
  39.1 0.0 copy-done
  39.1 0.4 field_parts.1
  39.5 0.0 copy-start.1
  39.5 0.0 collective-permute-done.1
  39.5 1.5 %collective-permute-start.2 = (f32[200,128]{1,0:T(8,128)S(1)}, f32[200,128]{1,0:T(8,128)S(1)}, u32[]{:S(2)}, u32[]{:S(2)}) collective-permute-start(f32[200,128]{1,0:T(8,128)S(1)} %add.6.mine_ref), channel_id=1, source_target_pairs={{0,16},{1,9},{2,18},{3,11},{4,20},{5,13},{6,22},{7,15},{8,24},{9,1... | collective-permute-start | bytes 307208 | tf_op jit(solution)/shard_map/ppermute | solution.py:464
  41.1 1.4 %reflection.1 = f32[2,16,128]{2,1,0:T(8,128)} custom-call(s32[1]{0:T(128)} %bitcast.me_ref, f32[9,128,256]{2,1,0:T(8,128)S(1)} %far_trees.1.mine_ref, f32[9,128,256]{2,1,0:T(8,128)S(1)} %collective-permute-done.theirs_ref, f32[2,128,256]{2,1,0:T(8,128)S(1)} %get-tuple-element.16.part_ref), custom_call_target="tpu_custom_call" | custom-call | flops 1006632960 | bytes 4194304 | tf_op jit(solution)/shard_map/reflection/pallas_call | solution.py:382
  42.5 0.5 %collective-permute-done.4.theirs_ref = f32[328,128]{1,0:T(8,128)S(1)} collective-permute-done((f32[328,128]{1,0:T(8,128)S(1)}, f32[328,128]{1,0:T(8,128)S(1)}, u32[]{:S(2)}, u32[]{:S(2)}) %collective-permute-start.4) | collective-permute-done | bytes 167968 | tf_op jit(solution)/shard_map/ppermute | solution.py:464
  42.9 1.5 %project.2.rest_0_ = f32[5,1024]{1,0:T(8,128)S(1)} custom-call(s32[8]{0:T(128)S(1)} %copy-done.1, bf16[4,128,1024]{2,1,0:T(8,128)(2,1)S(1)} %get-tuple-element.17.hi_ref, bf16[4,128,1024]{2,1,0:T(8,128)(2,1)S(1)} %get-tuple-element.18.lo_ref, f32[328,128]{1,0:T(8,128)S(1)} %add.7.mine_ref, f32[328,128]{1,0:T(8,128)S(1)} %collective-permute-done.4.theirs_ref), custom_call_target="tpu_custom_call" | custom-call | flops 402653184 | bytes 4194304 | tf_op jit(solution)/shard_map/project/pallas_call | solution.py:382
  44.5 0.0 collective-permute-done.2.theirs_ref
  44.5 1.8 %project.3 = f32[8,1024]{1,0:T(8,128)} custom-call(s32[8]{0:T(128)S(1)} %copy-done.1, bf16[4,128,1024]{2,1,0:T(8,128)(2,1)S(1)} %get-tuple-element.17.hi_ref, bf16[4,128,1024]{2,1,0:T(8,128)(2,1)S(1)} %get-tuple-element.18.lo_ref, f32[200,128]{1,0:T(8,128)S(1)} %add.6.mine_ref, f32[200,128]{1,0:T(8,128)S(1)} %collective-permute-done.2.theirs_ref, ...), custom_call_target="tpu_custom_call" | custom-call | flops 402653184 | bytes 4194304 | tf_op jit(solution)/shard_map/project/pallas_call | solution.py:382
  (5 shorter events, 0.0 us)
Async XLA Ops:
  1.9 11.8 %all-to-all-start = ((s32[8,1,8]{2,1,0:T(1,128)}), s32[8,1,8]{2,1,0:T(1,128)S(1)}, u32[]{:S(2)}, u32[]{:S(2)}) async-start(s32[8,1,8]{2,1,0:T(1,128)} %broadcast_in_dim.4), calls=%async_computation | async-start | bytes 8192 | tf_op jit(solution)/shard_map/all_to_all | solution.py:420
  13.7 1.9 %copy-start.2 = (f32[8,3,2,128,128]{4,3,2,1,0:T(8,128)S(1)}, f32[8,3,2,128,128]{4,3,2,1,0:T(8,128)}, u32[]{:S(2)}) copy-start(f32[8,3,2,128,128]{4,3,2,1,0:T(8,128)} %lib_ref.5) | copy-start | bytes 9437188
  15.6 2.8 %copy-start.3 = (f32[8,3,2,128,128]{4,3,2,1,0:T(8,128)S(1)}, f32[8,3,2,128,128]{4,3,2,1,0:T(8,128)}, u32[]{:S(2)}) copy-start(f32[8,3,2,128,128]{4,3,2,1,0:T(8,128)} %lib_ref.5) | copy-start | bytes 9437188
  26.1 2.9 %collective-permute-start = (f32[9,128,256]{2,1,0:T(8,128)S(1)}, f32[9,128,256]{2,1,0:T(8,128)S(1)}, u32[]{:S(2)}, u32[]{:S(2)}) collective-permute-start(f32[9,128,256]{2,1,0:T(8,128)S(1)} %far_trees.1.mine_ref), channel_id=1, source_target_pairs={{0,1},{1,0},{2,3},{3,2},{4,5},{5,4},{6,7},{7,6},{8,9},{9,8},{10,11... | collective-permute-start | bytes 3538952 | tf_op jit(solution)/shard_map/ppermute | solution.py:435
  26.1 2.8 %copy-start.4 = (f32[1,2,128,128]{3,2,1,0:T(8,128)S(1)}, f32[1,2,128,128]{3,2,1,0:T(8,128)}, u32[]{:S(2)}) copy-start(f32[1,2,128,128]{3,2,1,0:T(8,128)} %param.13) | copy-start | bytes 393220
  32.0 7.1 %copy-start = (f32[4,128,1024]{2,1,0:T(8,128)S(1)}, f32[4,128,1024]{2,1,0:T(8,128)}, u32[]{:S(2)}) copy-start(f32[4,128,1024]{2,1,0:T(8,128)} %field_ref.1) | copy-start | bytes 6291460
  32.1 5.4 %collective-permute-start.3 = (f32[328,128]{1,0:T(8,128)S(1)}, f32[328,128]{1,0:T(8,128)S(1)}, u32[]{:S(2)}, u32[]{:S(2)}) collective-permute-start(f32[328,128]{1,0:T(8,128)S(1)} %couplings.3), channel_id=1, source_target_pairs={{0,8},{1,17},{2,10},{3,19},{4,12},{5,21},{6,14},{7,23},{8,0},{9,25... | collective-permute-start | bytes 503816 | tf_op jit(solution)/shard_map/ppermute | solution.py:464
  34.7 4.8 %collective-permute-start.1 = (f32[200,128]{1,0:T(8,128)S(1)}, f32[200,128]{1,0:T(8,128)S(1)}, u32[]{:S(2)}, u32[]{:S(2)}) collective-permute-start(f32[200,128]{1,0:T(8,128)S(1)} %couplings.2), channel_id=1, source_target_pairs={{0,8},{1,17},{2,10},{3,19},{4,12},{5,21},{6,14},{7,23},{8,0},{9,25... | collective-permute-start | bytes 307208 | tf_op jit(solution)/shard_map/ppermute | solution.py:464
  37.5 5.4 %collective-permute-start.4 = (f32[328,128]{1,0:T(8,128)S(1)}, f32[328,128]{1,0:T(8,128)S(1)}, u32[]{:S(2)}, u32[]{:S(2)}) collective-permute-start(f32[328,128]{1,0:T(8,128)S(1)} %add.7.mine_ref), channel_id=1, source_target_pairs={{0,16},{1,9},{2,18},{3,11},{4,20},{5,13},{6,22},{7,15},{8,24},{9,1... | collective-permute-start | bytes 503816 | tf_op jit(solution)/shard_map/ppermute | solution.py:464
  39.5 3.5 %copy-start.1 = (s32[8]{0:T(128)S(1)}, s32[8]{0:T(128)}, u32[]{:S(2)}) copy-start(s32[8]{0:T(128)} %prof_ref.3) | copy-start | bytes 100
  39.5 4.9 %collective-permute-start.2 = (f32[200,128]{1,0:T(8,128)S(1)}, f32[200,128]{1,0:T(8,128)S(1)}, u32[]{:S(2)}, u32[]{:S(2)}) collective-permute-start(f32[200,128]{1,0:T(8,128)S(1)} %add.6.mine_ref), channel_id=1, source_target_pairs={{0,16},{1,9},{2,18},{3,11},{4,20},{5,13},{6,22},{7,15},{8,24},{9,1... | collective-permute-start | bytes 307208 | tf_op jit(solution)/shard_map/ppermute | solution.py:464

commit v3 on v2

--- a/solution.py
+++ b/solution.py
@@ -62,12 +62,11 @@
 def merge(former, latter):
     r1, t1, b1 = former
     r2, t2, b2 = latter
-    t1w = right(t1)
-    z = mul(b1, right(r2))
+    m = t1[0].shape[0]
+    z = split(mul(b1, right(r2)))
     back = mul(b1, right(b2))
-    trans = mul(t2, t1w)
-    refl = whole(r1) + mul(split(z), t1w)
-    return split(refl), split(trans), split(back)
+    both = mul([jnp.concatenate([a, b], axis=0) for a, b in zip(z, t2)], right(t1))
+    return split(whole(r1) + both[:m]), split(both[m:]), split(back)
 
 
 def triple(ref, *at):
@@ -115,14 +114,12 @@
     )
 
 
-def own_kernel(
-    me_ref, code_ref, lib_ref, real_ref, imag_ref, nodes_ref, own_ref, row_ref, col_ref
-):
-    cells = code_ref.shape[1]
+def own_kernel(code_ref, lib_ref, real_ref, imag_ref, nodes_ref, own_ref, row_ref, col_ref):
+    cells = code_ref.shape[0]
     spread((real_ref, imag_ref), row_ref, col_ref)
 
     def cell(i):
-        return leaf(lib_ref, row_ref, col_ref, code_ref[me_ref[0], i])
+        return leaf(lib_ref, row_ref, col_ref, code_ref[i])
 
     pairs = []
     for j in range(cells // 2):
@@ -138,16 +135,13 @@
 
 
 def scan_kernel(
-    me_ref, code_ref, lib_ref, row_ref, col_ref, nodes_ref, own_ref,
+    code_ref, lib_ref, row_ref, col_ref, nodes_ref, own_ref,
     grown_ref, back_ref, trans_ref,
 ):
     m = own_ref.shape[1]
 
-    def code(i):
-        return code_ref[me_ref[0], i]
-
     def cell(i):
-        return leaf(lib_ref, row_ref, col_ref, code(i))
+        return leaf(lib_ref, row_ref, col_ref, code_ref[i])
 
     def store(ref, i, pair):
         ref[0, i], ref[1, i] = pair
@@ -161,7 +155,7 @@
         store(grown_ref, i, split(whole(before) + mul(refl, right(before))))
 
     def trans_of(i):
-        return trans_leaf(lib_ref, col_ref, code(i))
+        return trans_leaf(lib_ref, col_ref, code_ref[i])
 
     suffix4 = put(4, triple(nodes_ref, 5))
     before2 = get(nodes_ref, 0, TRANS)
@@ -189,11 +183,12 @@
 
 
 def far_kernel(
-    me_ref, code_ref, lib_ref, row_ref, col_ref, own_ref, out_ref, pairs_ref, fours_ref, acc_ref
+    me_ref, same_ref, other_ref, lib_ref, row_ref, col_ref, own_ref,
+    out_ref,
+    pairs_ref, fours_ref, acc_ref,
 ):
-    blocks, cells = code_ref.shape
+    chips, cells = same_ref.shape
     m = own_ref.shape[1]
-    chips = blocks // 2
     chip = me_ref[0] >> 1
     core = me_ref[0] & 1
     right_count = chips - 1 - chip
@@ -211,13 +206,15 @@
 
     def pair_step(i, _):
         k = place(i)
+
+        def cell(j):
+            same, other = same_ref[k >> 1, j], other_ref[k >> 1, j]
+            return leaf(lib_ref, row_ref, col_ref, jnp.where((k & 1) == core, same, other))
+
         for j in range(cells // 2):
             keep_triple(
                 pairs_ref,
-                merge(
-                    leaf(lib_ref, row_ref, col_ref, code_ref[k, 2 * j]),
-                    leaf(lib_ref, row_ref, col_ref, code_ref[k, 2 * j + 1]),
-                ),
+                merge(cell(2 * j), cell(2 * j + 1)),
                 i,
                 j,
             )
@@ -416,27 +413,31 @@
 
     tables = [f32(profiles, 2, 8, m), f32(profiles, 2, m, m)]
     codes = (cell_profile << SHIFT) | cell_section
-    codes = jnp.broadcast_to(codes[None], (blocks, cells))
-    all_codes = lax.all_to_all(codes, "cell", 0, 0)
+    same = lax.all_to_all(
+        jnp.broadcast_to(codes[None], (chips, cells)), "cell", 0, 0,
+        axis_index_groups=[list(range(core, blocks, 2)) for core in range(2)],
+    )
+    swap = [(i, i ^ 1) for i in range(blocks)]
+    other = lax.ppermute(same, "cell", swap)
     nodes, own, row_table, col_table = call(
-        own_kernel, "own_tree", "ssvvv", [bf16(*pairs(6, 3)), f32(3, m, 2 * m), *tables], [], 12, 28,
-        me, all_codes, interfaces, *factors,
+        own_kernel, "own_tree", "svvv", [bf16(*pairs(6, 3)), f32(3, m, 2 * m), *tables], [], 12, 28,
+        codes, interfaces, *factors,
     )
     mine = call(
-        far_kernel, "far_trees", "ssvvvv", f32(9, m, 2 * m),
+        far_kernel, "far_trees", "sssvvvv", f32(9, m, 2 * m),
         [
             pltpu.VMEM(pairs(chips - 1, cells // 2, 3), BF16),
             pltpu.VMEM(pairs(chips - 1, cells // 4, 3), BF16),
             pltpu.VMEM(pairs(2, 3), BF16),
         ],
         8 + 3 * blocks // 2, 32 * (chips - 1),
-        me, all_codes, interfaces, row_table, col_table, own,
-    )
-    theirs = lax.ppermute(mine, "cell", [(i, i ^ 1) for i in range(blocks)])
+        me, same, other, interfaces, row_table, col_table, own,
+    )
+    theirs = lax.ppermute(mine, "cell", swap)
     parts_shape = bf16(2, cells, m, 2 * m)
     grown, back, trans = call(
-        scan_kernel, "own_scan", "ssvvvvv", [parts_shape] * 3, [], 16, 27,
-        me, all_codes, interfaces, row_table, col_table, nodes, own,
+        scan_kernel, "own_scan", "svvvvv", [parts_shape] * 3, [], 16, 27,
+        codes, interfaces, row_table, col_table, nodes, own,
     )
     x, part = call(
         chain_kernel, "chain", "svvv", [bf16(2, 2, 2 * m, 2 * m), f32(2, m, 2 * m)], [], 12, 20,

time: 46.6 us -> 48.5 us (1.041)
  local copies, waits for them, and re-layouts: 2.51 us -> 7.13 us
  waiting for transfers between devices: 7.5 us -> 3.84 us
  Pallas kernels: 22.4 us -> 23.2 us
    all_to_all x1, waiting for transfers between devices: 4.74 us -> 0.01 us  [body(): lax.all_to_all(jnp.broadcast_to(codes[None], (chips, cells)), 'cell', 0,...]
    unnamed x10 -> x26, local copies, waits for them, and re-layouts: 1.91 us -> 6.55 us
    ppermute x1 -> x2, waiting for transfers between devices: 0.13 us -> 1.16 us  [the longest x1 1.15 us: body(): other = lax.ppermute(same, 'cell', swap)]
    pallas_call x10, Pallas kernels: 22.4 us -> 23.2 us  [call(): pl.pallas_call(kernel, out_shape=outs, in_specs=[spec(kind) for kind in k...]
  transfers between devices with their start and end apart: 6 -> 7, of which waited for: 4 -> 3; matrix products, arithmetic and copies ran while one was open for 2% -> 2% of each run, Pallas kernels for 15% -> 21%
where the time goes in v3:
time: 48.5 us; the launch traced here: 48.2 us
  Pallas kernels  23.2 us (48%)
  starting transfers between devices  11.8 us (24%)
  local copies, waits for them, and re-layouts  7.13 us (15%)
  waiting for transfers between devices  3.84 us (8%)
  other arithmetic  1.45 us (3%)
  between operations  0.78 us (2%)
    pallas_call x10, Pallas kernels, call(): pl.pallas_call(kernel, out_shape=outs, in_specs=[spec(kind) for kind in k...  23.2 us
    unnamed x26, local copies, waits for them, and re-layouts  6.55 us
    all_to_all x1, starting transfers between devices, body(): lax.all_to_all(jnp.broadcast_to(codes[None], (chips, cells)), 'cell', 0,...  6.32 us
    ppermute x4, starting transfers between devices, exchange(): return lax.ppermute(part, ('wl', 'cell'), pairs_of)  5.25 us
    ppermute x4, waiting for transfers between devices, exchange(): return lax.ppermute(part, ('wl', 'cell'), pairs_of)  2.68 us
    ppermute x1, waiting for transfers between devices, body(): other = lax.ppermute(same, 'cell', swap)  1.15 us
  transfers between devices with their start and end apart: 7, of which 3 were waited for; matrix products, arithmetic and copies ran while one was open for 2% of the time, Pallas kernels for 21%

profile of v3, /device:TPU:0, one launch (start us, length us, event | category | flops | bytes accessed | tf_op | source)
XLA Modules:
  0.0 48.2 jit_solution(353542301681042179)
XLA Ops:
  0.6 0.7 %shift-left_or_fusion.code_ref = s32[8]{0:T(128)S(1)} fusion(s32[8]{0:T(128)} %param.9, s32[8]{0:T(128)} %prof_ref.3), kind=kLoop, calls=%fused_computation.2 | loop fusion | flops 16 | bytes 96 | tf_op jit(solution)/shard_map/or | solution.py:415
  1.3 0.6 %broadcast_in_dim.4 = s32[4,1,8]{2,1,0:T(1,128)} broadcast(s32[8]{0:T(128)S(1)} %shift-left_or_fusion.code_ref), dimensions={2} | broadcast | bytes 160 | tf_op jit(solution)/shard_map/broadcast_in_dim | solution.py:417
  1.9 6.3 %all-to-all-start = ((s32[4,1,8]{2,1,0:T(1,128)}), s32[4,1,8]{2,1,0:T(1,128)S(1)}, u32[]{:S(2)}, u32[]{:S(2)}) async-start(s32[4,1,8]{2,1,0:T(1,128)} %broadcast_in_dim.4), calls=%async_computation | async-start | bytes 4096 | tf_op jit(solution)/shard_map/all_to_all | solution.py:416
  8.2 0.7 %bitcast_multiply_fusion = (f32[4,128]{1,0:T(4,128)S(1)}, f32[4,128]{1,0:T(4,128)S(1)}) fusion(f32[4,128]{1,0:T(4,128)} %param.10, f32[4,1,128]{2,0,1:T(4,128)} %bitcast.12), kind=kLoop, calls=%fused_computation | loop fusion | flops 1024 | bytes 8192 | tf_op jit(solution)/shard_map/mul | solution.py:401
  8.9 0.0 copy-start.2
  9.0 1.9 %copy-done.2 = f32[8,3,2,128,128]{4,3,2,1,0:T(8,128)S(1)} copy-done((f32[8,3,2,128,128]{4,3,2,1,0:T(8,128)S(1)}, f32[8,3,2,128,128]{4,3,2,1,0:T(8,128)}, u32[]{:S(2)}) %copy-start.2) | copy-done | bytes 3145752
  10.8 2.9 %own_tree.1 = (bf16[6,3,2,128,256]{4,3,2,1,0:T(8,128)(2,1)S(1)}, f32[3,128,256]{2,1,0:T(8,128)S(1)}, f32[4,2,8,128]{3,2,1,0:T(8,128)S(1)}, f32[4,2,128,128]{3,2,1,0:T(8,128)S(1)}) custom-call(s32[8]{0:T(128)S(1)} %shift-left_or_fusion.code_ref, f32[8,3,2,128,128]{4,3,2,1,0:T(8,128)S(1)} %copy-done.2, f32[4,128]{1,0:T(4,128)S(1)} %get-tuple-element.25.real_ref, ...), custom_call_target="tpu_custom_call" | custom-call | flops 2818572288 | bytes 4194304 | tf_op jit(solution)/shard_map/own_tree/pallas_call | solution.py:379
  13.8 1.4 %copy-done.5 = bf16[6,3,2,128,256]{4,3,2,1,0:T(8,128)(2,1)} copy-done((bf16[6,3,2,128,256]{4,3,2,1,0:T(8,128)(2,1)}, bf16[6,3,2,128,256]{4,3,2,1,0:T(8,128)(2,1)S(1)}, u32[]{:S(2)}) %copy-start.5) | copy-done | bytes 2359320
  15.2 0.8 %copy-done.7 = f32[4,2,128,128]{3,2,1,0:T(8,128)} copy-done((f32[4,2,128,128]{3,2,1,0:T(8,128)}, f32[4,2,128,128]{3,2,1,0:T(8,128)S(1)}, u32[]{:S(2)}) %copy-start.7) | copy-done | bytes 524312
  16.0 0.6 %copy-done.10 = f32[4,2,8,128]{3,2,1,0:T(8,128)} copy-done((f32[4,2,8,128]{3,2,1,0:T(8,128)}, f32[4,2,8,128]{3,2,1,0:T(8,128)S(1)}, u32[]{:S(2)}) %copy-start.10) | copy-done | bytes 32792
  16.6 1.2 %collective-permute-done.other_ref = s32[4,8]{1,0:T(4,128)S(1)} collective-permute-done((s32[4,8]{1,0:T(4,128)S(1)}, s32[4,8]{1,0:T(4,128)S(1)}, u32[]{:S(2)}, u32[]{:S(2)}) %collective-permute-start) | collective-permute-done | bytes 160 | tf_op jit(solution)/shard_map/ppermute | solution.py:421
  17.8 1.0 %copy-done.8 = f32[4,2,128,128]{3,2,1,0:T(8,128)S(1)} copy-done((f32[4,2,128,128]{3,2,1,0:T(8,128)S(1)}, f32[4,2,128,128]{3,2,1,0:T(8,128)}, u32[]{:S(2)}) %copy-start.8) | copy-done | bytes 524312
  18.8 0.8 %copy-done.11 = f32[4,2,8,128]{3,2,1,0:T(8,128)S(1)} copy-done((f32[4,2,8,128]{3,2,1,0:T(8,128)S(1)}, f32[4,2,8,128]{3,2,1,0:T(8,128)}, u32[]{:S(2)}) %copy-start.11) | copy-done | bytes 32792
  19.6 8.3 %far_trees.1.mine_ref = f32[9,128,256]{2,1,0:T(8,128)S(1)} custom-call(s32[1]{0:T(128)} %bitcast.me_ref, s32[4,8]{1,0:T(4,128)S(1)} %bitcast.10, s32[4,8]{1,0:T(4,128)S(1)} %collective-permute-done.other_ref, f32[8,3,2,128,128]{4,3,2,1,0:T(8,128)S(1)} %copy-done.3, f32[4,2,8,128]{3,2,1,0:T(8,128)S(1)} %copy-done.11, f32[4,2,128,128]{3,2,1,0:T(8,128)S(1)} %copy-done.8, ...), custom_call_target="tpu_custom_call" | custom-call | flops 9663676416 | bytes 4194304 | tf_op jit(solution)/shard_map/far_trees/pallas_call | solution.py:379
  27.9 0.2 collective-permute-start.1
  28.1 2.7 %own_scan.1 = (bf16[2,8,128,256]{3,2,1,0:T(8,128)(2,1)S(1)}, bf16[2,8,128,256]{3,2,1,0:T(8,128)(2,1)S(1)}, bf16[2,8,128,256]{3,2,1,0:T(8,128)(2,1)S(1)}) custom-call(s32[8]{0:T(128)S(1)} %shift-left_or_fusion.code_ref, f32[8,3,2,128,128]{4,3,2,1,0:T(8,128)S(1)} %copy-done.3, f32[4,2,8,128]{3,2,1,0:T(8,128)S(1)} %copy-done.12, ...), custom_call_target="tpu_custom_call" | custom-call | flops 2717908992 | bytes 4194304 | tf_op jit(solution)/shard_map/own_scan/pallas_call | solution.py:379
  30.9 0.0 collective-permute-done.1.theirs_ref
  30.9 1.5 %chain.1 = (bf16[2,2,256,256]{3,2,1,0:T(8,128)(2,1)S(1)}, f32[2,128,256]{2,1,0:T(8,128)S(1)}) custom-call(s32[1]{0:T(128)} %bitcast.me_ref, f32[2,128,128]{2,1,0:T(8,128)S(1)} %bitcast.11, f32[9,128,256]{2,1,0:T(8,128)S(1)} %far_trees.1.mine_ref, f32[9,128,256]{2,1,0:T(8,128)S(1)} %collective-permute-done.1.theirs_ref), custom_call_target="tpu_custom_call" | custom-call | flops 2013265920 | bytes 4194304 | tf_op jit(solution)/shard_map/chain/pallas_call | solution.py:379
  32.4 1.5 %couplings.3 = f32[328,128]{1,0:T(8,128)S(1)} custom-call(bf16[2,2,256,256]{3,2,1,0:T(8,128)(2,1)S(1)} %get-tuple-element.19.x_ref, bf16[2,8,128,256]{3,2,1,0:T(8,128)(2,1)S(1)} %get-tuple-element.21.grown_ref, bf16[2,8,128,256]{3,2,1,0:T(8,128)(2,1)S(1)} %get-tuple-element.22.back_ref, bf16[2,8,128,256]{3,2,1,0:T(8,128)(2,1)S(1)} %get-tuple-element.23.trans_ref), custom_call_target="tpu_custom_call" | custom-call | flops 1006632960 | bytes 4194304 | tf_op jit(solution)/shard_map/couplings/pallas_call | solution.py:379
  33.9 0.0 copy-start
  33.9 1.6 %collective-permute-start.4 = (f32[328,128]{1,0:T(8,128)S(1)}, f32[328,128]{1,0:T(8,128)S(1)}, u32[]{:S(2)}, u32[]{:S(2)}) collective-permute-start(f32[328,128]{1,0:T(8,128)S(1)} %couplings.3), channel_id=1, source_target_pairs={{0,8},{1,17},{2,10},{3,19},{4,12},{5,21},{6,14},{7,23},{8,0},{9,25... | collective-permute-start | bytes 503816 | tf_op jit(solution)/shard_map/ppermute | solution.py:465
  35.5 1.1 %couplings.2 = f32[200,128]{1,0:T(8,128)S(1)} custom-call(bf16[2,2,256,256]{3,2,1,0:T(8,128)(2,1)S(1)} %get-tuple-element.19.x_ref, bf16[2,8,128,256]{3,2,1,0:T(8,128)(2,1)S(1)} %get-tuple-element.21.grown_ref, bf16[2,8,128,256]{3,2,1,0:T(8,128)(2,1)S(1)} %get-tuple-element.22.back_ref, bf16[2,8,128,256]{3,2,1,0:T(8,128)(2,1)S(1)} %get-tuple-element.23.trans_ref), custom_call_target="tpu_custom_call" | custom-call | flops 1006632960 | bytes 4194304 | tf_op jit(solution)/shard_map/couplings/pallas_call | solution.py:379
  36.6 0.6 %collective-permute-start.2 = (f32[200,128]{1,0:T(8,128)S(1)}, f32[200,128]{1,0:T(8,128)S(1)}, u32[]{:S(2)}, u32[]{:S(2)}) collective-permute-start(f32[200,128]{1,0:T(8,128)S(1)} %couplings.2), channel_id=1, source_target_pairs={{0,8},{1,17},{2,10},{3,19},{4,12},{5,21},{6,14},{7,23},{8,0},{9,25... | collective-permute-start | bytes 307208 | tf_op jit(solution)/shard_map/ppermute | solution.py:465
  37.2 2.2 %collective-permute-done.4 = f32[328,128]{1,0:T(8,128)S(1)} collective-permute-done((f32[328,128]{1,0:T(8,128)S(1)}, f32[328,128]{1,0:T(8,128)S(1)}, u32[]{:S(2)}, u32[]{:S(2)}) %collective-permute-start.4) | collective-permute-done | bytes 167968 | tf_op jit(solution)/shard_map/ppermute | solution.py:465
  39.4 1.6 %collective-permute-start.5 = (f32[328,128]{1,0:T(8,128)S(1)}, f32[328,128]{1,0:T(8,128)S(1)}, u32[]{:S(2)}, u32[]{:S(2)}) collective-permute-start(f32[328,128]{1,0:T(8,128)S(1)} %add.7.mine_ref), channel_id=1, source_target_pairs={{0,16},{1,9},{2,18},{3,11},{4,20},{5,13},{6,22},{7,15},{8,24},{9,1... | collective-permute-start | bytes 503816 | tf_op jit(solution)/shard_map/ppermute | solution.py:465
  41.0 0.4 field_parts.1
  41.3 0.0 copy-start.1
  41.4 1.5 %collective-permute-start.3 = (f32[200,128]{1,0:T(8,128)S(1)}, f32[200,128]{1,0:T(8,128)S(1)}, u32[]{:S(2)}, u32[]{:S(2)}) collective-permute-start(f32[200,128]{1,0:T(8,128)S(1)} %add.6.mine_ref), channel_id=1, source_target_pairs={{0,16},{1,9},{2,18},{3,11},{4,20},{5,13},{6,22},{7,15},{8,24},{9,1... | collective-permute-start | bytes 307208 | tf_op jit(solution)/shard_map/ppermute | solution.py:465
  42.9 1.4 %reflection.1 = f32[2,16,128]{2,1,0:T(8,128)} custom-call(s32[1]{0:T(128)} %bitcast.me_ref, f32[9,128,256]{2,1,0:T(8,128)S(1)} %far_trees.1.mine_ref, f32[9,128,256]{2,1,0:T(8,128)S(1)} %collective-permute-done.1.theirs_ref, f32[2,128,256]{2,1,0:T(8,128)S(1)} %get-tuple-element.16.part_ref), custom_call_target="tpu_custom_call" | custom-call | flops 1006632960 | bytes 4194304 | tf_op jit(solution)/shard_map/reflection/pallas_call | solution.py:379
  44.3 0.5 %collective-permute-done.5.theirs_ref = f32[328,128]{1,0:T(8,128)S(1)} collective-permute-done((f32[328,128]{1,0:T(8,128)S(1)}, f32[328,128]{1,0:T(8,128)S(1)}, u32[]{:S(2)}, u32[]{:S(2)}) %collective-permute-start.5) | collective-permute-done | bytes 167968 | tf_op jit(solution)/shard_map/ppermute | solution.py:465
  44.8 1.5 %project.2.rest_0_ = f32[5,1024]{1,0:T(8,128)S(1)} custom-call(s32[8]{0:T(128)S(1)} %copy-done.1, bf16[4,128,1024]{2,1,0:T(8,128)(2,1)S(1)} %get-tuple-element.17.hi_ref, bf16[4,128,1024]{2,1,0:T(8,128)(2,1)S(1)} %get-tuple-element.18.lo_ref, f32[328,128]{1,0:T(8,128)S(1)} %add.7.mine_ref, f32[328,128]{1,0:T(8,128)S(1)} %collective-permute-done.5.theirs_ref), custom_call_target="tpu_custom_call" | custom-call | flops 402653184 | bytes 4194304 | tf_op jit(solution)/shard_map/project/pallas_call | solution.py:379
  46.4 1.8 %project.3 = f32[8,1024]{1,0:T(8,128)} custom-call(s32[8]{0:T(128)S(1)} %copy-done.1, bf16[4,128,1024]{2,1,0:T(8,128)(2,1)S(1)} %get-tuple-element.17.hi_ref, bf16[4,128,1024]{2,1,0:T(8,128)(2,1)S(1)} %get-tuple-element.18.lo_ref, f32[200,128]{1,0:T(8,128)S(1)} %add.6.mine_ref, f32[200,128]{1,0:T(8,128)S(1)} %collective-permute-done.3.theirs_ref, ...), custom_call_target="tpu_custom_call" | custom-call | flops 402653184 | bytes 4194304 | tf_op jit(solution)/shard_map/project/pallas_call | solution.py:379
  (23 shorter events, 0.1 us)
Async XLA Ops:
  1.9 14.7 %all-to-all-start = ((s32[4,1,8]{2,1,0:T(1,128)}), s32[4,1,8]{2,1,0:T(1,128)S(1)}, u32[]{:S(2)}, u32[]{:S(2)}) async-start(s32[4,1,8]{2,1,0:T(1,128)} %broadcast_in_dim.4), calls=%async_computation | async-start | bytes 4096 | tf_op jit(solution)/shard_map/all_to_all | solution.py:416
  8.9 1.9 %copy-start.2 = (f32[8,3,2,128,128]{4,3,2,1,0:T(8,128)S(1)}, f32[8,3,2,128,128]{4,3,2,1,0:T(8,128)}, u32[]{:S(2)}) copy-start(f32[8,3,2,128,128]{4,3,2,1,0:T(8,128)} %lib_ref.5) | copy-start | bytes 9437188
  10.8 6.9 %copy-start.3 = (f32[8,3,2,128,128]{4,3,2,1,0:T(8,128)S(1)}, f32[8,3,2,128,128]{4,3,2,1,0:T(8,128)}, u32[]{:S(2)}) copy-start(f32[8,3,2,128,128]{4,3,2,1,0:T(8,128)} %lib_ref.5) | copy-start | bytes 9437188
  13.8 1.4 %copy-start.5 = (bf16[6,3,2,128,256]{4,3,2,1,0:T(8,128)(2,1)}, bf16[6,3,2,128,256]{4,3,2,1,0:T(8,128)(2,1)S(1)}, u32[]{:S(2)}) copy-start(bf16[6,3,2,128,256]{4,3,2,1,0:T(8,128)(2,1)S(1)} %get-tuple-element.20.nodes_ref) | copy-start | bytes 7077892
  15.2 0.8 %copy-start.7 = (f32[4,2,128,128]{3,2,1,0:T(8,128)}, f32[4,2,128,128]{3,2,1,0:T(8,128)S(1)}, u32[]{:S(2)}) copy-start(f32[4,2,128,128]{3,2,1,0:T(8,128)S(1)} %get-tuple-element.14.col_ref) | copy-start | bytes 1572868
  16.0 0.6 %copy-start.10 = (f32[4,2,8,128]{3,2,1,0:T(8,128)}, f32[4,2,8,128]{3,2,1,0:T(8,128)S(1)}, u32[]{:S(2)}) copy-start(f32[4,2,8,128]{3,2,1,0:T(8,128)S(1)} %get-tuple-element.13.row_ref) | copy-start | bytes 98308
  16.6 1.2 %collective-permute-start = (s32[4,8]{1,0:T(4,128)S(1)}, s32[4,8]{1,0:T(4,128)S(1)}, u32[]{:S(2)}, u32[]{:S(2)}) collective-permute-start(s32[4,8]{1,0:T(4,128)S(1)} %bitcast.9), channel_id=1, source_target_pairs={{0,1},{1,0},{2,3},{3,2},{4,5},{5,4},{6,7},{7,6},{8,9},{9,8},{10,11... | collective-permute-start | bytes 392 | tf_op jit(solution)/shard_map/ppermute | solution.py:421
  17.8 1.0 %copy-start.8 = (f32[4,2,128,128]{3,2,1,0:T(8,128)S(1)}, f32[4,2,128,128]{3,2,1,0:T(8,128)}, u32[]{:S(2)}) copy-start(f32[4,2,128,128]{3,2,1,0:T(8,128)} %copy-done.7) | copy-start | bytes 1572868
  18.8 0.8 %copy-start.11 = (f32[4,2,8,128]{3,2,1,0:T(8,128)S(1)}, f32[4,2,8,128]{3,2,1,0:T(8,128)}, u32[]{:S(2)}) copy-start(f32[4,2,8,128]{3,2,1,0:T(8,128)} %copy-done.10) | copy-start | bytes 98308
  19.6 8.5 %copy-start.6 = (bf16[6,3,2,128,256]{4,3,2,1,0:T(8,128)(2,1)S(1)}, bf16[6,3,2,128,256]{4,3,2,1,0:T(8,128)(2,1)}, u32[]{:S(2)}) copy-start(bf16[6,3,2,128,256]{4,3,2,1,0:T(8,128)(2,1)} %copy-done.5) | copy-start | bytes 7077892
  19.6 8.5 %copy-start.9 = (f32[4,2,128,128]{3,2,1,0:T(8,128)S(1)}, f32[4,2,128,128]{3,2,1,0:T(8,128)}, u32[]{:S(2)}) copy-start(f32[4,2,128,128]{3,2,1,0:T(8,128)} %copy-done.7) | copy-start | bytes 1572868
  19.6 8.5 %copy-start.12 = (f32[4,2,8,128]{3,2,1,0:T(8,128)S(1)}, f32[4,2,8,128]{3,2,1,0:T(8,128)}, u32[]{:S(2)}) copy-start(f32[4,2,8,128]{3,2,1,0:T(8,128)} %copy-done.10) | copy-start | bytes 98308
  27.9 3.0 %collective-permute-start.1 = (f32[9,128,256]{2,1,0:T(8,128)S(1)}, f32[9,128,256]{2,1,0:T(8,128)S(1)}, u32[]{:S(2)}, u32[]{:S(2)}) collective-permute-start(f32[9,128,256]{2,1,0:T(8,128)S(1)} %far_trees.1.mine_ref), channel_id=1, source_target_pairs={{0,1},{1,0},{2,3},{3,2},{4,5},{5,4},{6,7},{7,6},{8,9},{9,8},{10,11... | collective-permute-start | bytes 3538952 | tf_op jit(solution)/shard_map/ppermute | solution.py:436
  28.1 2.8 %copy-start.4 = (f32[1,2,128,128]{3,2,1,0:T(8,128)S(1)}, f32[1,2,128,128]{3,2,1,0:T(8,128)}, u32[]{:S(2)}) copy-start(f32[1,2,128,128]{3,2,1,0:T(8,128)} %param.13) | copy-start | bytes 393220
  33.9 7.1 %copy-start = (f32[4,128,1024]{2,1,0:T(8,128)S(1)}, f32[4,128,1024]{2,1,0:T(8,128)}, u32[]{:S(2)}) copy-start(f32[4,128,1024]{2,1,0:T(8,128)} %field_ref.1) | copy-start | bytes 6291460
  33.9 5.4 %collective-permute-start.4 = (f32[328,128]{1,0:T(8,128)S(1)}, f32[328,128]{1,0:T(8,128)S(1)}, u32[]{:S(2)}, u32[]{:S(2)}) collective-permute-start(f32[328,128]{1,0:T(8,128)S(1)} %couplings.3), channel_id=1, source_target_pairs={{0,8},{1,17},{2,10},{3,19},{4,12},{5,21},{6,14},{7,23},{8,0},{9,25... | collective-permute-start | bytes 503816 | tf_op jit(solution)/shard_map/ppermute | solution.py:465
  36.6 4.8 %collective-permute-start.2 = (f32[200,128]{1,0:T(8,128)S(1)}, f32[200,128]{1,0:T(8,128)S(1)}, u32[]{:S(2)}, u32[]{:S(2)}) collective-permute-start(f32[200,128]{1,0:T(8,128)S(1)} %couplings.2), channel_id=1, source_target_pairs={{0,8},{1,17},{2,10},{3,19},{4,12},{5,21},{6,14},{7,23},{8,0},{9,25... | collective-permute-start | bytes 307208 | tf_op jit(solution)/shard_map/ppermute | solution.py:465
  39.4 5.4 %collective-permute-start.5 = (f32[328,128]{1,0:T(8,128)S(1)}, f32[328,128]{1,0:T(8,128)S(1)}, u32[]{:S(2)}, u32[]{:S(2)}) collective-permute-start(f32[328,128]{1,0:T(8,128)S(1)} %add.7.mine_ref), channel_id=1, source_target_pairs={{0,16},{1,9},{2,18},{3,11},{4,20},{5,13},{6,22},{7,15},{8,24},{9,1... | collective-permute-start | bytes 503816 | tf_op jit(solution)/shard_map/ppermute | solution.py:465
  41.3 3.5 %copy-start.1 = (s32[8]{0:T(128)S(1)}, s32[8]{0:T(128)}, u32[]{:S(2)}) copy-start(s32[8]{0:T(128)} %prof_ref.3) | copy-start | bytes 100
  41.4 5.0 %collective-permute-start.3 = (f32[200,128]{1,0:T(8,128)S(1)}, f32[200,128]{1,0:T(8,128)S(1)}, u32[]{:S(2)}, u32[]{:S(2)}) collective-permute-start(f32[200,128]{1,0:T(8,128)S(1)} %add.6.mine_ref), channel_id=1, source_target_pairs={{0,16},{1,9},{2,18},{3,11},{4,20},{5,13},{6,22},{7,15},{8,24},{9,1... | collective-permute-start | bytes 307208 | tf_op jit(solution)/shard_map/ppermute | solution.py:465

commit v4 on v3

--- a/solution.py
+++ b/solution.py
@@ -40,9 +40,10 @@
 
 def mul(left, weights):
     hi, lo = left
-    m = hi.shape[0]
-    both = dot(jnp.concatenate([hi, lo], axis=0), weights[0])
-    return both[:m] + both[m:] + dot(hi, weights[1])
+    return dot(
+        jnp.concatenate([hi, lo, hi], axis=1),
+        jnp.concatenate([weights[0], weights[0], weights[1]], axis=0),
+    )
 
 
 def get(ref, *at):
@@ -62,11 +63,12 @@
 def merge(former, latter):
     r1, t1, b1 = former
     r2, t2, b2 = latter
-    m = t1[0].shape[0]
-    z = split(mul(b1, right(r2)))
+    t1w = right(t1)
+    z = mul(b1, right(r2))
     back = mul(b1, right(b2))
-    both = mul([jnp.concatenate([a, b], axis=0) for a, b in zip(z, t2)], right(t1))
-    return split(whole(r1) + both[:m]), split(both[m:]), split(back)
+    trans = mul(t2, t1w)
+    refl = whole(r1) + mul(split(z), t1w)
+    return split(refl), split(trans), split(back)
 
 
 def triple(ref, *at):
@@ -182,13 +184,50 @@
     store(back_ref, 0, split(own_ref[BACK]))
 
 
-def far_kernel(
-    me_ref, same_ref, other_ref, lib_ref, row_ref, col_ref, own_ref,
-    out_ref,
-    pairs_ref, fours_ref, acc_ref,
-):
-    chips, cells = same_ref.shape
+def far_core(chip, block, chips):
+    if block < 2 * chip:
+        return int(block >= chip)
+    return int(block >= 2 * chip + 2 + chips - 1 - chip)
+
+
+def routes(chips):
+    blocks = 2 * chips
+    wanted = [
+        {2 * chip + far_core(chip, block, chips) for chip in range(chips) if chip != block // 2}
+        for block in range(blocks)
+    ]
+    found = []
+    for _ in range(chips - 1):
+        source = [None] * blocks
+
+        def place(block, seen):
+            for device in sorted(wanted[block] - seen):
+                seen.add(device)
+                if source[device] is None or place(source[device], seen):
+                    source[device] = block
+                    return True
+            return False
+
+        for block in range(blocks):
+            place(block, set())
+        for device, block in enumerate(source):
+            wanted[block].discard(device)
+        found.append(source)
+    return found
+
+
+def far_kernel(*refs):
+    me_ref, *got_refs = refs[:-9]
+    lib_ref, row_ref, col_ref, own_ref, out_ref, code_ref, pairs_ref, fours_ref, acc_ref = refs[-9:]
+    blocks, cells = code_ref.shape
+    chips = blocks // 2
     m = own_ref.shape[1]
+    for ref, source in zip(got_refs, routes(chips)):
+        k = source[0]
+        for device in range(1, blocks):
+            k = jnp.where(me_ref[0] == device, source[device], k)
+        for i in range(cells):
+            code_ref[k, i] = ref[i]
     chip = me_ref[0] >> 1
     core = me_ref[0] & 1
     right_count = chips - 1 - chip
@@ -208,8 +247,7 @@
         k = place(i)
 
         def cell(j):
-            same, other = same_ref[k >> 1, j], other_ref[k >> 1, j]
-            return leaf(lib_ref, row_ref, col_ref, jnp.where((k & 1) == core, same, other))
+            return leaf(lib_ref, row_ref, col_ref, code_ref[k, j])
 
         for j in range(cells // 2):
             keep_triple(
@@ -413,27 +451,26 @@
 
     tables = [f32(profiles, 2, 8, m), f32(profiles, 2, m, m)]
     codes = (cell_profile << SHIFT) | cell_section
-    same = lax.all_to_all(
-        jnp.broadcast_to(codes[None], (chips, cells)), "cell", 0, 0,
-        axis_index_groups=[list(range(core, blocks, 2)) for core in range(2)],
-    )
-    swap = [(i, i ^ 1) for i in range(blocks)]
-    other = lax.ppermute(same, "cell", swap)
+    got = [
+        lax.ppermute(codes, "cell", [(block, device) for device, block in enumerate(source)])
+        for source in routes(chips)
+    ]
     nodes, own, row_table, col_table = call(
         own_kernel, "own_tree", "svvv", [bf16(*pairs(6, 3)), f32(3, m, 2 * m), *tables], [], 12, 28,
         codes, interfaces, *factors,
     )
     mine = call(
-        far_kernel, "far_trees", "sssvvvv", f32(9, m, 2 * m),
+        far_kernel, "far_trees", "s" * chips + "vvvv", f32(9, m, 2 * m),
         [
+            pltpu.SMEM((blocks, cells), jnp.int32),
             pltpu.VMEM(pairs(chips - 1, cells // 2, 3), BF16),
             pltpu.VMEM(pairs(chips - 1, cells // 4, 3), BF16),
             pltpu.VMEM(pairs(2, 3), BF16),
         ],
         8 + 3 * blocks // 2, 32 * (chips - 1),
-        me, same, other, interfaces, row_table, col_table, own,
-    )
-    theirs = lax.ppermute(mine, "cell", swap)
+        me, *got, interfaces, row_table, col_table, own,
+    )
+    theirs = lax.ppermute(mine, "cell", [(i, i ^ 1) for i in range(blocks)])
     parts_shape = bf16(2, cells, m, 2 * m)
     grown, back, trans = call(
         scan_kernel, "own_scan", "svvvvv", [parts_shape] * 3, [], 16, 27,

time: 48.5 us -> 40.3 us (0.83)
  local copies, waits for them, and re-layouts: 7.13 us -> 1.91 us
  waiting for transfers between devices: 3.84 us -> 2.55 us
  starting transfers between devices: 11.8 us -> 10.9 us
  Pallas kernels: 23.2 us -> 22.5 us
    all_to_all x1 -> x0, starting transfers between devices: 6.32 us -> none  [body(): lax.all_to_all(jnp.broadcast_to(codes[None], (chips, cells)), 'cell', 0,...]
    ppermute x2 -> x4, starting transfers between devices: 0.24 us -> 5.68 us  [the longest x3 5.05 us: body(): lax.ppermute(codes, 'cell', [(block, device) for device, block in enumera...]
    unnamed x26 -> x10, local copies, waits for them, and re-layouts: 6.55 us -> 1.91 us
    ppermute x2 -> x4, waiting for transfers between devices: 1.16 us -> 0.01 us  [the longest x3 0.01 us: body(): lax.ppermute(codes, 'cell', [(block, device) for device, block in enumera...]
    pallas_call x10, Pallas kernels: 23.2 us -> 22.5 us  [call(): pl.pallas_call(kernel, out_shape=outs, in_specs=[spec(kind) for kind in k...]
    broadcast_in_dim x1 -> x0, local copies, waits for them, and re-layouts: 0.58 us -> none  [body(): jnp.broadcast_to(codes[None], (chips, cells))]
  transfers between devices with their start and end apart: 7 -> 8, of which waited for: 3 -> 2; matrix products, arithmetic and copies ran while one was open for 2% -> 2% of each run, Pallas kernels for 21% -> 25%
where the time goes in v4:
time: 40.3 us; the launch traced here: 40.1 us
  Pallas kernels  22.5 us (56%)
  starting transfers between devices  10.9 us (27%)
  waiting for transfers between devices  2.55 us (6%)
  local copies, waits for them, and re-layouts  1.91 us (5%)
  other arithmetic  1.45 us (4%)
  between operations  0.79 us (2%)
    pallas_call x10, Pallas kernels, call(): pl.pallas_call(kernel, out_shape=outs, in_specs=[spec(kind) for kind in k...  22.5 us
    ppermute x4, starting transfers between devices, exchange(): return lax.ppermute(part, ('wl', 'cell'), pairs_of)  5.25 us
    ppermute x3, starting transfers between devices, body(): lax.ppermute(codes, 'cell', [(block, device) for device, block in enumera...  5.05 us
    ppermute x4, waiting for transfers between devices, exchange(): return lax.ppermute(part, ('wl', 'cell'), pairs_of)  2.54 us
    unnamed x10, local copies, waits for them, and re-layouts  1.91 us
  transfers between devices with their start and end apart: 8, of which 2 were waited for; matrix products, arithmetic and copies ran while one was open for 2% of the time, Pallas kernels for 25%

profile of v4, /device:TPU:0, one launch (start us, length us, event | category | flops | bytes accessed | tf_op | source)
XLA Modules:
  0.0 40.1 jit_solution(323393434155020935)
XLA Ops:
  0.6 0.7 %shift-left_or_fusion.code_ref = s32[8]{0:T(128)S(1)} fusion(s32[8]{0:T(128)} %param.9, s32[8]{0:T(128)} %prof_ref.3), kind=kLoop, calls=%fused_computation.2 | loop fusion | flops 16 | bytes 96 | tf_op jit(solution)/shard_map/or | solution.py:453
  1.3 5.0 %collective-permute-start.2 = (s32[8]{0:T(128)S(1)}, s32[8]{0:T(128)S(1)}, u32[]{:S(2)}, u32[]{:S(2)}) collective-permute-start(s32[8]{0:T(128)S(1)} %shift-left_or_fusion.code_ref), channel_id=1, source_target_pairs={{2,0},{5,1},{4,2},{1,3},{6,4},{7,5},{0,6},{3,7},{10,8},{13,9},{12,... | collective-permute-start | bytes 104 | tf_op jit(solution)/shard_map/ppermute | solution.py:455
  6.4 0.0 collective-permute-start.1
  6.4 0.0 collective-permute-start
  6.4 0.7 %bitcast_multiply_fusion = (f32[4,128]{1,0:T(4,128)S(1)}, f32[4,128]{1,0:T(4,128)S(1)}) fusion(f32[4,128]{1,0:T(4,128)} %param.10, f32[4,1,128]{2,0,1:T(4,128)} %bitcast.9), kind=kLoop, calls=%fused_computation | loop fusion | flops 1024 | bytes 8192 | tf_op jit(solution)/shard_map/mul | solution.py:439
  7.1 0.0 copy-start.2
  7.1 1.9 %copy-done.2 = f32[8,3,2,128,128]{4,3,2,1,0:T(8,128)S(1)} copy-done((f32[8,3,2,128,128]{4,3,2,1,0:T(8,128)S(1)}, f32[8,3,2,128,128]{4,3,2,1,0:T(8,128)}, u32[]{:S(2)}) %copy-start.2) | copy-done | bytes 3145752
  9.0 2.8 %own_tree.1 = (bf16[6,3,2,128,256]{4,3,2,1,0:T(8,128)(2,1)S(1)}, f32[3,128,256]{2,1,0:T(8,128)S(1)}, f32[4,2,8,128]{3,2,1,0:T(8,128)S(1)}, f32[4,2,128,128]{3,2,1,0:T(8,128)S(1)}) custom-call(s32[8]{0:T(128)S(1)} %shift-left_or_fusion.code_ref, f32[8,3,2,128,128]{4,3,2,1,0:T(8,128)S(1)} %copy-done.2, f32[4,128]{1,0:T(4,128)S(1)} %get-tuple-element.25.real_ref, ...), custom_call_target="tpu_custom_call" | custom-call | flops 2818572288 | bytes 4194304 | tf_op jit(solution)/shard_map/own_tree/pallas_call | solution.py:417
  11.8 0.0 collective-permute-done.2.refs_3_
  11.8 0.0 collective-permute-done.1.refs_2_
  11.8 0.0 collective-permute-done.refs_1_
  11.8 7.7 %far_trees.1.mine_ref = f32[9,128,256]{2,1,0:T(8,128)S(1)} custom-call(s32[1]{0:T(128)} %bitcast.refs_0_.me_ref, s32[8]{0:T(128)S(1)} %collective-permute-done.refs_1_, s32[8]{0:T(128)S(1)} %collective-permute-done.1.refs_2_, s32[8]{0:T(128)S(1)} %collective-permute-done.2.refs_3_, f32[8,3,2,128,128]{4,3,2,1,0:T(8,128)S(1)} %copy-done.3, ...), custom_call_target="tpu_custom_call" | custom-call | flops 9663676416 | bytes 4194304 | tf_op jit(solution)/shard_map/far_trees/pallas_call | solution.py:417
  19.5 0.6 %collective-permute-start.3 = (f32[9,128,256]{2,1,0:T(8,128)S(1)}, f32[9,128,256]{2,1,0:T(8,128)S(1)}, u32[]{:S(2)}, u32[]{:S(2)}) collective-permute-start(f32[9,128,256]{2,1,0:T(8,128)S(1)} %far_trees.1.mine_ref), channel_id=1, source_target_pairs={{0,1},{1,0},{2,3},{3,2},{4,5},{5,4},{6,7},{7,6},{8,9},{9,8},{10,11... | collective-permute-start | bytes 3538952 | tf_op jit(solution)/shard_map/ppermute | solution.py:473
  20.1 2.6 %own_scan.1 = (bf16[2,8,128,256]{3,2,1,0:T(8,128)(2,1)S(1)}, bf16[2,8,128,256]{3,2,1,0:T(8,128)(2,1)S(1)}, bf16[2,8,128,256]{3,2,1,0:T(8,128)(2,1)S(1)}) custom-call(s32[8]{0:T(128)S(1)} %shift-left_or_fusion.code_ref, f32[8,3,2,128,128]{4,3,2,1,0:T(8,128)S(1)} %copy-done.3, f32[4,2,8,128]{3,2,1,0:T(8,128)S(1)} %get-tuple-element.13.refs_5_.row_ref, ...), custom_call_target="tpu_custom_call" | custom-call | flops 2717908992 | bytes 4194304 | tf_op jit(solution)/shard_map/own_scan/pallas_call | solution.py:417
  22.7 0.0 collective-permute-done.3.theirs_ref
  22.8 1.5 %chain.1 = (bf16[2,2,256,256]{3,2,1,0:T(8,128)(2,1)S(1)}, f32[2,128,256]{2,1,0:T(8,128)S(1)}) custom-call(s32[1]{0:T(128)} %bitcast.refs_0_.me_ref, f32[2,128,128]{2,1,0:T(8,128)S(1)} %bitcast.8, f32[9,128,256]{2,1,0:T(8,128)S(1)} %far_trees.1.mine_ref, f32[9,128,256]{2,1,0:T(8,128)S(1)} %collective-permute-done.3.theirs_ref), custom_call_target="tpu_custom_call" | custom-call | flops 2013265920 | bytes 4194304 | tf_op jit(solution)/shard_map/chain/pallas_call | solution.py:417
  24.3 1.5 %couplings.3 = f32[328,128]{1,0:T(8,128)S(1)} custom-call(bf16[2,2,256,256]{3,2,1,0:T(8,128)(2,1)S(1)} %get-tuple-element.19.x_ref, bf16[2,8,128,256]{3,2,1,0:T(8,128)(2,1)S(1)} %get-tuple-element.21.grown_ref, bf16[2,8,128,256]{3,2,1,0:T(8,128)(2,1)S(1)} %get-tuple-element.22.back_ref, bf16[2,8,128,256]{3,2,1,0:T(8,128)(2,1)S(1)} %get-tuple-element.23.trans_ref), custom_call_target="tpu_custom_call" | custom-call | flops 1006632960 | bytes 4194304 | tf_op jit(solution)/shard_map/couplings/pallas_call | solution.py:417
  25.8 0.0 copy-start
  25.8 1.5 %collective-permute-start.6 = (f32[328,128]{1,0:T(8,128)S(1)}, f32[328,128]{1,0:T(8,128)S(1)}, u32[]{:S(2)}, u32[]{:S(2)}) collective-permute-start(f32[328,128]{1,0:T(8,128)S(1)} %couplings.3), channel_id=1, source_target_pairs={{0,8},{1,17},{2,10},{3,19},{4,12},{5,21},{6,14},{7,23},{8,0},{9,25... | collective-permute-start | bytes 503816 | tf_op jit(solution)/shard_map/ppermute | solution.py:502
  27.4 1.1 %couplings.2 = f32[200,128]{1,0:T(8,128)S(1)} custom-call(bf16[2,2,256,256]{3,2,1,0:T(8,128)(2,1)S(1)} %get-tuple-element.19.x_ref, bf16[2,8,128,256]{3,2,1,0:T(8,128)(2,1)S(1)} %get-tuple-element.21.grown_ref, bf16[2,8,128,256]{3,2,1,0:T(8,128)(2,1)S(1)} %get-tuple-element.22.back_ref, bf16[2,8,128,256]{3,2,1,0:T(8,128)(2,1)S(1)} %get-tuple-element.23.trans_ref), custom_call_target="tpu_custom_call" | custom-call | flops 1006632960 | bytes 4194304 | tf_op jit(solution)/shard_map/couplings/pallas_call | solution.py:417
  28.5 0.6 %collective-permute-start.4 = (f32[200,128]{1,0:T(8,128)S(1)}, f32[200,128]{1,0:T(8,128)S(1)}, u32[]{:S(2)}, u32[]{:S(2)}) collective-permute-start(f32[200,128]{1,0:T(8,128)S(1)} %couplings.2), channel_id=1, source_target_pairs={{0,8},{1,17},{2,10},{3,19},{4,12},{5,21},{6,14},{7,23},{8,0},{9,25... | collective-permute-start | bytes 307208 | tf_op jit(solution)/shard_map/ppermute | solution.py:502
  29.1 2.2 %collective-permute-done.6 = f32[328,128]{1,0:T(8,128)S(1)} collective-permute-done((f32[328,128]{1,0:T(8,128)S(1)}, f32[328,128]{1,0:T(8,128)S(1)}, u32[]{:S(2)}, u32[]{:S(2)}) %collective-permute-start.6) | collective-permute-done | bytes 167968 | tf_op jit(solution)/shard_map/ppermute | solution.py:502
  31.3 1.6 %collective-permute-start.7 = (f32[328,128]{1,0:T(8,128)S(1)}, f32[328,128]{1,0:T(8,128)S(1)}, u32[]{:S(2)}, u32[]{:S(2)}) collective-permute-start(f32[328,128]{1,0:T(8,128)S(1)} %add.7.mine_ref), channel_id=1, source_target_pairs={{0,16},{1,9},{2,18},{3,11},{4,20},{5,13},{6,22},{7,15},{8,24},{9,1... | collective-permute-start | bytes 503816 | tf_op jit(solution)/shard_map/ppermute | solution.py:502
  32.9 0.4 field_parts.1
  33.2 0.0 copy-start.1
  33.3 0.0 collective-permute-done.4
  33.3 1.5 %collective-permute-start.5 = (f32[200,128]{1,0:T(8,128)S(1)}, f32[200,128]{1,0:T(8,128)S(1)}, u32[]{:S(2)}, u32[]{:S(2)}) collective-permute-start(f32[200,128]{1,0:T(8,128)S(1)} %add.6.mine_ref), channel_id=1, source_target_pairs={{0,16},{1,9},{2,18},{3,11},{4,20},{5,13},{6,22},{7,15},{8,24},{9,1... | collective-permute-start | bytes 307208 | tf_op jit(solution)/shard_map/ppermute | solution.py:502
  34.8 1.5 %reflection.1 = f32[2,16,128]{2,1,0:T(8,128)} custom-call(s32[1]{0:T(128)} %bitcast.refs_0_.me_ref, f32[9,128,256]{2,1,0:T(8,128)S(1)} %far_trees.1.mine_ref, f32[9,128,256]{2,1,0:T(8,128)S(1)} %collective-permute-done.3.theirs_ref, f32[2,128,256]{2,1,0:T(8,128)S(1)} %get-tuple-element.16.part_ref), custom_call_target="tpu_custom_call" | custom-call | flops 1006632960 | bytes 4194304 | tf_op jit(solution)/shard_map/reflection/pallas_call | solution.py:417
  36.4 0.4 collective-permute-done.7.theirs_ref
  36.7 1.5 %project.2.rest_0_ = f32[5,1024]{1,0:T(8,128)S(1)} custom-call(s32[8]{0:T(128)S(1)} %copy-done.1, bf16[4,128,1024]{2,1,0:T(8,128)(2,1)S(1)} %get-tuple-element.17.hi_ref, bf16[4,128,1024]{2,1,0:T(8,128)(2,1)S(1)} %get-tuple-element.18.lo_ref, f32[328,128]{1,0:T(8,128)S(1)} %add.7.mine_ref, f32[328,128]{1,0:T(8,128)S(1)} %collective-permute-done.7.theirs_ref), custom_call_target="tpu_custom_call" | custom-call | flops 402653184 | bytes 4194304 | tf_op jit(solution)/shard_map/project/pallas_call | solution.py:417
  38.2 0.0 collective-permute-done.5.theirs_ref
  38.3 1.8 %project.3 = f32[8,1024]{1,0:T(8,128)} custom-call(s32[8]{0:T(128)S(1)} %copy-done.1, bf16[4,128,1024]{2,1,0:T(8,128)(2,1)S(1)} %get-tuple-element.17.hi_ref, bf16[4,128,1024]{2,1,0:T(8,128)(2,1)S(1)} %get-tuple-element.18.lo_ref, f32[200,128]{1,0:T(8,128)S(1)} %add.6.mine_ref, f32[200,128]{1,0:T(8,128)S(1)} %collective-permute-done.5.theirs_ref, ...), custom_call_target="tpu_custom_call" | custom-call | flops 402653184 | bytes 4194304 | tf_op jit(solution)/shard_map/project/pallas_call | solution.py:417
  (8 shorter events, 0.0 us)
Async XLA Ops:
  1.3 10.5 %collective-permute-start.2 = (s32[8]{0:T(128)S(1)}, s32[8]{0:T(128)S(1)}, u32[]{:S(2)}, u32[]{:S(2)}) collective-permute-start(s32[8]{0:T(128)S(1)} %shift-left_or_fusion.code_ref), channel_id=1, source_target_pairs={{2,0},{5,1},{4,2},{1,3},{6,4},{7,5},{0,6},{3,7},{10,8},{13,9},{12,... | collective-permute-start | bytes 104 | tf_op jit(solution)/shard_map/ppermute | solution.py:455
  6.4 5.4 %collective-permute-start.1 = (s32[8]{0:T(128)S(1)}, s32[8]{0:T(128)S(1)}, u32[]{:S(2)}, u32[]{:S(2)}) collective-permute-start(s32[8]{0:T(128)S(1)} %shift-left_or_fusion.code_ref), channel_id=1, source_target_pairs={{3,0},{6,1},{5,2},{7,3},{0,4},{2,5},{1,6},{4,7},{11,8},{14,9},{13,... | collective-permute-start | bytes 104 | tf_op jit(solution)/shard_map/ppermute | solution.py:455
  6.4 5.4 %collective-permute-start = (s32[8]{0:T(128)S(1)}, s32[8]{0:T(128)S(1)}, u32[]{:S(2)}, u32[]{:S(2)}) collective-permute-start(s32[8]{0:T(128)S(1)} %shift-left_or_fusion.code_ref), channel_id=1, source_target_pairs={{4,0},{7,1},{0,2},{6,3},{1,4},{3,5},{2,6},{5,7},{12,8},{15,9},{8,1... | collective-permute-start | bytes 104 | tf_op jit(solution)/shard_map/ppermute | solution.py:455
  7.1 1.9 %copy-start.2 = (f32[8,3,2,128,128]{4,3,2,1,0:T(8,128)S(1)}, f32[8,3,2,128,128]{4,3,2,1,0:T(8,128)}, u32[]{:S(2)}) copy-start(f32[8,3,2,128,128]{4,3,2,1,0:T(8,128)} %lib_ref.3) | copy-start | bytes 9437188
  9.0 2.8 %copy-start.3 = (f32[8,3,2,128,128]{4,3,2,1,0:T(8,128)S(1)}, f32[8,3,2,128,128]{4,3,2,1,0:T(8,128)}, u32[]{:S(2)}) copy-start(f32[8,3,2,128,128]{4,3,2,1,0:T(8,128)} %lib_ref.3) | copy-start | bytes 9437188
  19.5 3.3 %collective-permute-start.3 = (f32[9,128,256]{2,1,0:T(8,128)S(1)}, f32[9,128,256]{2,1,0:T(8,128)S(1)}, u32[]{:S(2)}, u32[]{:S(2)}) collective-permute-start(f32[9,128,256]{2,1,0:T(8,128)S(1)} %far_trees.1.mine_ref), channel_id=1, source_target_pairs={{0,1},{1,0},{2,3},{3,2},{4,5},{5,4},{6,7},{7,6},{8,9},{9,8},{10,11... | collective-permute-start | bytes 3538952 | tf_op jit(solution)/shard_map/ppermute | solution.py:473
  20.1 2.7 %copy-start.4 = (f32[1,2,128,128]{3,2,1,0:T(8,128)S(1)}, f32[1,2,128,128]{3,2,1,0:T(8,128)}, u32[]{:S(2)}) copy-start(f32[1,2,128,128]{3,2,1,0:T(8,128)} %param.13) | copy-start | bytes 393220
  25.8 7.0 %copy-start = (f32[4,128,1024]{2,1,0:T(8,128)S(1)}, f32[4,128,1024]{2,1,0:T(8,128)}, u32[]{:S(2)}) copy-start(f32[4,128,1024]{2,1,0:T(8,128)} %field_ref.1) | copy-start | bytes 6291460
  25.8 5.4 %collective-permute-start.6 = (f32[328,128]{1,0:T(8,128)S(1)}, f32[328,128]{1,0:T(8,128)S(1)}, u32[]{:S(2)}, u32[]{:S(2)}) collective-permute-start(f32[328,128]{1,0:T(8,128)S(1)} %couplings.3), channel_id=1, source_target_pairs={{0,8},{1,17},{2,10},{3,19},{4,12},{5,21},{6,14},{7,23},{8,0},{9,25... | collective-permute-start | bytes 503816 | tf_op jit(solution)/shard_map/ppermute | solution.py:502
  28.5 4.8 %collective-permute-start.4 = (f32[200,128]{1,0:T(8,128)S(1)}, f32[200,128]{1,0:T(8,128)S(1)}, u32[]{:S(2)}, u32[]{:S(2)}) collective-permute-start(f32[200,128]{1,0:T(8,128)S(1)} %couplings.2), channel_id=1, source_target_pairs={{0,8},{1,17},{2,10},{3,19},{4,12},{5,21},{6,14},{7,23},{8,0},{9,25... | collective-permute-start | bytes 307208 | tf_op jit(solution)/shard_map/ppermute | solution.py:502
  31.3 5.4 %collective-permute-start.7 = (f32[328,128]{1,0:T(8,128)S(1)}, f32[328,128]{1,0:T(8,128)S(1)}, u32[]{:S(2)}, u32[]{:S(2)}) collective-permute-start(f32[328,128]{1,0:T(8,128)S(1)} %add.7.mine_ref), channel_id=1, source_target_pairs={{0,16},{1,9},{2,18},{3,11},{4,20},{5,13},{6,22},{7,15},{8,24},{9,1... | collective-permute-start | bytes 503816 | tf_op jit(solution)/shard_map/ppermute | solution.py:502
  33.2 3.5 %copy-start.1 = (s32[8]{0:T(128)S(1)}, s32[8]{0:T(128)}, u32[]{:S(2)}) copy-start(s32[8]{0:T(128)} %prof_ref.3) | copy-start | bytes 100
  33.3 5.0 %collective-permute-start.5 = (f32[200,128]{1,0:T(8,128)S(1)}, f32[200,128]{1,0:T(8,128)S(1)}, u32[]{:S(2)}, u32[]{:S(2)}) collective-permute-start(f32[200,128]{1,0:T(8,128)S(1)} %add.6.mine_ref), channel_id=1, source_target_pairs={{0,16},{1,9},{2,18},{3,11},{4,20},{5,13},{6,22},{7,15},{8,24},{9,1... | collective-permute-start | bytes 307208 | tf_op jit(solution)/shard_map/ppermute | solution.py:502

commit v5 on v4

--- a/solution.py
+++ b/solution.py
@@ -38,12 +38,16 @@
     return jnp.dot(a, b, preferred_element_type=F32)
 
 
+def deep(left):
+    return jnp.concatenate([left[0], left[1], left[0]], axis=1)
+
+
+def tall(weights):
+    return jnp.concatenate([weights[0], weights[0], weights[1]], axis=0)
+
+
 def mul(left, weights):
-    hi, lo = left
-    return dot(
-        jnp.concatenate([hi, lo, hi], axis=1),
-        jnp.concatenate([weights[0], weights[0], weights[1]], axis=0),
-    )
+    return dot(deep(left), tall(weights))
 
 
 def get(ref, *at):
@@ -63,12 +67,12 @@
 def merge(former, latter):
     r1, t1, b1 = former
     r2, t2, b2 = latter
-    t1w = right(t1)
-    z = mul(b1, right(r2))
-    back = mul(b1, right(b2))
-    trans = mul(t2, t1w)
-    refl = whole(r1) + mul(split(z), t1w)
-    return split(refl), split(trans), split(back)
+    m = t1[0].shape[0]
+    t1w = tall(right(t1))
+    both = dot(deep(b1), jnp.concatenate([tall(right(r2)), tall(right(b2))], axis=1))
+    trans = dot(deep(t2), t1w)
+    refl = whole(r1) + dot(deep(split(both[:, : 2 * m])), t1w)
+    return split(refl), split(trans), split(both[:, 2 * m :])
 
 
 def triple(ref, *at):
@@ -258,7 +262,11 @@
             )
         return 0
 
-    lax.fori_loop(0, chips - 1, pair_step, 0)
+    if chips <= 4:
+        for i in range(chips - 1):
+            pair_step(i, 0)
+    else:
+        lax.fori_loop(0, chips - 1, pair_step, 0)
     for i in range(chips - 1):
         for j in range(cells // 4):
             keep_triple(
@@ -374,6 +382,14 @@
         out_ref[group * h + j : group * h + j + 1] = jnp.sum(
             jnp.where(eye, c, 0.0), axis=0, keepdims=True
         )
+
+
+def first_kernel(
+    group, me_ref, target_ref, mine_ref, theirs_ref, grown_ref, back_ref, trans_ref,
+    x_ref, part_ref, out_ref,
+):
+    chain_kernel(me_ref, target_ref, mine_ref, theirs_ref, x_ref, part_ref)
+    coupling_kernel(0, group, x_ref, grown_ref, back_ref, trans_ref, out_ref)
 
 
 def field_kernel(field_ref, hi_ref, lo_ref):
@@ -401,8 +417,8 @@
         ch, cl = split(c)
         q = prof_ref[start + j]
         fh, fl = hi_ref[q], lo_ref[q]
-        w = dot(jnp.concatenate([ch, cl], axis=1), jnp.concatenate([fh, fh], axis=0))
-        w = w + dot(ch, fl)
+        both = dot(jnp.concatenate([ch, cl], axis=0), fh)
+        w = both[:m] + both[m:] + dot(ch, fl)
         i = start + j
         out_ref[i : i + 1] = jnp.sum(
             (fh.astype(F32) + fl.astype(F32)) * w, axis=0, keepdims=True
@@ -476,9 +492,22 @@
         scan_kernel, "own_scan", "svvvvv", [parts_shape] * 3, [], 16, 27,
         codes, interfaces, row_table, col_table, nodes, own,
     )
-    x, part = call(
-        chain_kernel, "chain", "svvv", [bf16(2, 2, 2 * m, 2 * m), f32(2, m, 2 * m)], [], 12, 20,
-        me, wanted, mine, theirs,
+    def packed_shape(group):
+        return f32(group * (m // 2) + 8, m)
+
+    more = cells - FEWER
+    x, part, packed = call(
+        functools.partial(first_kernel, more), "couplings", "svvvvvv",
+        [bf16(2, 2, 2 * m, 2 * m), f32(2, m, 2 * m), packed_shape(more)], [], 12, 35,
+        me, wanted, mine, theirs, grown, back, trans,
+    )
+    groups = [packed]
+    groups.append(
+        call(
+            functools.partial(coupling_kernel, more, FEWER), "couplings", "vvvv",
+            packed_shape(FEWER), [], 12, 10,
+            x, grown, back, trans,
+        )
     )
     reflection = call(
         reflect_kernel, "reflection", "svvv", f32(2, m // blocks, m),
@@ -505,12 +534,7 @@
     fields = call(field_kernel, "field_parts", "v", [field, field], [], 12, 1, mode_field)
     gradient = []
     start = 0
-    for group in (cells - FEWER, FEWER):
-        packed = call(
-            functools.partial(coupling_kernel, start, group), "couplings", "vvvv",
-            f32(group * (m // 2) + 8, m), [], 12, 10,
-            x, grown, back, trans,
-        )
+    for group, packed in zip((more, FEWER), groups):
         other = jnp.zeros_like(packed)
         for number in range(len(steps)):
             if number:

time: 40.3 us -> 40.3 us (level)
    pallas_call x10 -> x9, Pallas kernels: 22.5 us -> 22.5 us  [call(): pl.pallas_call(kernel, out_shape=outs, in_specs=[spec(kind) for kind in k...]
where the time goes in v5:
time: 40.3 us; the launch traced here: 40.1 us
  Pallas kernels  22.5 us (56%)
  starting transfers between devices  10.9 us (27%)
  waiting for transfers between devices  2.54 us (6%)
  local copies, waits for them, and re-layouts  1.9 us (5%)
  other arithmetic  1.45 us (4%)
  between operations  0.77 us (2%)
    pallas_call x9, Pallas kernels, call(): pl.pallas_call(kernel, out_shape=outs, in_specs=[spec(kind) for kind in k...  22.5 us
    ppermute x4, starting transfers between devices, exchange(): return lax.ppermute(part, ('wl', 'cell'), pairs_of)  5.26 us
    ppermute x3, starting transfers between devices, body(): lax.ppermute(codes, 'cell', [(block, device) for device, block in enumera...  5.05 us
    ppermute x4, waiting for transfers between devices, exchange(): return lax.ppermute(part, ('wl', 'cell'), pairs_of)  2.53 us
    unnamed x10, local copies, waits for them, and re-layouts  1.9 us
  transfers between devices with their start and end apart: 8, of which 2 were waited for; matrix products, arithmetic and copies ran while one was open for 2% of the time, Pallas kernels for 25%

profile of v5, /device:TPU:0, one launch (start us, length us, event | category | flops | bytes accessed | tf_op | source)
XLA Modules:
  0.0 40.1 jit_solution(3416248691877558144)
XLA Ops:
  0.6 0.7 %shift-left_or_fusion.code_ref = s32[8]{0:T(128)S(1)} fusion(s32[8]{0:T(128)} %param.9, s32[8]{0:T(128)} %prof_ref.3), kind=kLoop, calls=%fused_computation.2 | loop fusion | flops 16 | bytes 96 | tf_op jit(solution)/shard_map/or | solution.py:469
  1.3 5.0 %collective-permute-start.2 = (s32[8]{0:T(128)S(1)}, s32[8]{0:T(128)S(1)}, u32[]{:S(2)}, u32[]{:S(2)}) collective-permute-start(s32[8]{0:T(128)S(1)} %shift-left_or_fusion.code_ref), channel_id=1, source_target_pairs={{2,0},{5,1},{4,2},{1,3},{6,4},{7,5},{0,6},{3,7},{10,8},{13,9},{12,... | collective-permute-start | bytes 104 | tf_op jit(solution)/shard_map/ppermute | solution.py:471
  6.4 0.0 collective-permute-start.1
  6.4 0.0 collective-permute-start
  6.4 0.7 %bitcast_multiply_fusion = (f32[4,128]{1,0:T(4,128)S(1)}, f32[4,128]{1,0:T(4,128)S(1)}) fusion(f32[4,128]{1,0:T(4,128)} %param.10, f32[4,1,128]{2,0,1:T(4,128)} %bitcast.9), kind=kLoop, calls=%fused_computation | loop fusion | flops 1024 | bytes 8192 | tf_op jit(solution)/shard_map/mul | solution.py:455
  7.1 0.0 copy-start.2
  7.1 1.9 %copy-done.2 = f32[8,3,2,128,128]{4,3,2,1,0:T(8,128)S(1)} copy-done((f32[8,3,2,128,128]{4,3,2,1,0:T(8,128)S(1)}, f32[8,3,2,128,128]{4,3,2,1,0:T(8,128)}, u32[]{:S(2)}) %copy-start.2) | copy-done | bytes 3145752
  9.0 2.8 %own_tree.1 = (bf16[6,3,2,128,256]{4,3,2,1,0:T(8,128)(2,1)S(1)}, f32[3,128,256]{2,1,0:T(8,128)S(1)}, f32[4,2,8,128]{3,2,1,0:T(8,128)S(1)}, f32[4,2,128,128]{3,2,1,0:T(8,128)S(1)}) custom-call(s32[8]{0:T(128)S(1)} %shift-left_or_fusion.code_ref, f32[8,3,2,128,128]{4,3,2,1,0:T(8,128)S(1)} %copy-done.2, f32[4,128]{1,0:T(4,128)S(1)} %get-tuple-element.27.real_ref, ...), custom_call_target="tpu_custom_call" | custom-call | flops 2818572288 | bytes 4194304 | tf_op jit(solution)/shard_map/own_tree/pallas_call | solution.py:433
  11.8 0.0 collective-permute-done.2.refs_3_
  11.8 0.0 collective-permute-done.1.refs_2_
  11.8 0.0 collective-permute-done.refs_1_
  11.8 0.0 copy-done.3
  11.8 7.1 %far_trees.1.mine_ref = f32[9,128,256]{2,1,0:T(8,128)S(1)} custom-call(s32[1]{0:T(128)} %bitcast.refs_0_.me_ref, s32[8]{0:T(128)S(1)} %collective-permute-done.refs_1_, s32[8]{0:T(128)S(1)} %collective-permute-done.1.refs_2_, s32[8]{0:T(128)S(1)} %collective-permute-done.2.refs_3_, f32[8,3,2,128,128]{4,3,2,1,0:T(8,128)S(1)} %copy-done.3, ...), custom_call_target="tpu_custom_call" | custom-call | flops 9663676416 | bytes 4194304 | tf_op jit(solution)/shard_map/far_trees/pallas_call | solution.py:433
  18.9 0.6 %collective-permute-start.3 = (f32[9,128,256]{2,1,0:T(8,128)S(1)}, f32[9,128,256]{2,1,0:T(8,128)S(1)}, u32[]{:S(2)}, u32[]{:S(2)}) collective-permute-start(f32[9,128,256]{2,1,0:T(8,128)S(1)} %far_trees.1.mine_ref), channel_id=1, source_target_pairs={{0,1},{1,0},{2,3},{3,2},{4,5},{5,4},{6,7},{7,6},{8,9},{9,8},{10,11... | collective-permute-start | bytes 3538952 | tf_op jit(solution)/shard_map/ppermute | solution.py:489
  19.5 2.6 %own_scan.1 = (bf16[2,8,128,256]{3,2,1,0:T(8,128)(2,1)S(1)}, bf16[2,8,128,256]{3,2,1,0:T(8,128)(2,1)S(1)}, bf16[2,8,128,256]{3,2,1,0:T(8,128)(2,1)S(1)}) custom-call(s32[8]{0:T(128)S(1)} %shift-left_or_fusion.code_ref, f32[8,3,2,128,128]{4,3,2,1,0:T(8,128)S(1)} %copy-done.3, f32[4,2,8,128]{3,2,1,0:T(8,128)S(1)} %get-tuple-element.14.refs_5_.row_ref, ...), custom_call_target="tpu_custom_call" | custom-call | flops 2717908992 | bytes 4194304 | tf_op jit(solution)/shard_map/own_scan/pallas_call | solution.py:433
  22.2 0.0 collective-permute-done.3.theirs_ref
  22.2 0.0 copy-done.4
  22.2 3.2 %couplings.2 = (bf16[2,2,256,256]{3,2,1,0:T(8,128)(2,1)S(1)}, f32[2,128,256]{2,1,0:T(8,128)S(1)}, f32[328,128]{1,0:T(8,128)S(1)}) custom-call(s32[1]{0:T(128)} %bitcast.refs_0_.me_ref, f32[2,128,128]{2,1,0:T(8,128)S(1)} %bitcast.8, f32[9,128,256]{2,1,0:T(8,128)S(1)} %far_trees.1.mine_ref, f32[9,128,256]{2,1,0:T(8,128)S(1)} %collective-permute-done.3.theirs_ref, ...), custom_call_target="tpu_custom_call" | custom-call | flops 3523215360 | bytes 4194304 | tf_op jit(solution)/shard_map/couplings/pallas_call | solution.py:433
  25.4 1.6 %collective-permute-start.6 = (f32[328,128]{1,0:T(8,128)S(1)}, f32[328,128]{1,0:T(8,128)S(1)}, u32[]{:S(2)}, u32[]{:S(2)}) collective-permute-start(f32[328,128]{1,0:T(8,128)S(1)} %get-tuple-element.25), channel_id=1, source_target_pairs={{0,8},{1,17},{2,10},{3,19},{4,12},{5,21},{6,14},{7,23},{8,0},{9,25... | collective-permute-start | bytes 503816 | tf_op jit(solution)/shard_map/ppermute | solution.py:531
  26.9 1.1 %couplings.3 = f32[200,128]{1,0:T(8,128)S(1)} custom-call(bf16[2,2,256,256]{3,2,1,0:T(8,128)(2,1)S(1)} %get-tuple-element.24.x_ref, bf16[2,8,128,256]{3,2,1,0:T(8,128)(2,1)S(1)} %get-tuple-element.18.grown_ref, bf16[2,8,128,256]{3,2,1,0:T(8,128)(2,1)S(1)} %get-tuple-element.19.back_ref, bf16[2,8,128,256]{3,2,1,0:T(8,128)(2,1)S(1)} %get-tuple-element.20.trans_ref), custom_call_target="tpu_custom_call" | custom-call | flops 1006632960 | bytes 4194304 | tf_op jit(solution)/shard_map/couplings/pallas_call | solution.py:433
  28.0 0.6 %collective-permute-start.4 = (f32[200,128]{1,0:T(8,128)S(1)}, f32[200,128]{1,0:T(8,128)S(1)}, u32[]{:S(2)}, u32[]{:S(2)}) collective-permute-start(f32[200,128]{1,0:T(8,128)S(1)} %couplings.3), channel_id=1, source_target_pairs={{0,8},{1,17},{2,10},{3,19},{4,12},{5,21},{6,14},{7,23},{8,0},{9,25... | collective-permute-start | bytes 307208 | tf_op jit(solution)/shard_map/ppermute | solution.py:531
  28.6 2.2 %collective-permute-done.6 = f32[328,128]{1,0:T(8,128)S(1)} collective-permute-done((f32[328,128]{1,0:T(8,128)S(1)}, f32[328,128]{1,0:T(8,128)S(1)}, u32[]{:S(2)}, u32[]{:S(2)}) %collective-permute-start.6) | collective-permute-done | bytes 167968 | tf_op jit(solution)/shard_map/ppermute | solution.py:531
  30.8 1.6 %collective-permute-start.7 = (f32[328,128]{1,0:T(8,128)S(1)}, f32[328,128]{1,0:T(8,128)S(1)}, u32[]{:S(2)}, u32[]{:S(2)}) collective-permute-start(f32[328,128]{1,0:T(8,128)S(1)} %add.7.mine_ref), channel_id=1, source_target_pairs={{0,16},{1,9},{2,18},{3,11},{4,20},{5,13},{6,22},{7,15},{8,24},{9,1... | collective-permute-start | bytes 503816 | tf_op jit(solution)/shard_map/ppermute | solution.py:531
  32.4 0.4 field_parts.1
  32.8 0.0 copy-start.1
  32.8 0.0 collective-permute-done.4
  32.9 1.5 %collective-permute-start.5 = (f32[200,128]{1,0:T(8,128)S(1)}, f32[200,128]{1,0:T(8,128)S(1)}, u32[]{:S(2)}, u32[]{:S(2)}) collective-permute-start(f32[200,128]{1,0:T(8,128)S(1)} %add.6.mine_ref), channel_id=1, source_target_pairs={{0,16},{1,9},{2,18},{3,11},{4,20},{5,13},{6,22},{7,15},{8,24},{9,1... | collective-permute-start | bytes 307208 | tf_op jit(solution)/shard_map/ppermute | solution.py:531
  34.4 1.5 %reflection.1 = f32[2,16,128]{2,1,0:T(8,128)} custom-call(s32[1]{0:T(128)} %bitcast.refs_0_.me_ref, f32[9,128,256]{2,1,0:T(8,128)S(1)} %far_trees.1.mine_ref, f32[9,128,256]{2,1,0:T(8,128)S(1)} %collective-permute-done.3.theirs_ref, f32[2,128,256]{2,1,0:T(8,128)S(1)} %get-tuple-element.21.part_ref), custom_call_target="tpu_custom_call" | custom-call | flops 1006632960 | bytes 4194304 | tf_op jit(solution)/shard_map/reflection/pallas_call | solution.py:433
  35.9 0.4 collective-permute-done.7.theirs_ref
  36.3 1.8 %project.2.rest_0_ = f32[5,1024]{1,0:T(8,128)S(1)} custom-call(s32[8]{0:T(128)S(1)} %copy-done.1, bf16[4,128,1024]{2,1,0:T(8,128)(2,1)S(1)} %get-tuple-element.22.hi_ref, bf16[4,128,1024]{2,1,0:T(8,128)(2,1)S(1)} %get-tuple-element.23.lo_ref, f32[328,128]{1,0:T(8,128)S(1)} %add.7.mine_ref, f32[328,128]{1,0:T(8,128)S(1)} %collective-permute-done.7.theirs_ref), custom_call_target="tpu_custom_call" | custom-call | flops 402653184 | bytes 4194304 | tf_op jit(solution)/shard_map/project/pallas_call | solution.py:433
  38.1 0.0 collective-permute-done.5.theirs_ref
  38.1 2.0 %project.3 = f32[8,1024]{1,0:T(8,128)} custom-call(s32[8]{0:T(128)S(1)} %copy-done.1, bf16[4,128,1024]{2,1,0:T(8,128)(2,1)S(1)} %get-tuple-element.22.hi_ref, bf16[4,128,1024]{2,1,0:T(8,128)(2,1)S(1)} %get-tuple-element.23.lo_ref, f32[200,128]{1,0:T(8,128)S(1)} %add.6.mine_ref, f32[200,128]{1,0:T(8,128)S(1)} %collective-permute-done.5.theirs_ref, ...), custom_call_target="tpu_custom_call" | custom-call | flops 402653184 | bytes 4194304 | tf_op jit(solution)/shard_map/project/pallas_call | solution.py:433
  (7 shorter events, 0.0 us)
Async XLA Ops:
  1.3 10.5 %collective-permute-start.2 = (s32[8]{0:T(128)S(1)}, s32[8]{0:T(128)S(1)}, u32[]{:S(2)}, u32[]{:S(2)}) collective-permute-start(s32[8]{0:T(128)S(1)} %shift-left_or_fusion.code_ref), channel_id=1, source_target_pairs={{2,0},{5,1},{4,2},{1,3},{6,4},{7,5},{0,6},{3,7},{10,8},{13,9},{12,... | collective-permute-start | bytes 104 | tf_op jit(solution)/shard_map/ppermute | solution.py:471
  6.4 5.4 %collective-permute-start.1 = (s32[8]{0:T(128)S(1)}, s32[8]{0:T(128)S(1)}, u32[]{:S(2)}, u32[]{:S(2)}) collective-permute-start(s32[8]{0:T(128)S(1)} %shift-left_or_fusion.code_ref), channel_id=1, source_target_pairs={{3,0},{6,1},{5,2},{7,3},{0,4},{2,5},{1,6},{4,7},{11,8},{14,9},{13,... | collective-permute-start | bytes 104 | tf_op jit(solution)/shard_map/ppermute | solution.py:471
  6.4 5.4 %collective-permute-start = (s32[8]{0:T(128)S(1)}, s32[8]{0:T(128)S(1)}, u32[]{:S(2)}, u32[]{:S(2)}) collective-permute-start(s32[8]{0:T(128)S(1)} %shift-left_or_fusion.code_ref), channel_id=1, source_target_pairs={{4,0},{7,1},{0,2},{6,3},{1,4},{3,5},{2,6},{5,7},{12,8},{15,9},{8,1... | collective-permute-start | bytes 104 | tf_op jit(solution)/shard_map/ppermute | solution.py:471
  7.1 1.9 %copy-start.2 = (f32[8,3,2,128,128]{4,3,2,1,0:T(8,128)S(1)}, f32[8,3,2,128,128]{4,3,2,1,0:T(8,128)}, u32[]{:S(2)}) copy-start(f32[8,3,2,128,128]{4,3,2,1,0:T(8,128)} %lib_ref.3) | copy-start | bytes 9437188
  9.0 2.8 %copy-start.3 = (f32[8,3,2,128,128]{4,3,2,1,0:T(8,128)S(1)}, f32[8,3,2,128,128]{4,3,2,1,0:T(8,128)}, u32[]{:S(2)}) copy-start(f32[8,3,2,128,128]{4,3,2,1,0:T(8,128)} %lib_ref.3) | copy-start | bytes 9437188
  18.9 3.3 %collective-permute-start.3 = (f32[9,128,256]{2,1,0:T(8,128)S(1)}, f32[9,128,256]{2,1,0:T(8,128)S(1)}, u32[]{:S(2)}, u32[]{:S(2)}) collective-permute-start(f32[9,128,256]{2,1,0:T(8,128)S(1)} %far_trees.1.mine_ref), channel_id=1, source_target_pairs={{0,1},{1,0},{2,3},{3,2},{4,5},{5,4},{6,7},{7,6},{8,9},{9,8},{10,11... | collective-permute-start | bytes 3538952 | tf_op jit(solution)/shard_map/ppermute | solution.py:489
  19.5 2.6 %copy-start.4 = (f32[1,2,128,128]{3,2,1,0:T(8,128)S(1)}, f32[1,2,128,128]{3,2,1,0:T(8,128)}, u32[]{:S(2)}) copy-start(f32[1,2,128,128]{3,2,1,0:T(8,128)} %param.13) | copy-start | bytes 393220
  25.4 5.4 %collective-permute-start.6 = (f32[328,128]{1,0:T(8,128)S(1)}, f32[328,128]{1,0:T(8,128)S(1)}, u32[]{:S(2)}, u32[]{:S(2)}) collective-permute-start(f32[328,128]{1,0:T(8,128)S(1)} %get-tuple-element.25), channel_id=1, source_target_pairs={{0,8},{1,17},{2,10},{3,19},{4,12},{5,21},{6,14},{7,23},{8,0},{9,25... | collective-permute-start | bytes 503816 | tf_op jit(solution)/shard_map/ppermute | solution.py:531
  26.9 5.5 %copy-start = (f32[4,128,1024]{2,1,0:T(8,128)S(1)}, f32[4,128,1024]{2,1,0:T(8,128)}, u32[]{:S(2)}) copy-start(f32[4,128,1024]{2,1,0:T(8,128)} %field_ref.1) | copy-start | bytes 6291460
  28.0 4.8 %collective-permute-start.4 = (f32[200,128]{1,0:T(8,128)S(1)}, f32[200,128]{1,0:T(8,128)S(1)}, u32[]{:S(2)}, u32[]{:S(2)}) collective-permute-start(f32[200,128]{1,0:T(8,128)S(1)} %couplings.3), channel_id=1, source_target_pairs={{0,8},{1,17},{2,10},{3,19},{4,12},{5,21},{6,14},{7,23},{8,0},{9,25... | collective-permute-start | bytes 307208 | tf_op jit(solution)/shard_map/ppermute | solution.py:531
  30.8 5.4 %collective-permute-start.7 = (f32[328,128]{1,0:T(8,128)S(1)}, f32[328,128]{1,0:T(8,128)S(1)}, u32[]{:S(2)}, u32[]{:S(2)}) collective-permute-start(f32[328,128]{1,0:T(8,128)S(1)} %add.7.mine_ref), channel_id=1, source_target_pairs={{0,16},{1,9},{2,18},{3,11},{4,20},{5,13},{6,22},{7,15},{8,24},{9,1... | collective-permute-start | bytes 503816 | tf_op jit(solution)/shard_map/ppermute | solution.py:531
  32.8 3.5 %copy-start.1 = (s32[8]{0:T(128)S(1)}, s32[8]{0:T(128)}, u32[]{:S(2)}) copy-start(s32[8]{0:T(128)} %prof_ref.3) | copy-start | bytes 100
  32.9 5.2 %collective-permute-start.5 = (f32[200,128]{1,0:T(8,128)S(1)}, f32[200,128]{1,0:T(8,128)S(1)}, u32[]{:S(2)}, u32[]{:S(2)}) collective-permute-start(f32[200,128]{1,0:T(8,128)S(1)} %add.6.mine_ref), channel_id=1, source_target_pairs={{0,16},{1,9},{2,18},{3,11},{4,20},{5,13},{6,22},{7,15},{8,24},{9,1... | collective-permute-start | bytes 307208 | tf_op jit(solution)/shard_map/ppermute | solution.py:531

commit v6 on v5

--- a/solution.py
+++ b/solution.py
@@ -12,7 +12,7 @@
 SHIFT = 8
 LOW = (1 << SHIFT) - 1
 REFL, TRANS, BACK = 0, 1, 2
-FEWER = 3
+FEWER = 4
 
 
 def split(x):
@@ -338,8 +338,9 @@
     x_ref[1, 0], x_ref[1, 1] = right(split(mul(split(s_block), x1)))
 
 
-def reflect_kernel(me_ref, mine_ref, theirs_ref, part_ref, out_ref, left_ref):
+def reflect_kernel(me_ref, mine_ref, theirs_ref, part_ref, out_ref, mark_ref, left_ref):
     rows, m = out_ref.shape[1:]
+    mark_ref[...] = jnp.zeros_like(mark_ref)
     _, first, second = sides(me_ref, mine_ref, theirs_ref)
     left_ref[0] = first(LEFT + REFL)
     left_ref[1] = first(LEFT + BACK)
@@ -384,12 +385,8 @@
         )
 
 
-def first_kernel(
-    group, me_ref, target_ref, mine_ref, theirs_ref, grown_ref, back_ref, trans_ref,
-    x_ref, part_ref, out_ref,
-):
-    chain_kernel(me_ref, target_ref, mine_ref, theirs_ref, x_ref, part_ref)
-    coupling_kernel(0, group, x_ref, grown_ref, back_ref, trans_ref, out_ref)
+def add_kernel(a_ref, b_ref, *refs):
+    refs[-1][...] = a_ref[...] + b_ref[...]
 
 
 def field_kernel(field_ref, hi_ref, lo_ref):
@@ -417,8 +414,8 @@
         ch, cl = split(c)
         q = prof_ref[start + j]
         fh, fl = hi_ref[q], lo_ref[q]
-        both = dot(jnp.concatenate([ch, cl], axis=0), fh)
-        w = both[:m] + both[m:] + dot(ch, fl)
+        w = dot(jnp.concatenate([ch, cl], axis=1), jnp.concatenate([fh, fh], axis=0))
+        w = w + dot(ch, fl)
         i = start + j
         out_ref[i : i + 1] = jnp.sum(
             (fh.astype(F32) + fl.astype(F32)) * w, axis=0, keepdims=True
@@ -427,7 +424,8 @@
 
 def call(kernel, name, kinds, outs, scratch, limit, products, *args):
     def spec(kind):
-        return pl.BlockSpec(memory_space=pltpu.SMEM if kind == "s" else pltpu.VMEM)
+        spaces = {"s": pltpu.SMEM, "v": pltpu.VMEM, "a": pl.ANY}
+        return pl.BlockSpec(memory_space=spaces[kind])
 
     several = isinstance(outs, list)
     return pl.pallas_call(
@@ -496,21 +494,20 @@
         return f32(group * (m // 2) + 8, m)
 
     more = cells - FEWER
-    x, part, packed = call(
-        functools.partial(first_kernel, more), "couplings", "svvvvvv",
-        [bf16(2, 2, 2 * m, 2 * m), f32(2, m, 2 * m), packed_shape(more)], [], 12, 35,
-        me, wanted, mine, theirs, grown, back, trans,
-    )
-    groups = [packed]
-    groups.append(
+    x, part = call(
+        chain_kernel, "chain", "svvv", [bf16(2, 2, 2 * m, 2 * m), f32(2, m, 2 * m)], [], 12, 20,
+        me, wanted, mine, theirs,
+    )
+    groups = [
         call(
-            functools.partial(coupling_kernel, more, FEWER), "couplings", "vvvv",
-            packed_shape(FEWER), [], 12, 10,
+            functools.partial(coupling_kernel, start, group), "couplings", "vvvv",
+            packed_shape(group), [], 12, 10,
             x, grown, back, trans,
         )
-    )
-    reflection = call(
-        reflect_kernel, "reflection", "svvv", f32(2, m // blocks, m),
+        for start, group in ((0, more), (more, FEWER))
+    ]
+    reflection, mark = call(
+        reflect_kernel, "reflection", "svvv", [f32(2, m // blocks, m), f32(8, m)],
         [pltpu.VMEM((2, m, 2 * m), F32)], 12, 10,
         me, mine, theirs, part,
     )
@@ -537,7 +534,12 @@
     for group, packed in zip((more, FEWER), groups):
         other = jnp.zeros_like(packed)
         for number in range(len(steps)):
-            if number:
+            if number == 1 and not start:
+                packed = call(
+                    add_kernel, "sum_of_two", "vvaa", packed_shape(group), [], 12, 0,
+                    packed, other, mark, fields[0],
+                )
+            elif number:
                 packed = packed + other
             other = exchange(packed, number)
         gradient = [

time: 40.3 us -> 40.5 us (level)
  waiting for transfers between devices: 2.54 us -> 3.29 us
  Pallas kernels: 22.5 us -> 21.9 us
    ppermute x4, waiting for transfers between devices: 2.53 us -> 3.28 us  [exchange(): return lax.ppermute(part, ('wl', 'cell'), pairs_of)]
    pallas_call x9 -> x11, Pallas kernels: 22.5 us -> 21.9 us  [call(): pl.pallas_call(kernel, out_shape=outs, in_specs=[spec(kind) for kind in k...]
  transfers between devices with their start and end apart: 8 -> 8, of which waited for: 2 -> 3; matrix products, arithmetic and copies ran while one was open for 2% -> 2% of each run, Pallas kernels for 25% -> 25%
where the time goes in v6:
time: 40.5 us; the launch traced here: 40.3 us
  Pallas kernels  21.9 us (54%)
  starting transfers between devices  11 us (27%)
  waiting for transfers between devices  3.29 us (8%)
  local copies, waits for them, and re-layouts  1.91 us (5%)
  other arithmetic  1.43 us (4%)
  between operations  0.77 us (2%)
    pallas_call x11, Pallas kernels, call(): pl.pallas_call(kernel, out_shape=outs, in_specs=[spec(kind) for kind in k...  21.9 us
    ppermute x4, starting transfers between devices, exchange(): return lax.ppermute(part, ('wl', 'cell'), pairs_of)  5.32 us
    ppermute x3, starting transfers between devices, body(): lax.ppermute(codes, 'cell', [(block, device) for device, block in enumera...  5.05 us
    ppermute x4, waiting for transfers between devices, exchange(): return lax.ppermute(part, ('wl', 'cell'), pairs_of)  3.28 us
    unnamed x10, local copies, waits for them, and re-layouts  1.91 us
  transfers between devices with their start and end apart: 8, of which 3 were waited for; matrix products, arithmetic and copies ran while one was open for 2% of the time, Pallas kernels for 25%

profile of v6, /device:TPU:0, one launch (start us, length us, event | category | flops | bytes accessed | tf_op | source)
XLA Modules:
  0.0 40.3 jit_solution(1324427010791775537)
XLA Ops:
  0.6 0.7 %shift-left_or_fusion.code_ref = s32[8]{0:T(128)S(1)} fusion(s32[8]{0:T(128)} %param.9, s32[8]{0:T(128)} %prof_ref.3), kind=kLoop, calls=%fused_computation.2 | loop fusion | flops 16 | bytes 96 | tf_op jit(solution)/shard_map/or | solution.py:467
  1.3 5.0 %collective-permute-start.2 = (s32[8]{0:T(128)S(1)}, s32[8]{0:T(128)S(1)}, u32[]{:S(2)}, u32[]{:S(2)}) collective-permute-start(s32[8]{0:T(128)S(1)} %shift-left_or_fusion.code_ref), channel_id=1, source_target_pairs={{2,0},{5,1},{4,2},{1,3},{6,4},{7,5},{0,6},{3,7},{10,8},{13,9},{12,... | collective-permute-start | bytes 104 | tf_op jit(solution)/shard_map/ppermute | solution.py:469
  6.4 0.0 collective-permute-start.1
  6.4 0.0 collective-permute-start
  6.4 0.7 %bitcast_multiply_fusion = (f32[4,128]{1,0:T(4,128)S(1)}, f32[4,128]{1,0:T(4,128)S(1)}) fusion(f32[4,128]{1,0:T(4,128)} %param.10, f32[4,1,128]{2,0,1:T(4,128)} %bitcast.9), kind=kLoop, calls=%fused_computation | loop fusion | flops 1024 | bytes 8192 | tf_op jit(solution)/shard_map/mul | solution.py:453
  7.1 0.0 copy-start.2
  7.1 1.9 %copy-done.2 = f32[8,3,2,128,128]{4,3,2,1,0:T(8,128)S(1)} copy-done((f32[8,3,2,128,128]{4,3,2,1,0:T(8,128)S(1)}, f32[8,3,2,128,128]{4,3,2,1,0:T(8,128)}, u32[]{:S(2)}) %copy-start.2) | copy-done | bytes 3145752
  9.0 2.8 %own_tree.1 = (bf16[6,3,2,128,256]{4,3,2,1,0:T(8,128)(2,1)S(1)}, f32[3,128,256]{2,1,0:T(8,128)S(1)}, f32[4,2,8,128]{3,2,1,0:T(8,128)S(1)}, f32[4,2,128,128]{3,2,1,0:T(8,128)S(1)}) custom-call(s32[8]{0:T(128)S(1)} %shift-left_or_fusion.code_ref, f32[8,3,2,128,128]{4,3,2,1,0:T(8,128)S(1)} %copy-done.2, f32[4,128]{1,0:T(4,128)S(1)} %get-tuple-element.29.real_ref, ...), custom_call_target="tpu_custom_call" | custom-call | flops 2818572288 | bytes 4194304 | tf_op jit(solution)/shard_map/own_tree/pallas_call | solution.py:431
  11.8 0.0 collective-permute-done.2.refs_3_
  11.8 0.0 collective-permute-done.1.refs_2_
  11.8 0.0 collective-permute-done.refs_1_
  11.8 7.1 %far_trees.1.mine_ref = f32[9,128,256]{2,1,0:T(8,128)S(1)} custom-call(s32[1]{0:T(128)} %bitcast.refs_0_.me_ref, s32[8]{0:T(128)S(1)} %collective-permute-done.refs_1_, s32[8]{0:T(128)S(1)} %collective-permute-done.1.refs_2_, s32[8]{0:T(128)S(1)} %collective-permute-done.2.refs_3_, f32[8,3,2,128,128]{4,3,2,1,0:T(8,128)S(1)} %copy-done.3, ...), custom_call_target="tpu_custom_call" | custom-call | flops 9663676416 | bytes 4194304 | tf_op jit(solution)/shard_map/far_trees/pallas_call | solution.py:431
  18.9 0.6 %collective-permute-start.3 = (f32[9,128,256]{2,1,0:T(8,128)S(1)}, f32[9,128,256]{2,1,0:T(8,128)S(1)}, u32[]{:S(2)}, u32[]{:S(2)}) collective-permute-start(f32[9,128,256]{2,1,0:T(8,128)S(1)} %far_trees.1.mine_ref), channel_id=1, source_target_pairs={{0,1},{1,0},{2,3},{3,2},{4,5},{5,4},{6,7},{7,6},{8,9},{9,8},{10,11... | collective-permute-start | bytes 3538952 | tf_op jit(solution)/shard_map/ppermute | solution.py:487
  19.5 2.6 %own_scan.1 = (bf16[2,8,128,256]{3,2,1,0:T(8,128)(2,1)S(1)}, bf16[2,8,128,256]{3,2,1,0:T(8,128)(2,1)S(1)}, bf16[2,8,128,256]{3,2,1,0:T(8,128)(2,1)S(1)}) custom-call(s32[8]{0:T(128)S(1)} %shift-left_or_fusion.code_ref, f32[8,3,2,128,128]{4,3,2,1,0:T(8,128)S(1)} %copy-done.3, f32[4,2,8,128]{3,2,1,0:T(8,128)S(1)} %get-tuple-element.15.refs_5_.row_ref, ...), custom_call_target="tpu_custom_call" | custom-call | flops 2717908992 | bytes 4194304 | tf_op jit(solution)/shard_map/own_scan/pallas_call | solution.py:431
  22.2 0.0 collective-permute-done.3.theirs_ref
  22.2 1.5 %chain.1 = (bf16[2,2,256,256]{3,2,1,0:T(8,128)(2,1)S(1)}, f32[2,128,256]{2,1,0:T(8,128)S(1)}) custom-call(s32[1]{0:T(128)} %bitcast.refs_0_.me_ref, f32[2,128,128]{2,1,0:T(8,128)S(1)} %bitcast.8, f32[9,128,256]{2,1,0:T(8,128)S(1)} %far_trees.1.mine_ref, f32[9,128,256]{2,1,0:T(8,128)S(1)} %collective-permute-done.3.theirs_ref), custom_call_target="tpu_custom_call" | custom-call | flops 2013265920 | bytes 4194304 | tf_op jit(solution)/shard_map/chain/pallas_call | solution.py:431
  23.7 1.3 %couplings.3.a_ref = f32[264,128]{1,0:T(8,128)S(1)} custom-call(bf16[2,2,256,256]{3,2,1,0:T(8,128)(2,1)S(1)} %get-tuple-element.22.x_ref, bf16[2,8,128,256]{3,2,1,0:T(8,128)(2,1)S(1)} %get-tuple-element.24.grown_ref, bf16[2,8,128,256]{3,2,1,0:T(8,128)(2,1)S(1)} %get-tuple-element.25.back_ref, bf16[2,8,128,256]{3,2,1,0:T(8,128)(2,1)S(1)} %get-tuple-element.26.trans_ref), custom_call_target="tpu_custom_call" | custom-call | flops 1006632960 | bytes 4194304 | tf_op jit(solution)/shard_map/couplings/pallas_call | solution.py:431
  25.1 0.0 copy-start
  25.1 1.6 %collective-permute-start.6 = (f32[264,128]{1,0:T(8,128)S(1)}, f32[264,128]{1,0:T(8,128)S(1)}, u32[]{:S(2)}, u32[]{:S(2)}) collective-permute-start(f32[264,128]{1,0:T(8,128)S(1)} %couplings.3.a_ref), channel_id=1, source_target_pairs={{0,8},{1,17},{2,10},{3,19},{4,12},{5,21},{6,14},{7,23},{8,0},{9,25... | collective-permute-start | bytes 405512 | tf_op jit(solution)/shard_map/ppermute | solution.py:528
  26.7 1.3 %couplings.2 = f32[264,128]{1,0:T(8,128)S(1)} custom-call(bf16[2,2,256,256]{3,2,1,0:T(8,128)(2,1)S(1)} %get-tuple-element.22.x_ref, bf16[2,8,128,256]{3,2,1,0:T(8,128)(2,1)S(1)} %get-tuple-element.24.grown_ref, bf16[2,8,128,256]{3,2,1,0:T(8,128)(2,1)S(1)} %get-tuple-element.25.back_ref, bf16[2,8,128,256]{3,2,1,0:T(8,128)(2,1)S(1)} %get-tuple-element.26.trans_ref), custom_call_target="tpu_custom_call" | custom-call | flops 1006632960 | bytes 4194304 | tf_op jit(solution)/shard_map/couplings/pallas_call | solution.py:431
  28.0 0.6 %collective-permute-start.4 = (f32[264,128]{1,0:T(8,128)S(1)}, f32[264,128]{1,0:T(8,128)S(1)}, u32[]{:S(2)}, u32[]{:S(2)}) collective-permute-start(f32[264,128]{1,0:T(8,128)S(1)} %couplings.2), channel_id=1, source_target_pairs={{0,8},{1,17},{2,10},{3,19},{4,12},{5,21},{6,14},{7,23},{8,0},{9,25... | collective-permute-start | bytes 405512 | tf_op jit(solution)/shard_map/ppermute | solution.py:528
  28.6 0.4 field_parts.1
  29.0 0.0 copy-start.1
  29.0 1.6 %reflection.1 = (f32[2,16,128]{2,1,0:T(8,128)}, f32[8,128]{1,0:T(8,128)S(1)}) custom-call(s32[1]{0:T(128)} %bitcast.refs_0_.me_ref, f32[9,128,256]{2,1,0:T(8,128)S(1)} %far_trees.1.mine_ref, f32[9,128,256]{2,1,0:T(8,128)S(1)} %collective-permute-done.3.theirs_ref, f32[2,128,256]{2,1,0:T(8,128)S(1)} %get-tuple-element.18.part_ref), custom_call_target="tpu_custom_call" | custom-call | flops 1006632960 | bytes 4194304 | tf_op jit(solution)/shard_map/reflection/pallas_call | solution.py:431
  30.5 0.0 collective-permute-done.6.b_ref
  30.6 1.6 %collective-permute-start.7 = (f32[264,128]{1,0:T(8,128)S(1)}, f32[264,128]{1,0:T(8,128)S(1)}, u32[]{:S(2)}, u32[]{:S(2)}) collective-permute-start(f32[264,128]{1,0:T(8,128)S(1)} %sum_of_two.1.mine_ref), channel_id=1, source_target_pairs={{0,16},{1,9},{2,18},{3,11},{4,20},{5,13},{6,22},{7,15},{8,24},{9,1... | collective-permute-start | bytes 405512 | tf_op jit(solution)/shard_map/ppermute | solution.py:528
  32.2 1.1 %collective-permute-done.4 = f32[264,128]{1,0:T(8,128)S(1)} collective-permute-done((f32[264,128]{1,0:T(8,128)S(1)}, f32[264,128]{1,0:T(8,128)S(1)}, u32[]{:S(2)}, u32[]{:S(2)}) %collective-permute-start.4) | collective-permute-done | bytes 135200 | tf_op jit(solution)/shard_map/ppermute | solution.py:528
  33.3 1.6 %collective-permute-start.5 = (f32[264,128]{1,0:T(8,128)S(1)}, f32[264,128]{1,0:T(8,128)S(1)}, u32[]{:S(2)}, u32[]{:S(2)}) collective-permute-start(f32[264,128]{1,0:T(8,128)S(1)} %add.3.mine_ref), channel_id=1, source_target_pairs={{0,16},{1,9},{2,18},{3,11},{4,20},{5,13},{6,22},{7,15},{8,24},{9,1... | collective-permute-start | bytes 405512 | tf_op jit(solution)/shard_map/ppermute | solution.py:528
  34.9 0.8 %collective-permute-done.7.theirs_ref = f32[264,128]{1,0:T(8,128)S(1)} collective-permute-done((f32[264,128]{1,0:T(8,128)S(1)}, f32[264,128]{1,0:T(8,128)S(1)}, u32[]{:S(2)}, u32[]{:S(2)}) %collective-permute-start.7) | collective-permute-done | bytes 135200 | tf_op jit(solution)/shard_map/ppermute | solution.py:528
  35.6 1.3 %project.2.rest_0_ = f32[4,1024]{1,0:T(4,128)S(1)} custom-call(s32[8]{0:T(128)S(1)} %copy-done.1, bf16[4,128,1024]{2,1,0:T(8,128)(2,1)S(1)} %get-tuple-element.20.refs_1_.hi_ref, bf16[4,128,1024]{2,1,0:T(8,128)(2,1)S(1)} %get-tuple-element.21.lo_ref, f32[264,128]{1,0:T(8,128)S(1)} %sum_of_two.1.mine_ref, f32[264,128]{1,0:T(8,128)S(1)} %collective-permute-done.7.theirs_ref), custom_call_target="tpu_custom_call" | custom-call | flops 402653184 | bytes 4194304 | tf_op jit(solution)/shard_map/project/pallas_call | solution.py:431
  37.0 1.4 %collective-permute-done.5.theirs_ref = f32[264,128]{1,0:T(8,128)S(1)} collective-permute-done((f32[264,128]{1,0:T(8,128)S(1)}, f32[264,128]{1,0:T(8,128)S(1)}, u32[]{:S(2)}, u32[]{:S(2)}) %collective-permute-start.5) | collective-permute-done | bytes 135200 | tf_op jit(solution)/shard_map/ppermute | solution.py:528
  38.4 2.0 %project.3 = f32[8,1024]{1,0:T(8,128)} custom-call(s32[8]{0:T(128)S(1)} %copy-done.1, bf16[4,128,1024]{2,1,0:T(8,128)(2,1)S(1)} %get-tuple-element.20.refs_1_.hi_ref, bf16[4,128,1024]{2,1,0:T(8,128)(2,1)S(1)} %get-tuple-element.21.lo_ref, f32[264,128]{1,0:T(8,128)S(1)} %add.3.mine_ref, f32[264,128]{1,0:T(8,128)S(1)} %collective-permute-done.5.theirs_ref, ...), custom_call_target="tpu_custom_call" | custom-call | flops 402653184 | bytes 4194304 | tf_op jit(solution)/shard_map/project/pallas_call | solution.py:431
  (8 shorter events, 0.0 us)
Async XLA Ops:
  1.3 10.5 %collective-permute-start.2 = (s32[8]{0:T(128)S(1)}, s32[8]{0:T(128)S(1)}, u32[]{:S(2)}, u32[]{:S(2)}) collective-permute-start(s32[8]{0:T(128)S(1)} %shift-left_or_fusion.code_ref), channel_id=1, source_target_pairs={{2,0},{5,1},{4,2},{1,3},{6,4},{7,5},{0,6},{3,7},{10,8},{13,9},{12,... | collective-permute-start | bytes 104 | tf_op jit(solution)/shard_map/ppermute | solution.py:469
  6.4 5.4 %collective-permute-start.1 = (s32[8]{0:T(128)S(1)}, s32[8]{0:T(128)S(1)}, u32[]{:S(2)}, u32[]{:S(2)}) collective-permute-start(s32[8]{0:T(128)S(1)} %shift-left_or_fusion.code_ref), channel_id=1, source_target_pairs={{3,0},{6,1},{5,2},{7,3},{0,4},{2,5},{1,6},{4,7},{11,8},{14,9},{13,... | collective-permute-start | bytes 104 | tf_op jit(solution)/shard_map/ppermute | solution.py:469
  6.4 5.4 %collective-permute-start = (s32[8]{0:T(128)S(1)}, s32[8]{0:T(128)S(1)}, u32[]{:S(2)}, u32[]{:S(2)}) collective-permute-start(s32[8]{0:T(128)S(1)} %shift-left_or_fusion.code_ref), channel_id=1, source_target_pairs={{4,0},{7,1},{0,2},{6,3},{1,4},{3,5},{2,6},{5,7},{12,8},{15,9},{8,1... | collective-permute-start | bytes 104 | tf_op jit(solution)/shard_map/ppermute | solution.py:469
  7.1 1.9 %copy-start.2 = (f32[8,3,2,128,128]{4,3,2,1,0:T(8,128)S(1)}, f32[8,3,2,128,128]{4,3,2,1,0:T(8,128)}, u32[]{:S(2)}) copy-start(f32[8,3,2,128,128]{4,3,2,1,0:T(8,128)} %lib_ref.3) | copy-start | bytes 9437188
  9.0 2.8 %copy-start.3 = (f32[8,3,2,128,128]{4,3,2,1,0:T(8,128)S(1)}, f32[8,3,2,128,128]{4,3,2,1,0:T(8,128)}, u32[]{:S(2)}) copy-start(f32[8,3,2,128,128]{4,3,2,1,0:T(8,128)} %lib_ref.3) | copy-start | bytes 9437188
  18.9 3.3 %collective-permute-start.3 = (f32[9,128,256]{2,1,0:T(8,128)S(1)}, f32[9,128,256]{2,1,0:T(8,128)S(1)}, u32[]{:S(2)}, u32[]{:S(2)}) collective-permute-start(f32[9,128,256]{2,1,0:T(8,128)S(1)} %far_trees.1.mine_ref), channel_id=1, source_target_pairs={{0,1},{1,0},{2,3},{3,2},{4,5},{5,4},{6,7},{7,6},{8,9},{9,8},{10,11... | collective-permute-start | bytes 3538952 | tf_op jit(solution)/shard_map/ppermute | solution.py:487
  19.5 2.6 %copy-start.4 = (f32[1,2,128,128]{3,2,1,0:T(8,128)S(1)}, f32[1,2,128,128]{3,2,1,0:T(8,128)}, u32[]{:S(2)}) copy-start(f32[1,2,128,128]{3,2,1,0:T(8,128)} %param.13) | copy-start | bytes 393220
  25.1 3.5 %copy-start = (f32[4,128,1024]{2,1,0:T(8,128)S(1)}, f32[4,128,1024]{2,1,0:T(8,128)}, u32[]{:S(2)}) copy-start(f32[4,128,1024]{2,1,0:T(8,128)} %field_ref.1) | copy-start | bytes 6291460
  25.1 5.5 %collective-permute-start.6 = (f32[264,128]{1,0:T(8,128)S(1)}, f32[264,128]{1,0:T(8,128)S(1)}, u32[]{:S(2)}, u32[]{:S(2)}) collective-permute-start(f32[264,128]{1,0:T(8,128)S(1)} %couplings.3.a_ref), channel_id=1, source_target_pairs={{0,8},{1,17},{2,10},{3,19},{4,12},{5,21},{6,14},{7,23},{8,0},{9,25... | collective-permute-start | bytes 405512 | tf_op jit(solution)/shard_map/ppermute | solution.py:528
  28.0 5.3 %collective-permute-start.4 = (f32[264,128]{1,0:T(8,128)S(1)}, f32[264,128]{1,0:T(8,128)S(1)}, u32[]{:S(2)}, u32[]{:S(2)}) collective-permute-start(f32[264,128]{1,0:T(8,128)S(1)} %couplings.2), channel_id=1, source_target_pairs={{0,8},{1,17},{2,10},{3,19},{4,12},{5,21},{6,14},{7,23},{8,0},{9,25... | collective-permute-start | bytes 405512 | tf_op jit(solution)/shard_map/ppermute | solution.py:528
  29.0 6.7 %copy-start.1 = (s32[8]{0:T(128)S(1)}, s32[8]{0:T(128)}, u32[]{:S(2)}) copy-start(s32[8]{0:T(128)} %prof_ref.3) | copy-start | bytes 100
  30.6 5.1 %collective-permute-start.7 = (f32[264,128]{1,0:T(8,128)S(1)}, f32[264,128]{1,0:T(8,128)S(1)}, u32[]{:S(2)}, u32[]{:S(2)}) collective-permute-start(f32[264,128]{1,0:T(8,128)S(1)} %sum_of_two.1.mine_ref), channel_id=1, source_target_pairs={{0,16},{1,9},{2,18},{3,11},{4,20},{5,13},{6,22},{7,15},{8,24},{9,1... | collective-permute-start | bytes 405512 | tf_op jit(solution)/shard_map/ppermute | solution.py:528
  33.3 5.1 %collective-permute-start.5 = (f32[264,128]{1,0:T(8,128)S(1)}, f32[264,128]{1,0:T(8,128)S(1)}, u32[]{:S(2)}, u32[]{:S(2)}) collective-permute-start(f32[264,128]{1,0:T(8,128)S(1)} %add.3.mine_ref), channel_id=1, source_target_pairs={{0,16},{1,9},{2,18},{3,11},{4,20},{5,13},{6,22},{7,15},{8,24},{9,1... | collective-permute-start | bytes 405512 | tf_op jit(solution)/shard_map/ppermute | solution.py:528

commit v7 on v6

--- a/solution.py
+++ b/solution.py
@@ -12,7 +12,7 @@
 SHIFT = 8
 LOW = (1 << SHIFT) - 1
 REFL, TRANS, BACK = 0, 1, 2
-FEWER = 4
+FEWER = 3
 
 
 def split(x):
@@ -84,8 +84,36 @@
         keep(ref, values[kind], *at, kind)
 
 
-def spread(factor_refs, row_ref, col_ref):
-    for part, ref in enumerate(factor_refs):
+def trans_leaf(lib_ref, col_ref, code):
+    q, s = code >> SHIFT, code & LOW
+    re, im = lib_ref[s, TRANS, 0], lib_ref[s, TRANS, 1]
+    cr, ci = col_ref[q, 0], col_ref[q, 1]
+    return split(jnp.concatenate([cr * re - ci * im, cr * im + ci * re], axis=1))
+
+
+def back_leaf(lib_ref, row_ref, code):
+    q, s = code >> SHIFT, code & LOW
+    re, im = lib_ref[s, BACK, 0], lib_ref[s, BACK, 1]
+    rr, ri = row_ref[q, 0][:1], row_ref[q, 1][:1]
+    return split(jnp.concatenate([re * rr - im * ri, re * ri + im * rr], axis=1))
+
+
+def refl_leaf(lib_ref, code):
+    s = code & LOW
+    return split(jnp.concatenate([lib_ref[s, REFL, 0], lib_ref[s, REFL, 1]], axis=1))
+
+
+def leaf(lib_ref, row_ref, col_ref, code):
+    return (
+        refl_leaf(lib_ref, code),
+        trans_leaf(lib_ref, col_ref, code),
+        back_leaf(lib_ref, row_ref, code),
+    )
+
+
+def table_kernel(code_ref, real_ref, imag_ref, sent_ref, row_ref, col_ref):
+    sent_ref[...] = code_ref[...]
+    for part, ref in enumerate((real_ref, imag_ref)):
         profiles, m = ref.shape
         for q in range(profiles):
             wide = jnp.broadcast_to(ref[q : q + 1], (m, m))
@@ -93,39 +121,11 @@
             col_ref[q, part] = wide.T
 
 
-def trans_leaf(lib_ref, col_ref, code):
-    q, s = code >> SHIFT, code & LOW
-    re, im = lib_ref[s, TRANS, 0], lib_ref[s, TRANS, 1]
-    cr, ci = col_ref[q, 0], col_ref[q, 1]
-    return split(jnp.concatenate([cr * re - ci * im, cr * im + ci * re], axis=1))
-
-
-def back_leaf(lib_ref, row_ref, code):
-    q, s = code >> SHIFT, code & LOW
-    re, im = lib_ref[s, BACK, 0], lib_ref[s, BACK, 1]
-    rr, ri = row_ref[q, 0][:1], row_ref[q, 1][:1]
-    return split(jnp.concatenate([re * rr - im * ri, re * ri + im * rr], axis=1))
-
-
-def refl_leaf(lib_ref, code):
-    s = code & LOW
-    return split(jnp.concatenate([lib_ref[s, REFL, 0], lib_ref[s, REFL, 1]], axis=1))
-
-
-def leaf(lib_ref, row_ref, col_ref, code):
-    return (
-        refl_leaf(lib_ref, code),
-        trans_leaf(lib_ref, col_ref, code),
-        back_leaf(lib_ref, row_ref, code),
-    )
-
-
-def own_kernel(code_ref, lib_ref, real_ref, imag_ref, nodes_ref, own_ref, row_ref, col_ref):
-    cells = code_ref.shape[0]
-    spread((real_ref, imag_ref), row_ref, col_ref)
+def own_kernel(code_ref, lib_ref, row_ref, col_ref, nodes_ref, own_ref):
+    cells = code_ref.shape[1]
 
     def cell(i):
-        return leaf(lib_ref, row_ref, col_ref, code_ref[i])
+        return leaf(lib_ref, row_ref, col_ref, code_ref[0, i])
 
     pairs = []
     for j in range(cells // 2):
@@ -147,7 +147,7 @@
     m = own_ref.shape[1]
 
     def cell(i):
-        return leaf(lib_ref, row_ref, col_ref, code_ref[i])
+        return leaf(lib_ref, row_ref, col_ref, code_ref[0, i])
 
     def store(ref, i, pair):
         ref[0, i], ref[1, i] = pair
@@ -161,7 +161,7 @@
         store(grown_ref, i, split(whole(before) + mul(refl, right(before))))
 
     def trans_of(i):
-        return trans_leaf(lib_ref, col_ref, code_ref[i])
+        return trans_leaf(lib_ref, col_ref, code_ref[0, i])
 
     suffix4 = put(4, triple(nodes_ref, 5))
     before2 = get(nodes_ref, 0, TRANS)
@@ -231,7 +231,7 @@
         for device in range(1, blocks):
             k = jnp.where(me_ref[0] == device, source[device], k)
         for i in range(cells):
-            code_ref[k, i] = ref[i]
+            code_ref[k, i] = ref[0, i]
     chip = me_ref[0] >> 1
     core = me_ref[0] & 1
     right_count = chips - 1 - chip
@@ -464,14 +464,18 @@
         return jax.ShapeDtypeStruct(shape, BF16)
 
     tables = [f32(profiles, 2, 8, m), f32(profiles, 2, m, m)]
-    codes = (cell_profile << SHIFT) | cell_section
+    codes = ((cell_profile << SHIFT) | cell_section).reshape(1, cells)
+    codes, row_table, col_table = call(
+        table_kernel, "tables", "vvv", [jax.ShapeDtypeStruct((1, cells), jnp.int32), *tables], [],
+        12, 60, codes, *factors,
+    )
     got = [
         lax.ppermute(codes, "cell", [(block, device) for device, block in enumerate(source)])
         for source in routes(chips)
     ]
-    nodes, own, row_table, col_table = call(
-        own_kernel, "own_tree", "svvv", [bf16(*pairs(6, 3)), f32(3, m, 2 * m), *tables], [], 12, 28,
-        codes, interfaces, *factors,
+    nodes, own = call(
+        own_kernel, "own_tree", "svvv", [bf16(*pairs(6, 3)), f32(3, m, 2 * m)], [], 12, 28,
+        codes, interfaces, row_table, col_table,
     )
     mine = call(
         far_kernel, "far_trees", "s" * chips + "vvvv", f32(9, m, 2 * m),

time: 40.5 us -> 46.8 us (1.16)
  waiting for transfers between devices: 3.29 us -> 8.03 us
  starting transfers between devices: 11 us -> 12.9 us
    ppermute x4, waiting for transfers between devices: 3.28 us -> 7.8 us  [exchange(): return lax.ppermute(part, ('wl', 'cell'), pairs_of)]
    ppermute x3, starting transfers between devices: 5.05 us -> 7.58 us  [body(): lax.ppermute(codes, 'cell', [(block, device) for device, block in enumera...]
    reshape x0 -> x1, other arithmetic: none -> 0.68 us  [body(): codes = (cell_profile << SHIFT | cell_section).reshape(1, cells)]
    or x1 -> x0, other arithmetic: 0.68 us -> none  [body(): codes = cell_profile << SHIFT | cell_section]
    ppermute x1, starting transfers between devices: 0.62 us -> 0.07 us  [body(): theirs = lax.ppermute(mine, 'cell', [(i, i ^ 1) for i in range(blocks)])]
    pallas_call x11 -> x12, Pallas kernels: 21.9 us -> 21.5 us  [call(): pl.pallas_call(kernel, out_shape=outs, in_specs=[spec(kind) for kind in k...]
    unnamed x10 -> x14, local copies, waits for them, and re-layouts: 1.91 us -> 1.87 us
  transfers between devices with their start and end apart: 8 -> 8, of which waited for: 3 -> 4; matrix products, arithmetic and copies ran while one was open for 2% -> 0% of each run, Pallas kernels for 25% -> 21%
where the time goes in v7:
time: 46.8 us; the launch traced here: 46.6 us
  Pallas kernels  21.5 us (46%)
  starting transfers between devices  12.9 us (28%)
  waiting for transfers between devices  8.03 us (17%)
  local copies, waits for them, and re-layouts  1.87 us (4%)
  other arithmetic  1.43 us (3%)
  between operations  0.78 us (2%)
    pallas_call x12, Pallas kernels, call(): pl.pallas_call(kernel, out_shape=outs, in_specs=[spec(kind) for kind in k...  21.5 us
    ppermute x4, waiting for transfers between devices, exchange(): return lax.ppermute(part, ('wl', 'cell'), pairs_of)  7.8 us
    ppermute x3, starting transfers between devices, body(): lax.ppermute(codes, 'cell', [(block, device) for device, block in enumera...  7.58 us
    ppermute x4, starting transfers between devices, exchange(): return lax.ppermute(part, ('wl', 'cell'), pairs_of)  5.27 us
    unnamed x14, local copies, waits for them, and re-layouts  1.87 us
  transfers between devices with their start and end apart: 8, of which 4 were waited for; matrix products, arithmetic and copies ran while one was open for 0% of the time, Pallas kernels for 21%

profile of v7, /device:TPU:0, one launch (start us, length us, event | category | flops | bytes accessed | tf_op | source)
XLA Modules:
  0.0 46.6 jit_solution(330920752231547811)
XLA Ops:
  0.6 0.7 %bitcast_multiply_fusion = (f32[4,128]{1,0:T(4,128)S(1)}, f32[4,128]{1,0:T(4,128)S(1)}) fusion(f32[4,128]{1,0:T(4,128)} %param.10, f32[4,1,128]{2,0,1:T(4,128)} %bitcast.11), kind=kLoop, calls=%fused_computation | loop fusion | flops 1024 | bytes 8192 | tf_op jit(solution)/shard_map/mul | solution.py:453
  1.4 0.7 %or_bitcast_fusion.code_ref = s32[1,8]{1,0:T(1,128)S(1)} fusion(s32[8]{0:T(128)} %param.9, s32[8]{0:T(128)} %prof_ref.3), kind=kLoop, calls=%fused_computation.2 | loop fusion | flops 16 | bytes 96 | tf_op jit(solution)/shard_map/reshape | solution.py:467
  2.1 0.2 tables.1
  2.3 0.8 %copy-done.4 = f32[4,2,128,128]{3,2,1,0:T(8,128)} copy-done((f32[4,2,128,128]{3,2,1,0:T(8,128)}, f32[4,2,128,128]{3,2,1,0:T(8,128)S(1)}, u32[]{:S(2)}) %copy-start.4) | copy-done | bytes 524312
  3.1 3.0 %collective-permute-start = (s32[1,8]{1,0:T(1,128)S(1)}, s32[1,8]{1,0:T(1,128)S(1)}, u32[]{:S(2)}, u32[]{:S(2)}) collective-permute-start(s32[1,8]{1,0:T(1,128)S(1)} %get-tuple-element.16.code_ref), channel_id=1, source_target_pairs={{4,0},{7,1},{0,2},{6,3},{1,4},{3,5},{2,6},{5,7},{12,8},{15,9},{8,1... | collective-permute-start | bytes 104 | tf_op jit(solution)/shard_map/ppermute | solution.py:473
  6.1 1.0 %collective-permute-start.1 = (s32[1,8]{1,0:T(1,128)S(1)}, s32[1,8]{1,0:T(1,128)S(1)}, u32[]{:S(2)}, u32[]{:S(2)}) collective-permute-start(s32[1,8]{1,0:T(1,128)S(1)} %get-tuple-element.16.code_ref), channel_id=1, source_target_pairs={{3,0},{6,1},{5,2},{7,3},{0,4},{2,5},{1,6},{4,7},{11,8},{14,9},{13,... | collective-permute-start | bytes 104 | tf_op jit(solution)/shard_map/ppermute | solution.py:473
  7.1 3.5 %collective-permute-start.2 = (s32[1,8]{1,0:T(1,128)S(1)}, s32[1,8]{1,0:T(1,128)S(1)}, u32[]{:S(2)}, u32[]{:S(2)}) collective-permute-start(s32[1,8]{1,0:T(1,128)S(1)} %get-tuple-element.16.code_ref), channel_id=1, source_target_pairs={{2,0},{5,1},{4,2},{1,3},{6,4},{7,5},{0,6},{3,7},{10,8},{13,9},{12,... | collective-permute-start | bytes 104 | tf_op jit(solution)/shard_map/ppermute | solution.py:473
  10.6 1.0 %copy-done.5 = f32[4,2,128,128]{3,2,1,0:T(8,128)S(1)} copy-done((f32[4,2,128,128]{3,2,1,0:T(8,128)S(1)}, f32[4,2,128,128]{3,2,1,0:T(8,128)}, u32[]{:S(2)}) %copy-start.5) | copy-done | bytes 524312
  11.7 2.6 %own_tree.1 = (bf16[6,3,2,128,256]{4,3,2,1,0:T(8,128)(2,1)S(1)}, f32[3,128,256]{2,1,0:T(8,128)S(1)}) custom-call(s32[1,8]{1,0:T(1,128)S(1)} %get-tuple-element.16.code_ref, f32[8,3,2,128,128]{4,3,2,1,0:T(8,128)S(1)} %copy-done.2, f32[4,2,8,128]{3,2,1,0:T(8,128)S(1)} %get-tuple-element.17.row_ref.refs_5_, f32[4,2,128,128]{3,2,1,0:T(8,128)S(1)} %copy-done.5), custom_call_target="tpu_custom_call" | custom-call | flops 2818572288 | bytes 4194304 | tf_op jit(solution)/shard_map/own_tree/pallas_call | solution.py:431
  14.3 0.0 collective-permute-done.refs_1_
  14.3 0.0 collective-permute-done.1.refs_2_
  14.4 6.8 %far_trees.1.mine_ref = f32[9,128,256]{2,1,0:T(8,128)S(1)} custom-call(s32[1]{0:T(128)} %bitcast.refs_0_.me_ref, s32[1,8]{1,0:T(1,128)S(1)} %collective-permute-done.refs_1_, s32[1,8]{1,0:T(1,128)S(1)} %collective-permute-done.1.refs_2_, s32[1,8]{1,0:T(1,128)S(1)} %collective-permute-done.2.refs_3_, f32[8,3,2,128,128]{4,3,2,1,0:T(8,128)S(1)} %copy-done.2, ...), custom_call_target="tpu_custom_call" | custom-call | flops 9663676416 | bytes 4194304 | tf_op jit(solution)/shard_map/far_trees/pallas_call | solution.py:431
  21.2 0.1 collective-permute-start.3
  21.3 0.0 copy-start.3
  21.3 2.6 %own_scan.1 = (bf16[2,8,128,256]{3,2,1,0:T(8,128)(2,1)S(1)}, bf16[2,8,128,256]{3,2,1,0:T(8,128)(2,1)S(1)}, bf16[2,8,128,256]{3,2,1,0:T(8,128)(2,1)S(1)}) custom-call(s32[1,8]{1,0:T(1,128)S(1)} %get-tuple-element.16.code_ref, f32[8,3,2,128,128]{4,3,2,1,0:T(8,128)S(1)} %copy-done.2, f32[4,2,8,128]{3,2,1,0:T(8,128)S(1)} %get-tuple-element.17.row_ref.refs_5_, ...), custom_call_target="tpu_custom_call" | custom-call | flops 2717908992 | bytes 4194304 | tf_op jit(solution)/shard_map/own_scan/pallas_call | solution.py:431
  23.9 0.2 collective-permute-done.3.theirs_ref
  24.1 1.5 %chain.1 = (bf16[2,2,256,256]{3,2,1,0:T(8,128)(2,1)S(1)}, f32[2,128,256]{2,1,0:T(8,128)S(1)}) custom-call(s32[1]{0:T(128)} %bitcast.refs_0_.me_ref, f32[2,128,128]{2,1,0:T(8,128)S(1)} %bitcast.10, f32[9,128,256]{2,1,0:T(8,128)S(1)} %far_trees.1.mine_ref, f32[9,128,256]{2,1,0:T(8,128)S(1)} %collective-permute-done.3.theirs_ref), custom_call_target="tpu_custom_call" | custom-call | flops 2013265920 | bytes 4194304 | tf_op jit(solution)/shard_map/chain/pallas_call | solution.py:431
  25.6 0.0 copy-start
  25.6 1.5 %couplings.3.a_ref = f32[328,128]{1,0:T(8,128)S(1)} custom-call(bf16[2,2,256,256]{3,2,1,0:T(8,128)(2,1)S(1)} %get-tuple-element.24.x_ref, bf16[2,8,128,256]{3,2,1,0:T(8,128)(2,1)S(1)} %get-tuple-element.26.grown_ref, bf16[2,8,128,256]{3,2,1,0:T(8,128)(2,1)S(1)} %get-tuple-element.27.back_ref, bf16[2,8,128,256]{3,2,1,0:T(8,128)(2,1)S(1)} %get-tuple-element.28.trans_ref), custom_call_target="tpu_custom_call" | custom-call | flops 1006632960 | bytes 4194304 | tf_op jit(solution)/shard_map/couplings/pallas_call | solution.py:431
  27.1 1.6 %collective-permute-start.6 = (f32[328,128]{1,0:T(8,128)S(1)}, f32[328,128]{1,0:T(8,128)S(1)}, u32[]{:S(2)}, u32[]{:S(2)}) collective-permute-start(f32[328,128]{1,0:T(8,128)S(1)} %couplings.3.a_ref), channel_id=1, source_target_pairs={{0,8},{1,17},{2,10},{3,19},{4,12},{5,21},{6,14},{7,23},{8,0},{9,25... | collective-permute-start | bytes 503816 | tf_op jit(solution)/shard_map/ppermute | solution.py:532
  28.7 0.4 field_parts.1
  29.1 1.5 %reflection.1 = (f32[2,16,128]{2,1,0:T(8,128)}, f32[8,128]{1,0:T(8,128)S(1)}) custom-call(s32[1]{0:T(128)} %bitcast.refs_0_.me_ref, f32[9,128,256]{2,1,0:T(8,128)S(1)} %far_trees.1.mine_ref, f32[9,128,256]{2,1,0:T(8,128)S(1)} %collective-permute-done.3.theirs_ref, f32[2,128,256]{2,1,0:T(8,128)S(1)} %get-tuple-element.20.part_ref), custom_call_target="tpu_custom_call" | custom-call | flops 1006632960 | bytes 4194304 | tf_op jit(solution)/shard_map/reflection/pallas_call | solution.py:431
  30.6 1.9 %collective-permute-done.6.b_ref = f32[328,128]{1,0:T(8,128)S(1)} collective-permute-done((f32[328,128]{1,0:T(8,128)S(1)}, f32[328,128]{1,0:T(8,128)S(1)}, u32[]{:S(2)}, u32[]{:S(2)}) %collective-permute-start.6) | collective-permute-done | bytes 167968 | tf_op jit(solution)/shard_map/ppermute | solution.py:532
  32.6 0.0 copy-start.1
  32.6 1.6 %collective-permute-start.7 = (f32[328,128]{1,0:T(8,128)S(1)}, f32[328,128]{1,0:T(8,128)S(1)}, u32[]{:S(2)}, u32[]{:S(2)}) collective-permute-start(f32[328,128]{1,0:T(8,128)S(1)} %sum_of_two.1.mine_ref), channel_id=1, source_target_pairs={{0,16},{1,9},{2,18},{3,11},{4,20},{5,13},{6,22},{7,15},{8,24},{9,1... | collective-permute-start | bytes 503816 | tf_op jit(solution)/shard_map/ppermute | solution.py:532
  34.2 1.1 %couplings.2 = f32[200,128]{1,0:T(8,128)S(1)} custom-call(bf16[2,2,256,256]{3,2,1,0:T(8,128)(2,1)S(1)} %get-tuple-element.24.x_ref, bf16[2,8,128,256]{3,2,1,0:T(8,128)(2,1)S(1)} %get-tuple-element.26.grown_ref, bf16[2,8,128,256]{3,2,1,0:T(8,128)(2,1)S(1)} %get-tuple-element.27.back_ref, bf16[2,8,128,256]{3,2,1,0:T(8,128)(2,1)S(1)} %get-tuple-element.28.trans_ref), custom_call_target="tpu_custom_call" | custom-call | flops 1006632960 | bytes 4194304 | tf_op jit(solution)/shard_map/couplings/pallas_call | solution.py:431
  35.3 1.6 %collective-permute-start.4 = (f32[200,128]{1,0:T(8,128)S(1)}, f32[200,128]{1,0:T(8,128)S(1)}, u32[]{:S(2)}, u32[]{:S(2)}) collective-permute-start(f32[200,128]{1,0:T(8,128)S(1)} %couplings.2), channel_id=1, source_target_pairs={{0,8},{1,17},{2,10},{3,19},{4,12},{5,21},{6,14},{7,23},{8,0},{9,25... | collective-permute-start | bytes 307208 | tf_op jit(solution)/shard_map/ppermute | solution.py:532
  36.9 3.2 %collective-permute-done.4 = f32[200,128]{1,0:T(8,128)S(1)} collective-permute-done((f32[200,128]{1,0:T(8,128)S(1)}, f32[200,128]{1,0:T(8,128)S(1)}, u32[]{:S(2)}, u32[]{:S(2)}) %collective-permute-start.4) | collective-permute-done | bytes 102432 | tf_op jit(solution)/shard_map/ppermute | solution.py:532
  40.0 0.6 %collective-permute-start.5 = (f32[200,128]{1,0:T(8,128)S(1)}, f32[200,128]{1,0:T(8,128)S(1)}, u32[]{:S(2)}, u32[]{:S(2)}) collective-permute-start(f32[200,128]{1,0:T(8,128)S(1)} %add.3.mine_ref), channel_id=1, source_target_pairs={{0,16},{1,9},{2,18},{3,11},{4,20},{5,13},{6,22},{7,15},{8,24},{9,1... | collective-permute-start | bytes 307208 | tf_op jit(solution)/shard_map/ppermute | solution.py:532
  40.6 1.5 %project.2.rest_0_ = f32[5,1024]{1,0:T(8,128)S(1)} custom-call(s32[8]{0:T(128)S(1)} %copy-done.1, bf16[4,128,1024]{2,1,0:T(8,128)(2,1)S(1)} %get-tuple-element.22.refs_1_.hi_ref, bf16[4,128,1024]{2,1,0:T(8,128)(2,1)S(1)} %get-tuple-element.23.lo_ref, f32[328,128]{1,0:T(8,128)S(1)} %sum_of_two.1.mine_ref, f32[328,128]{1,0:T(8,128)S(1)} %collective-permute-done.7.theirs_ref), custom_call_target="tpu_custom_call" | custom-call | flops 402653184 | bytes 4194304 | tf_op jit(solution)/shard_map/project/pallas_call | solution.py:431
  42.1 2.7 %collective-permute-done.5.theirs_ref = f32[200,128]{1,0:T(8,128)S(1)} collective-permute-done((f32[200,128]{1,0:T(8,128)S(1)}, f32[200,128]{1,0:T(8,128)S(1)}, u32[]{:S(2)}, u32[]{:S(2)}) %collective-permute-start.5) | collective-permute-done | bytes 102432 | tf_op jit(solution)/shard_map/ppermute | solution.py:532
  44.8 1.8 %project.3 = f32[8,1024]{1,0:T(8,128)} custom-call(s32[8]{0:T(128)S(1)} %copy-done.1, bf16[4,128,1024]{2,1,0:T(8,128)(2,1)S(1)} %get-tuple-element.22.refs_1_.hi_ref, bf16[4,128,1024]{2,1,0:T(8,128)(2,1)S(1)} %get-tuple-element.23.lo_ref, f32[200,128]{1,0:T(8,128)S(1)} %add.3.mine_ref, f32[200,128]{1,0:T(8,128)S(1)} %collective-permute-done.5.theirs_ref, ...), custom_call_target="tpu_custom_call" | custom-call | flops 402653184 | bytes 4194304 | tf_op jit(solution)/shard_map/project/pallas_call | solution.py:431
  (13 shorter events, 0.1 us)
Async XLA Ops:
  2.0 8.6 %copy-start.2 = (f32[8,3,2,128,128]{4,3,2,1,0:T(8,128)S(1)}, f32[8,3,2,128,128]{4,3,2,1,0:T(8,128)}, u32[]{:S(2)}) copy-start(f32[8,3,2,128,128]{4,3,2,1,0:T(8,128)} %lib_ref.3) | copy-start | bytes 9437188
  2.2 0.8 %copy-start.4 = (f32[4,2,128,128]{3,2,1,0:T(8,128)}, f32[4,2,128,128]{3,2,1,0:T(8,128)S(1)}, u32[]{:S(2)}) copy-start(f32[4,2,128,128]{3,2,1,0:T(8,128)S(1)} %get-tuple-element.18.col_ref.refs_6_) | copy-start | bytes 1572868
  3.1 11.3 %collective-permute-start = (s32[1,8]{1,0:T(1,128)S(1)}, s32[1,8]{1,0:T(1,128)S(1)}, u32[]{:S(2)}, u32[]{:S(2)}) collective-permute-start(s32[1,8]{1,0:T(1,128)S(1)} %get-tuple-element.16.code_ref), channel_id=1, source_target_pairs={{4,0},{7,1},{0,2},{6,3},{1,4},{3,5},{2,6},{5,7},{12,8},{15,9},{8,1... | collective-permute-start | bytes 104 | tf_op jit(solution)/shard_map/ppermute | solution.py:473
  6.1 8.3 %collective-permute-start.1 = (s32[1,8]{1,0:T(1,128)S(1)}, s32[1,8]{1,0:T(1,128)S(1)}, u32[]{:S(2)}, u32[]{:S(2)}) collective-permute-start(s32[1,8]{1,0:T(1,128)S(1)} %get-tuple-element.16.code_ref), channel_id=1, source_target_pairs={{3,0},{6,1},{5,2},{7,3},{0,4},{2,5},{1,6},{4,7},{11,8},{14,9},{13,... | collective-permute-start | bytes 104 | tf_op jit(solution)/shard_map/ppermute | solution.py:473
  7.1 7.2 %collective-permute-start.2 = (s32[1,8]{1,0:T(1,128)S(1)}, s32[1,8]{1,0:T(1,128)S(1)}, u32[]{:S(2)}, u32[]{:S(2)}) collective-permute-start(s32[1,8]{1,0:T(1,128)S(1)} %get-tuple-element.16.code_ref), channel_id=1, source_target_pairs={{2,0},{5,1},{4,2},{1,3},{6,4},{7,5},{0,6},{3,7},{10,8},{13,9},{12,... | collective-permute-start | bytes 104 | tf_op jit(solution)/shard_map/ppermute | solution.py:473
  10.6 1.0 %copy-start.5 = (f32[4,2,128,128]{3,2,1,0:T(8,128)S(1)}, f32[4,2,128,128]{3,2,1,0:T(8,128)}, u32[]{:S(2)}) copy-start(f32[4,2,128,128]{3,2,1,0:T(8,128)} %copy-done.4) | copy-start | bytes 1572868
  11.7 2.7 %copy-start.6 = (f32[4,2,128,128]{3,2,1,0:T(8,128)S(1)}, f32[4,2,128,128]{3,2,1,0:T(8,128)}, u32[]{:S(2)}) copy-start(f32[4,2,128,128]{3,2,1,0:T(8,128)} %copy-done.4) | copy-start | bytes 1572868
  21.2 2.9 %collective-permute-start.3 = (f32[9,128,256]{2,1,0:T(8,128)S(1)}, f32[9,128,256]{2,1,0:T(8,128)S(1)}, u32[]{:S(2)}, u32[]{:S(2)}) collective-permute-start(f32[9,128,256]{2,1,0:T(8,128)S(1)} %far_trees.1.mine_ref), channel_id=1, source_target_pairs={{0,1},{1,0},{2,3},{3,2},{4,5},{5,4},{6,7},{7,6},{8,9},{9,8},{10,11... | collective-permute-start | bytes 3538952 | tf_op jit(solution)/shard_map/ppermute | solution.py:491
  21.3 2.8 %copy-start.3 = (f32[1,2,128,128]{3,2,1,0:T(8,128)S(1)}, f32[1,2,128,128]{3,2,1,0:T(8,128)}, u32[]{:S(2)}) copy-start(f32[1,2,128,128]{3,2,1,0:T(8,128)} %param.13) | copy-start | bytes 393220
  25.6 3.1 %copy-start = (f32[4,128,1024]{2,1,0:T(8,128)S(1)}, f32[4,128,1024]{2,1,0:T(8,128)}, u32[]{:S(2)}) copy-start(f32[4,128,1024]{2,1,0:T(8,128)} %field_ref.1) | copy-start | bytes 6291460
  27.1 5.4 %collective-permute-start.6 = (f32[328,128]{1,0:T(8,128)S(1)}, f32[328,128]{1,0:T(8,128)S(1)}, u32[]{:S(2)}, u32[]{:S(2)}) collective-permute-start(f32[328,128]{1,0:T(8,128)S(1)} %couplings.3.a_ref), channel_id=1, source_target_pairs={{0,8},{1,17},{2,10},{3,19},{4,12},{5,21},{6,14},{7,23},{8,0},{9,25... | collective-permute-start | bytes 503816 | tf_op jit(solution)/shard_map/ppermute | solution.py:532
  32.6 8.0 %copy-start.1 = (s32[8]{0:T(128)S(1)}, s32[8]{0:T(128)}, u32[]{:S(2)}) copy-start(s32[8]{0:T(128)} %prof_ref.3) | copy-start | bytes 100
  32.6 8.0 %collective-permute-start.7 = (f32[328,128]{1,0:T(8,128)S(1)}, f32[328,128]{1,0:T(8,128)S(1)}, u32[]{:S(2)}, u32[]{:S(2)}) collective-permute-start(f32[328,128]{1,0:T(8,128)S(1)} %sum_of_two.1.mine_ref), channel_id=1, source_target_pairs={{0,16},{1,9},{2,18},{3,11},{4,20},{5,13},{6,22},{7,15},{8,24},{9,1... | collective-permute-start | bytes 503816 | tf_op jit(solution)/shard_map/ppermute | solution.py:532
  35.3 4.7 %collective-permute-start.4 = (f32[200,128]{1,0:T(8,128)S(1)}, f32[200,128]{1,0:T(8,128)S(1)}, u32[]{:S(2)}, u32[]{:S(2)}) collective-permute-start(f32[200,128]{1,0:T(8,128)S(1)} %couplings.2), channel_id=1, source_target_pairs={{0,8},{1,17},{2,10},{3,19},{4,12},{5,21},{6,14},{7,23},{8,0},{9,25... | collective-permute-start | bytes 307208 | tf_op jit(solution)/shard_map/ppermute | solution.py:532
  40.0 4.7 %collective-permute-start.5 = (f32[200,128]{1,0:T(8,128)S(1)}, f32[200,128]{1,0:T(8,128)S(1)}, u32[]{:S(2)}, u32[]{:S(2)}) collective-permute-start(f32[200,128]{1,0:T(8,128)S(1)} %add.3.mine_ref), channel_id=1, source_target_pairs={{0,16},{1,9},{2,18},{3,11},{4,20},{5,13},{6,22},{7,15},{8,24},{9,1... | collective-permute-start | bytes 307208 | tf_op jit(solution)/shard_map/ppermute | solution.py:532

commit v8 on v7

--- a/solution.py
+++ b/solution.py
@@ -111,17 +111,19 @@
     )
 
 
-def table_kernel(code_ref, real_ref, imag_ref, sent_ref, row_ref, col_ref):
+def table_kernel(code_ref, real_ref, imag_ref, sent_ref, row_ref):
     sent_ref[...] = code_ref[...]
     for part, ref in enumerate((real_ref, imag_ref)):
         profiles, m = ref.shape
         for q in range(profiles):
-            wide = jnp.broadcast_to(ref[q : q + 1], (m, m))
-            row_ref[q, part] = wide[:8]
-            col_ref[q, part] = wide.T
-
-
-def own_kernel(code_ref, lib_ref, row_ref, col_ref, nodes_ref, own_ref):
+            row_ref[q, part] = jnp.broadcast_to(ref[q : q + 1], (8, m))
+
+
+def own_kernel(code_ref, lib_ref, row_ref, nodes_ref, own_ref, col_ref):
+    profiles, parts, _, m = row_ref.shape
+    for q in range(profiles):
+        for part in range(parts):
+            col_ref[q, part] = jnp.broadcast_to(row_ref[q, part][:1], (m, m)).T
     cells = code_ref.shape[1]
 
     def cell(i):
@@ -338,9 +340,8 @@
     x_ref[1, 0], x_ref[1, 1] = right(split(mul(split(s_block), x1)))
 
 
-def reflect_kernel(me_ref, mine_ref, theirs_ref, part_ref, out_ref, mark_ref, left_ref):
+def reflect_kernel(me_ref, mine_ref, theirs_ref, part_ref, out_ref, left_ref):
     rows, m = out_ref.shape[1:]
-    mark_ref[...] = jnp.zeros_like(mark_ref)
     _, first, second = sides(me_ref, mine_ref, theirs_ref)
     left_ref[0] = first(LEFT + REFL)
     left_ref[1] = first(LEFT + BACK)
@@ -383,10 +384,6 @@
         out_ref[group * h + j : group * h + j + 1] = jnp.sum(
             jnp.where(eye, c, 0.0), axis=0, keepdims=True
         )
-
-
-def add_kernel(a_ref, b_ref, *refs):
-    refs[-1][...] = a_ref[...] + b_ref[...]
 
 
 def field_kernel(field_ref, hi_ref, lo_ref):
@@ -424,8 +421,7 @@
 
 def call(kernel, name, kinds, outs, scratch, limit, products, *args):
     def spec(kind):
-        spaces = {"s": pltpu.SMEM, "v": pltpu.VMEM, "a": pl.ANY}
-        return pl.BlockSpec(memory_space=spaces[kind])
+        return pl.BlockSpec(memory_space=pltpu.SMEM if kind == "s" else pltpu.VMEM)
 
     several = isinstance(outs, list)
     return pl.pallas_call(
@@ -463,19 +459,20 @@
     def bf16(*shape):
         return jax.ShapeDtypeStruct(shape, BF16)
 
-    tables = [f32(profiles, 2, 8, m), f32(profiles, 2, m, m)]
     codes = ((cell_profile << SHIFT) | cell_section).reshape(1, cells)
-    codes, row_table, col_table = call(
-        table_kernel, "tables", "vvv", [jax.ShapeDtypeStruct((1, cells), jnp.int32), *tables], [],
-        12, 60, codes, *factors,
+    codes, row_table = call(
+        table_kernel, "tables", "vvv",
+        [jax.ShapeDtypeStruct((1, cells), jnp.int32), f32(profiles, 2, 8, m)], [], 12, 60,
+        codes, *factors,
     )
     got = [
         lax.ppermute(codes, "cell", [(block, device) for device, block in enumerate(source)])
         for source in routes(chips)
     ]
-    nodes, own = call(
-        own_kernel, "own_tree", "svvv", [bf16(*pairs(6, 3)), f32(3, m, 2 * m)], [], 12, 28,
-        codes, interfaces, row_table, col_table,
+    nodes, own, col_table = call(
+        own_kernel, "own_tree", "svv",
+        [bf16(*pairs(6, 3)), f32(3, m, 2 * m), f32(profiles, 2, m, m)], [], 12, 28,
+        codes, interfaces, row_table,
     )
     mine = call(
         far_kernel, "far_trees", "s" * chips + "vvvv", f32(9, m, 2 * m),
@@ -510,8 +507,8 @@
         )
         for start, group in ((0, more), (more, FEWER))
     ]
-    reflection, mark = call(
-        reflect_kernel, "reflection", "svvv", [f32(2, m // blocks, m), f32(8, m)],
+    reflection = call(
+        reflect_kernel, "reflection", "svvv", f32(2, m // blocks, m),
         [pltpu.VMEM((2, m, 2 * m), F32)], 12, 10,
         me, mine, theirs, part,
     )
@@ -538,12 +535,7 @@
     for group, packed in zip((more, FEWER), groups):
         other = jnp.zeros_like(packed)
         for number in range(len(steps)):
-            if number == 1 and not start:
-                packed = call(
-                    add_kernel, "sum_of_two", "vvaa", packed_shape(group), [], 12, 0,
-                    packed, other, mark, fields[0],
-                )
-            elif number:
+            if number:
                 packed = packed + other
             other = exchange(packed, number)
         gradient = [

time: 46.8 us -> 38.9 us (0.83)
  waiting for transfers between devices: 8.03 us -> 4.26 us
  starting transfers between devices: 12.9 us -> 10.7 us
  local copies, waits for them, and re-layouts: 1.87 us -> 0.02 us
    ppermute x4, waiting for transfers between devices: 7.8 us -> 2.53 us  [exchange(): return lax.ppermute(part, ('wl', 'cell'), pairs_of)]
    ppermute x3, starting transfers between devices: 7.58 us -> 5.11 us  [body(): lax.ppermute(codes, 'cell', [(block, device) for device, block in enumera...]
    unnamed x14 -> x8, local copies, waits for them, and re-layouts: 1.87 us -> 0.02 us
    ppermute x3, waiting for transfers between devices: 0.01 us -> 1.73 us  [body(): lax.ppermute(codes, 'cell', [(block, device) for device, block in enumera...]
    pallas_call x12 -> x11, Pallas kernels: 21.5 us -> 21.5 us  [call(): pl.pallas_call(kernel, out_shape=outs, in_specs=[spec(kind) for kind in k...]
  transfers between devices with their start and end apart: 8 -> 8, of which waited for: 4 -> 4; matrix products, arithmetic and copies ran while one was open for 0% -> 0% of each run, Pallas kernels for 21% -> 25%
where the time goes in v8:
time: 38.9 us; the launch traced here: 38.7 us
  Pallas kernels  21.5 us (55%)
  starting transfers between devices  10.7 us (28%)
  waiting for transfers between devices  4.26 us (11%)
  other arithmetic  1.45 us (4%)
  between operations  0.77 us (2%)
    pallas_call x11, Pallas kernels, call(): pl.pallas_call(kernel, out_shape=outs, in_specs=[spec(kind) for kind in k...  21.5 us
    ppermute x4, starting transfers between devices, exchange(): return lax.ppermute(part, ('wl', 'cell'), pairs_of)  5.26 us
    ppermute x3, starting transfers between devices, body(): lax.ppermute(codes, 'cell', [(block, device) for device, block in enumera...  5.11 us
    ppermute x4, waiting for transfers between devices, exchange(): return lax.ppermute(part, ('wl', 'cell'), pairs_of)  2.53 us
    ppermute x3, waiting for transfers between devices, body(): lax.ppermute(codes, 'cell', [(block, device) for device, block in enumera...  1.73 us
  transfers between devices with their start and end apart: 8, of which 4 were waited for; matrix products, arithmetic and copies ran while one was open for 0% of the time, Pallas kernels for 25%

profile of v8, /device:TPU:0, one launch (start us, length us, event | category | flops | bytes accessed | tf_op | source)
XLA Modules:
  0.0 38.7 jit_solution(12375038047836573999)
XLA Ops:
  0.6 0.7 %or_bitcast_fusion.code_ref = s32[1,8]{1,0:T(1,128)S(1)} fusion(s32[8]{0:T(128)} %param.9, s32[8]{0:T(128)} %prof_ref.3), kind=kLoop, calls=%fused_computation.2 | loop fusion | flops 16 | bytes 96 | tf_op jit(solution)/shard_map/reshape | solution.py:462
  1.3 0.7 %bitcast_multiply_fusion = (f32[4,128]{1,0:T(4,128)S(1)}, f32[4,128]{1,0:T(4,128)S(1)}) fusion(f32[4,128]{1,0:T(4,128)} %param.10, f32[4,1,128]{2,0,1:T(4,128)} %bitcast.11), kind=kLoop, calls=%fused_computation | loop fusion | flops 1024 | bytes 8192 | tf_op jit(solution)/shard_map/mul | solution.py:449
  2.0 0.0 copy-start.2
  2.1 5.1 %collective-permute-start.2 = (s32[1,8]{1,0:T(1,128)S(1)}, s32[1,8]{1,0:T(1,128)S(1)}, u32[]{:S(2)}, u32[]{:S(2)}) collective-permute-start(s32[1,8]{1,0:T(1,128)S(1)} %get-tuple-element.14.code_ref), channel_id=1, source_target_pairs={{2,0},{5,1},{4,2},{1,3},{6,4},{7,5},{0,6},{3,7},{10,8},{13,9},{12,... | collective-permute-start | bytes 104 | tf_op jit(solution)/shard_map/ppermute | solution.py:469
  7.2 0.0 collective-permute-start.1
  7.2 0.0 collective-permute-start
  7.2 0.0 copy-done.2
  7.2 2.7 %own_tree.1 = (bf16[6,3,2,128,256]{4,3,2,1,0:T(8,128)(2,1)S(1)}, f32[3,128,256]{2,1,0:T(8,128)S(1)}, f32[4,2,128,128]{3,2,1,0:T(8,128)S(1)}) custom-call(s32[1,8]{1,0:T(1,128)S(1)} %get-tuple-element.14.code_ref, f32[8,3,2,128,128]{4,3,2,1,0:T(8,128)S(1)} %copy-done.2, f32[4,2,8,128]{3,2,1,0:T(8,128)S(1)} %get-tuple-element.15.row_ref.refs_5_), custom_call_target="tpu_custom_call" | custom-call | flops 2818572288 | bytes 4194304 | tf_op jit(solution)/shard_map/own_tree/pallas_call | solution.py:427
  9.9 0.0 collective-permute-done.2.refs_3_
  9.9 0.3 collective-permute-done.1.refs_2_
  10.1 1.5 %collective-permute-done.refs_1_ = s32[1,8]{1,0:T(1,128)S(1)} collective-permute-done((s32[1,8]{1,0:T(1,128)S(1)}, s32[1,8]{1,0:T(1,128)S(1)}, u32[]{:S(2)}, u32[]{:S(2)}) %collective-permute-start) | collective-permute-done | bytes 64 | tf_op jit(solution)/shard_map/ppermute | solution.py:469
  11.6 6.8 %far_trees.1.mine_ref = f32[9,128,256]{2,1,0:T(8,128)S(1)} custom-call(s32[1]{0:T(128)} %bitcast.refs_0_.me_ref, s32[1,8]{1,0:T(1,128)S(1)} %collective-permute-done.refs_1_, s32[1,8]{1,0:T(1,128)S(1)} %collective-permute-done.1.refs_2_, s32[1,8]{1,0:T(1,128)S(1)} %collective-permute-done.2.refs_3_, f32[8,3,2,128,128]{4,3,2,1,0:T(8,128)S(1)} %copy-done.2, ...), custom_call_target="tpu_custom_call" | custom-call | flops 9663676416 | bytes 4194304 | tf_op jit(solution)/shard_map/far_trees/pallas_call | solution.py:427
  18.4 0.4 collective-permute-start.3
  18.8 2.6 %own_scan.1 = (bf16[2,8,128,256]{3,2,1,0:T(8,128)(2,1)S(1)}, bf16[2,8,128,256]{3,2,1,0:T(8,128)(2,1)S(1)}, bf16[2,8,128,256]{3,2,1,0:T(8,128)(2,1)S(1)}) custom-call(s32[1,8]{1,0:T(1,128)S(1)} %get-tuple-element.14.code_ref, f32[8,3,2,128,128]{4,3,2,1,0:T(8,128)S(1)} %copy-done.2, f32[4,2,8,128]{3,2,1,0:T(8,128)S(1)} %get-tuple-element.15.row_ref.refs_5_, ...), custom_call_target="tpu_custom_call" | custom-call | flops 2717908992 | bytes 4194304 | tf_op jit(solution)/shard_map/own_scan/pallas_call | solution.py:427
  21.4 0.0 collective-permute-done.3.theirs_ref
  21.4 1.5 %chain.1 = (bf16[2,2,256,256]{3,2,1,0:T(8,128)(2,1)S(1)}, f32[2,128,256]{2,1,0:T(8,128)S(1)}) custom-call(s32[1]{0:T(128)} %bitcast.refs_0_.me_ref, f32[2,128,128]{2,1,0:T(8,128)S(1)} %bitcast.10, f32[9,128,256]{2,1,0:T(8,128)S(1)} %far_trees.1.mine_ref, f32[9,128,256]{2,1,0:T(8,128)S(1)} %collective-permute-done.3.theirs_ref), custom_call_target="tpu_custom_call" | custom-call | flops 2013265920 | bytes 4194304 | tf_op jit(solution)/shard_map/chain/pallas_call | solution.py:427
  22.9 1.5 %couplings.3 = f32[328,128]{1,0:T(8,128)S(1)} custom-call(bf16[2,2,256,256]{3,2,1,0:T(8,128)(2,1)S(1)} %get-tuple-element.21.x_ref, bf16[2,8,128,256]{3,2,1,0:T(8,128)(2,1)S(1)} %get-tuple-element.23.grown_ref, bf16[2,8,128,256]{3,2,1,0:T(8,128)(2,1)S(1)} %get-tuple-element.24.back_ref, bf16[2,8,128,256]{3,2,1,0:T(8,128)(2,1)S(1)} %get-tuple-element.25.trans_ref), custom_call_target="tpu_custom_call" | custom-call | flops 1006632960 | bytes 4194304 | tf_op jit(solution)/shard_map/couplings/pallas_call | solution.py:427
  24.4 0.0 copy-start
  24.5 1.6 %collective-permute-start.6 = (f32[328,128]{1,0:T(8,128)S(1)}, f32[328,128]{1,0:T(8,128)S(1)}, u32[]{:S(2)}, u32[]{:S(2)}) collective-permute-start(f32[328,128]{1,0:T(8,128)S(1)} %couplings.3), channel_id=1, source_target_pairs={{0,8},{1,17},{2,10},{3,19},{4,12},{5,21},{6,14},{7,23},{8,0},{9,25... | collective-permute-start | bytes 503816 | tf_op jit(solution)/shard_map/ppermute | solution.py:529
  26.0 1.1 %couplings.2 = f32[200,128]{1,0:T(8,128)S(1)} custom-call(bf16[2,2,256,256]{3,2,1,0:T(8,128)(2,1)S(1)} %get-tuple-element.21.x_ref, bf16[2,8,128,256]{3,2,1,0:T(8,128)(2,1)S(1)} %get-tuple-element.23.grown_ref, bf16[2,8,128,256]{3,2,1,0:T(8,128)(2,1)S(1)} %get-tuple-element.24.back_ref, bf16[2,8,128,256]{3,2,1,0:T(8,128)(2,1)S(1)} %get-tuple-element.25.trans_ref), custom_call_target="tpu_custom_call" | custom-call | flops 1006632960 | bytes 4194304 | tf_op jit(solution)/shard_map/couplings/pallas_call | solution.py:427
  27.1 0.6 %collective-permute-start.4 = (f32[200,128]{1,0:T(8,128)S(1)}, f32[200,128]{1,0:T(8,128)S(1)}, u32[]{:S(2)}, u32[]{:S(2)}) collective-permute-start(f32[200,128]{1,0:T(8,128)S(1)} %couplings.2), channel_id=1, source_target_pairs={{0,8},{1,17},{2,10},{3,19},{4,12},{5,21},{6,14},{7,23},{8,0},{9,25... | collective-permute-start | bytes 307208 | tf_op jit(solution)/shard_map/ppermute | solution.py:529
  27.7 2.2 %collective-permute-done.6 = f32[328,128]{1,0:T(8,128)S(1)} collective-permute-done((f32[328,128]{1,0:T(8,128)S(1)}, f32[328,128]{1,0:T(8,128)S(1)}, u32[]{:S(2)}, u32[]{:S(2)}) %collective-permute-start.6) | collective-permute-done | bytes 167968 | tf_op jit(solution)/shard_map/ppermute | solution.py:529
  29.9 1.6 %collective-permute-start.7 = (f32[328,128]{1,0:T(8,128)S(1)}, f32[328,128]{1,0:T(8,128)S(1)}, u32[]{:S(2)}, u32[]{:S(2)}) collective-permute-start(f32[328,128]{1,0:T(8,128)S(1)} %add.7.mine_ref), channel_id=1, source_target_pairs={{0,16},{1,9},{2,18},{3,11},{4,20},{5,13},{6,22},{7,15},{8,24},{9,1... | collective-permute-start | bytes 503816 | tf_op jit(solution)/shard_map/ppermute | solution.py:529
  31.5 0.4 field_parts.1
  31.9 0.0 copy-start.1
  31.9 0.0 collective-permute-done.4
  31.9 1.5 %collective-permute-start.5 = (f32[200,128]{1,0:T(8,128)S(1)}, f32[200,128]{1,0:T(8,128)S(1)}, u32[]{:S(2)}, u32[]{:S(2)}) collective-permute-start(f32[200,128]{1,0:T(8,128)S(1)} %add.6.mine_ref), channel_id=1, source_target_pairs={{0,16},{1,9},{2,18},{3,11},{4,20},{5,13},{6,22},{7,15},{8,24},{9,1... | collective-permute-start | bytes 307208 | tf_op jit(solution)/shard_map/ppermute | solution.py:529
  33.4 1.5 %reflection.1 = f32[2,16,128]{2,1,0:T(8,128)} custom-call(s32[1]{0:T(128)} %bitcast.refs_0_.me_ref, f32[9,128,256]{2,1,0:T(8,128)S(1)} %far_trees.1.mine_ref, f32[9,128,256]{2,1,0:T(8,128)S(1)} %collective-permute-done.3.theirs_ref, f32[2,128,256]{2,1,0:T(8,128)S(1)} %get-tuple-element.18.part_ref), custom_call_target="tpu_custom_call" | custom-call | flops 1006632960 | bytes 4194304 | tf_op jit(solution)/shard_map/reflection/pallas_call | solution.py:427
  35.0 0.3 collective-permute-done.7.theirs_ref
  35.3 1.5 %project.2.rest_0_ = f32[5,1024]{1,0:T(8,128)S(1)} custom-call(s32[8]{0:T(128)S(1)} %copy-done.1, bf16[4,128,1024]{2,1,0:T(8,128)(2,1)S(1)} %get-tuple-element.19.hi_ref, bf16[4,128,1024]{2,1,0:T(8,128)(2,1)S(1)} %get-tuple-element.20.lo_ref, f32[328,128]{1,0:T(8,128)S(1)} %add.7.mine_ref, f32[328,128]{1,0:T(8,128)S(1)} %collective-permute-done.7.theirs_ref), custom_call_target="tpu_custom_call" | custom-call | flops 402653184 | bytes 4194304 | tf_op jit(solution)/shard_map/project/pallas_call | solution.py:427
  36.9 0.0 collective-permute-done.5.theirs_ref
  36.9 1.8 %project.3 = f32[8,1024]{1,0:T(8,128)} custom-call(s32[8]{0:T(128)S(1)} %copy-done.1, bf16[4,128,1024]{2,1,0:T(8,128)(2,1)S(1)} %get-tuple-element.19.hi_ref, bf16[4,128,1024]{2,1,0:T(8,128)(2,1)S(1)} %get-tuple-element.20.lo_ref, f32[200,128]{1,0:T(8,128)S(1)} %add.6.mine_ref, f32[200,128]{1,0:T(8,128)S(1)} %collective-permute-done.5.theirs_ref, ...), custom_call_target="tpu_custom_call" | custom-call | flops 402653184 | bytes 4194304 | tf_op jit(solution)/shard_map/project/pallas_call | solution.py:427
  (7 shorter events, 0.1 us)
Async XLA Ops:
  2.0 5.1 %copy-start.2 = (f32[8,3,2,128,128]{4,3,2,1,0:T(8,128)S(1)}, f32[8,3,2,128,128]{4,3,2,1,0:T(8,128)}, u32[]{:S(2)}) copy-start(f32[8,3,2,128,128]{4,3,2,1,0:T(8,128)} %lib_ref.3) | copy-start | bytes 9437188
  2.1 7.8 %collective-permute-start.2 = (s32[1,8]{1,0:T(1,128)S(1)}, s32[1,8]{1,0:T(1,128)S(1)}, u32[]{:S(2)}, u32[]{:S(2)}) collective-permute-start(s32[1,8]{1,0:T(1,128)S(1)} %get-tuple-element.14.code_ref), channel_id=1, source_target_pairs={{2,0},{5,1},{4,2},{1,3},{6,4},{7,5},{0,6},{3,7},{10,8},{13,9},{12,... | collective-permute-start | bytes 104 | tf_op jit(solution)/shard_map/ppermute | solution.py:469
  7.2 3.0 %collective-permute-start.1 = (s32[1,8]{1,0:T(1,128)S(1)}, s32[1,8]{1,0:T(1,128)S(1)}, u32[]{:S(2)}, u32[]{:S(2)}) collective-permute-start(s32[1,8]{1,0:T(1,128)S(1)} %get-tuple-element.14.code_ref), channel_id=1, source_target_pairs={{3,0},{6,1},{5,2},{7,3},{0,4},{2,5},{1,6},{4,7},{11,8},{14,9},{13,... | collective-permute-start | bytes 104 | tf_op jit(solution)/shard_map/ppermute | solution.py:469
  7.2 4.4 %collective-permute-start = (s32[1,8]{1,0:T(1,128)S(1)}, s32[1,8]{1,0:T(1,128)S(1)}, u32[]{:S(2)}, u32[]{:S(2)}) collective-permute-start(s32[1,8]{1,0:T(1,128)S(1)} %get-tuple-element.14.code_ref), channel_id=1, source_target_pairs={{4,0},{7,1},{0,2},{6,3},{1,4},{3,5},{2,6},{5,7},{12,8},{15,9},{8,1... | collective-permute-start | bytes 104 | tf_op jit(solution)/shard_map/ppermute | solution.py:469
  18.4 3.0 %collective-permute-start.3 = (f32[9,128,256]{2,1,0:T(8,128)S(1)}, f32[9,128,256]{2,1,0:T(8,128)S(1)}, u32[]{:S(2)}, u32[]{:S(2)}) collective-permute-start(f32[9,128,256]{2,1,0:T(8,128)S(1)} %far_trees.1.mine_ref), channel_id=1, source_target_pairs={{0,1},{1,0},{2,3},{3,2},{4,5},{5,4},{6,7},{7,6},{8,9},{9,8},{10,11... | collective-permute-start | bytes 3538952 | tf_op jit(solution)/shard_map/ppermute | solution.py:488
  18.8 2.6 %copy-start.3 = (f32[1,2,128,128]{3,2,1,0:T(8,128)S(1)}, f32[1,2,128,128]{3,2,1,0:T(8,128)}, u32[]{:S(2)}) copy-start(f32[1,2,128,128]{3,2,1,0:T(8,128)} %param.13) | copy-start | bytes 393220
  24.4 7.1 %copy-start = (f32[4,128,1024]{2,1,0:T(8,128)S(1)}, f32[4,128,1024]{2,1,0:T(8,128)}, u32[]{:S(2)}) copy-start(f32[4,128,1024]{2,1,0:T(8,128)} %field_ref.1) | copy-start | bytes 6291460
  24.5 5.4 %collective-permute-start.6 = (f32[328,128]{1,0:T(8,128)S(1)}, f32[328,128]{1,0:T(8,128)S(1)}, u32[]{:S(2)}, u32[]{:S(2)}) collective-permute-start(f32[328,128]{1,0:T(8,128)S(1)} %couplings.3), channel_id=1, source_target_pairs={{0,8},{1,17},{2,10},{3,19},{4,12},{5,21},{6,14},{7,23},{8,0},{9,25... | collective-permute-start | bytes 503816 | tf_op jit(solution)/shard_map/ppermute | solution.py:529
  27.1 4.8 %collective-permute-start.4 = (f32[200,128]{1,0:T(8,128)S(1)}, f32[200,128]{1,0:T(8,128)S(1)}, u32[]{:S(2)}, u32[]{:S(2)}) collective-permute-start(f32[200,128]{1,0:T(8,128)S(1)} %couplings.2), channel_id=1, source_target_pairs={{0,8},{1,17},{2,10},{3,19},{4,12},{5,21},{6,14},{7,23},{8,0},{9,25... | collective-permute-start | bytes 307208 | tf_op jit(solution)/shard_map/ppermute | solution.py:529
  29.9 5.4 %collective-permute-start.7 = (f32[328,128]{1,0:T(8,128)S(1)}, f32[328,128]{1,0:T(8,128)S(1)}, u32[]{:S(2)}, u32[]{:S(2)}) collective-permute-start(f32[328,128]{1,0:T(8,128)S(1)} %add.7.mine_ref), channel_id=1, source_target_pairs={{0,16},{1,9},{2,18},{3,11},{4,20},{5,13},{6,22},{7,15},{8,24},{9,1... | collective-permute-start | bytes 503816 | tf_op jit(solution)/shard_map/ppermute | solution.py:529
  31.9 3.5 %copy-start.1 = (s32[8]{0:T(128)S(1)}, s32[8]{0:T(128)}, u32[]{:S(2)}) copy-start(s32[8]{0:T(128)} %prof_ref.3) | copy-start | bytes 100
  31.9 4.9 %collective-permute-start.5 = (f32[200,128]{1,0:T(8,128)S(1)}, f32[200,128]{1,0:T(8,128)S(1)}, u32[]{:S(2)}, u32[]{:S(2)}) collective-permute-start(f32[200,128]{1,0:T(8,128)S(1)} %add.6.mine_ref), channel_id=1, source_target_pairs={{0,16},{1,9},{2,18},{3,11},{4,20},{5,13},{6,22},{7,15},{8,24},{9,1... | collective-permute-start | bytes 307208 | tf_op jit(solution)/shard_map/ppermute | solution.py:529

commit v9 on v8

--- a/solution.py
+++ b/solution.py
@@ -111,19 +111,18 @@
     )
 
 
-def table_kernel(code_ref, real_ref, imag_ref, sent_ref, row_ref):
+def pass_kernel(code_ref, sent_ref):
     sent_ref[...] = code_ref[...]
-    for part, ref in enumerate((real_ref, imag_ref)):
-        profiles, m = ref.shape
+
+
+def own_kernel(code_ref, lib_ref, loss_ref, phase_ref, nodes_ref, own_ref, row_ref, col_ref):
+    profiles, m = loss_ref.shape
+    amp, angle = loss_ref[...], phase_ref[...]
+    for part, values in enumerate((amp * jnp.cos(angle), amp * jnp.sin(angle))):
         for q in range(profiles):
-            row_ref[q, part] = jnp.broadcast_to(ref[q : q + 1], (8, m))
-
-
-def own_kernel(code_ref, lib_ref, row_ref, nodes_ref, own_ref, col_ref):
-    profiles, parts, _, m = row_ref.shape
-    for q in range(profiles):
-        for part in range(parts):
-            col_ref[q, part] = jnp.broadcast_to(row_ref[q, part][:1], (m, m)).T
+            wide = jnp.broadcast_to(values[q : q + 1], (m, m))
+            row_ref[q, part] = wide[:8]
+            col_ref[q, part] = wide.T
     cells = code_ref.shape[1]
 
     def cell(i):
@@ -445,8 +444,6 @@
     waves = lax.axis_size("wl")
     pixels = mode_field.shape[2]
     chips = blocks // 2
-    angle = phase.reshape(profiles, m)
-    factors = (mode_loss * jnp.cos(angle), mode_loss * jnp.sin(angle))
     wanted = target.reshape(2, m, m)
     me = lax.axis_index("cell").astype(jnp.int32).reshape(1)
 
@@ -460,19 +457,21 @@
         return jax.ShapeDtypeStruct(shape, BF16)
 
     codes = ((cell_profile << SHIFT) | cell_section).reshape(1, cells)
-    codes, row_table = call(
-        table_kernel, "tables", "vvv",
-        [jax.ShapeDtypeStruct((1, cells), jnp.int32), f32(profiles, 2, 8, m)], [], 12, 60,
-        codes, *factors,
+    codes = call(
+        pass_kernel, "codes", "v", jax.ShapeDtypeStruct((1, cells), jnp.int32), [], 12, 60, codes
     )
     got = [
         lax.ppermute(codes, "cell", [(block, device) for device, block in enumerate(source)])
         for source in routes(chips)
     ]
-    nodes, own, col_table = call(
-        own_kernel, "own_tree", "svv",
-        [bf16(*pairs(6, 3)), f32(3, m, 2 * m), f32(profiles, 2, m, m)], [], 12, 28,
-        codes, interfaces, row_table,
+    nodes, own, row_table, col_table = call(
+        own_kernel, "own_tree", "svvv",
+        [
+            bf16(*pairs(6, 3)), f32(3, m, 2 * m),
+            f32(profiles, 2, 8, m), f32(profiles, 2, m, m),
+        ],
+        [], 12, 28,
+        codes, interfaces, mode_loss, phase.reshape(profiles, m),
     )
     mine = call(
         far_kernel, "far_trees", "s" * chips + "vvvv", f32(9, m, 2 * m),

time: 38.9 us -> 38.2 us (0.982)
  other arithmetic: 1.45 us -> 0.71 us
    mul x1 -> x0, other arithmetic: 0.74 us -> none  [body(): factors = (mode_loss * jnp.cos(angle), mode_loss * jnp.sin(angle))]
  transfers between devices with their start and end apart: 8 -> 8, of which waited for: 4 -> 4; matrix products, arithmetic and copies ran while one was open for 0% -> 0% of each run, Pallas kernels for 25% -> 26%
where the time goes in v9:
time: 38.2 us; the launch traced here: 38 us
  Pallas kernels  21.5 us (56%)
  starting transfers between devices  10.7 us (28%)
  waiting for transfers between devices  4.19 us (11%)
  between operations  0.78 us (2%)
  other arithmetic  0.71 us (2%)
    pallas_call x11, Pallas kernels, call(): pl.pallas_call(kernel, out_shape=outs, in_specs=[spec(kind) for kind in k...  21.5 us
    ppermute x4, starting transfers between devices, exchange(): return lax.ppermute(part, ('wl', 'cell'), pairs_of)  5.25 us
    ppermute x3, starting transfers between devices, body(): lax.ppermute(codes, 'cell', [(block, device) for device, block in enumera...  5.11 us
    ppermute x4, waiting for transfers between devices, exchange(): return lax.ppermute(part, ('wl', 'cell'), pairs_of)  2.53 us
    ppermute x3, waiting for transfers between devices, body(): lax.ppermute(codes, 'cell', [(block, device) for device, block in enumera...  1.66 us
  transfers between devices with their start and end apart: 8, of which 4 were waited for; matrix products, arithmetic and copies ran while one was open for 0% of the time, Pallas kernels for 26%

profile of v9, /device:TPU:0, one launch (start us, length us, event | category | flops | bytes accessed | tf_op | source)
XLA Modules:
  0.0 38.0 jit_solution(14362131123531702981)
XLA Ops:
  0.6 0.7 %or_bitcast_fusion.code_ref = s32[1,8]{1,0:T(1,128)S(1)} fusion(s32[8]{0:T(128)} %param.9, s32[8]{0:T(128)} %prof_ref.3), kind=kLoop, calls=%fused_computation | loop fusion | flops 16 | bytes 96 | tf_op jit(solution)/shard_map/reshape | solution.py:459
  1.3 5.1 %collective-permute-start.2 = (s32[1,8]{1,0:T(1,128)S(1)}, s32[1,8]{1,0:T(1,128)S(1)}, u32[]{:S(2)}, u32[]{:S(2)}) collective-permute-start(s32[1,8]{1,0:T(1,128)S(1)} %codes.1.code_ref), channel_id=1, source_target_pairs={{2,0},{5,1},{4,2},{1,3},{6,4},{7,5},{0,6},{3,7},{10,8},{13,9},{12,... | collective-permute-start | bytes 104 | tf_op jit(solution)/shard_map/ppermute | solution.py:464
  6.4 0.0 collective-permute-start.1
  6.4 0.0 collective-permute-start
  6.4 0.0 copy-done.2
  6.4 0.0 copy-done.4
  6.5 2.7 %own_tree.1 = (bf16[6,3,2,128,256]{4,3,2,1,0:T(8,128)(2,1)S(1)}, f32[3,128,256]{2,1,0:T(8,128)S(1)}, f32[4,2,8,128]{3,2,1,0:T(8,128)S(1)}, f32[4,2,128,128]{3,2,1,0:T(8,128)S(1)}) custom-call(s32[1,8]{1,0:T(1,128)S(1)} %codes.1.code_ref, f32[8,3,2,128,128]{4,3,2,1,0:T(8,128)S(1)} %copy-done.2, f32[4,128]{1,0:T(4,128)S(1)} %copy-done.4, f32[4,128]{1,0:T(4,128)S(1)} %bitcast.7), custom_call_target="tpu_custom_call" | custom-call | flops 2818572288 | bytes 4194304 | tf_op jit(solution)/shard_map/own_tree/pallas_call | solution.py:426
  9.2 0.0 collective-permute-done.2.refs_3_
  9.2 0.2 collective-permute-done.1.refs_2_
  9.4 1.5 %collective-permute-done.refs_1_ = s32[1,8]{1,0:T(1,128)S(1)} collective-permute-done((s32[1,8]{1,0:T(1,128)S(1)}, s32[1,8]{1,0:T(1,128)S(1)}, u32[]{:S(2)}, u32[]{:S(2)}) %collective-permute-start) | collective-permute-done | bytes 64 | tf_op jit(solution)/shard_map/ppermute | solution.py:464
  10.9 6.8 %far_trees.1.mine_ref = f32[9,128,256]{2,1,0:T(8,128)S(1)} custom-call(s32[1]{0:T(128)} %bitcast.refs_0_.me_ref, s32[1,8]{1,0:T(1,128)S(1)} %collective-permute-done.refs_1_, s32[1,8]{1,0:T(1,128)S(1)} %collective-permute-done.1.refs_2_, s32[1,8]{1,0:T(1,128)S(1)} %collective-permute-done.2.refs_3_, f32[8,3,2,128,128]{4,3,2,1,0:T(8,128)S(1)} %copy-done.2, ...), custom_call_target="tpu_custom_call" | custom-call | flops 9663676416 | bytes 4194304 | tf_op jit(solution)/shard_map/far_trees/pallas_call | solution.py:426
  17.7 0.4 collective-permute-start.3
  18.0 2.6 %own_scan.1 = (bf16[2,8,128,256]{3,2,1,0:T(8,128)(2,1)S(1)}, bf16[2,8,128,256]{3,2,1,0:T(8,128)(2,1)S(1)}, bf16[2,8,128,256]{3,2,1,0:T(8,128)(2,1)S(1)}) custom-call(s32[1,8]{1,0:T(1,128)S(1)} %codes.1.code_ref, f32[8,3,2,128,128]{4,3,2,1,0:T(8,128)S(1)} %copy-done.2, f32[4,2,8,128]{3,2,1,0:T(8,128)S(1)} %get-tuple-element.13.refs_5_.row_ref, ...), custom_call_target="tpu_custom_call" | custom-call | flops 2717908992 | bytes 4194304 | tf_op jit(solution)/shard_map/own_scan/pallas_call | solution.py:426
  20.6 0.0 collective-permute-done.3.theirs_ref
  20.7 1.5 %chain.1 = (bf16[2,2,256,256]{3,2,1,0:T(8,128)(2,1)S(1)}, f32[2,128,256]{2,1,0:T(8,128)S(1)}) custom-call(s32[1]{0:T(128)} %bitcast.refs_0_.me_ref, f32[2,128,128]{2,1,0:T(8,128)S(1)} %bitcast.6, f32[9,128,256]{2,1,0:T(8,128)S(1)} %far_trees.1.mine_ref, f32[9,128,256]{2,1,0:T(8,128)S(1)} %collective-permute-done.3.theirs_ref), custom_call_target="tpu_custom_call" | custom-call | flops 2013265920 | bytes 4194304 | tf_op jit(solution)/shard_map/chain/pallas_call | solution.py:426
  22.2 1.5 %couplings.3 = f32[328,128]{1,0:T(8,128)S(1)} custom-call(bf16[2,2,256,256]{3,2,1,0:T(8,128)(2,1)S(1)} %get-tuple-element.19.x_ref, bf16[2,8,128,256]{3,2,1,0:T(8,128)(2,1)S(1)} %get-tuple-element.21.grown_ref, bf16[2,8,128,256]{3,2,1,0:T(8,128)(2,1)S(1)} %get-tuple-element.22.back_ref, bf16[2,8,128,256]{3,2,1,0:T(8,128)(2,1)S(1)} %get-tuple-element.23.trans_ref), custom_call_target="tpu_custom_call" | custom-call | flops 1006632960 | bytes 4194304 | tf_op jit(solution)/shard_map/couplings/pallas_call | solution.py:426
  23.7 0.0 copy-start
  23.7 1.6 %collective-permute-start.6 = (f32[328,128]{1,0:T(8,128)S(1)}, f32[328,128]{1,0:T(8,128)S(1)}, u32[]{:S(2)}, u32[]{:S(2)}) collective-permute-start(f32[328,128]{1,0:T(8,128)S(1)} %couplings.3), channel_id=1, source_target_pairs={{0,8},{1,17},{2,10},{3,19},{4,12},{5,21},{6,14},{7,23},{8,0},{9,25... | collective-permute-start | bytes 503816 | tf_op jit(solution)/shard_map/ppermute | solution.py:528
  25.3 1.1 %couplings.2 = f32[200,128]{1,0:T(8,128)S(1)} custom-call(bf16[2,2,256,256]{3,2,1,0:T(8,128)(2,1)S(1)} %get-tuple-element.19.x_ref, bf16[2,8,128,256]{3,2,1,0:T(8,128)(2,1)S(1)} %get-tuple-element.21.grown_ref, bf16[2,8,128,256]{3,2,1,0:T(8,128)(2,1)S(1)} %get-tuple-element.22.back_ref, bf16[2,8,128,256]{3,2,1,0:T(8,128)(2,1)S(1)} %get-tuple-element.23.trans_ref), custom_call_target="tpu_custom_call" | custom-call | flops 1006632960 | bytes 4194304 | tf_op jit(solution)/shard_map/couplings/pallas_call | solution.py:426
  26.4 0.6 %collective-permute-start.4 = (f32[200,128]{1,0:T(8,128)S(1)}, f32[200,128]{1,0:T(8,128)S(1)}, u32[]{:S(2)}, u32[]{:S(2)}) collective-permute-start(f32[200,128]{1,0:T(8,128)S(1)} %couplings.2), channel_id=1, source_target_pairs={{0,8},{1,17},{2,10},{3,19},{4,12},{5,21},{6,14},{7,23},{8,0},{9,25... | collective-permute-start | bytes 307208 | tf_op jit(solution)/shard_map/ppermute | solution.py:528
  27.0 2.2 %collective-permute-done.6 = f32[328,128]{1,0:T(8,128)S(1)} collective-permute-done((f32[328,128]{1,0:T(8,128)S(1)}, f32[328,128]{1,0:T(8,128)S(1)}, u32[]{:S(2)}, u32[]{:S(2)}) %collective-permute-start.6) | collective-permute-done | bytes 167968 | tf_op jit(solution)/shard_map/ppermute | solution.py:528
  29.2 1.6 %collective-permute-start.7 = (f32[328,128]{1,0:T(8,128)S(1)}, f32[328,128]{1,0:T(8,128)S(1)}, u32[]{:S(2)}, u32[]{:S(2)}) collective-permute-start(f32[328,128]{1,0:T(8,128)S(1)} %add.7.mine_ref), channel_id=1, source_target_pairs={{0,16},{1,9},{2,18},{3,11},{4,20},{5,13},{6,22},{7,15},{8,24},{9,1... | collective-permute-start | bytes 503816 | tf_op jit(solution)/shard_map/ppermute | solution.py:528
  30.8 0.4 field_parts.1
  31.1 0.0 copy-start.1
  31.2 0.0 collective-permute-done.4
  31.2 1.5 %collective-permute-start.5 = (f32[200,128]{1,0:T(8,128)S(1)}, f32[200,128]{1,0:T(8,128)S(1)}, u32[]{:S(2)}, u32[]{:S(2)}) collective-permute-start(f32[200,128]{1,0:T(8,128)S(1)} %add.6.mine_ref), channel_id=1, source_target_pairs={{0,16},{1,9},{2,18},{3,11},{4,20},{5,13},{6,22},{7,15},{8,24},{9,1... | collective-permute-start | bytes 307208 | tf_op jit(solution)/shard_map/ppermute | solution.py:528
  32.7 1.5 %reflection.1 = f32[2,16,128]{2,1,0:T(8,128)} custom-call(s32[1]{0:T(128)} %bitcast.refs_0_.me_ref, f32[9,128,256]{2,1,0:T(8,128)S(1)} %far_trees.1.mine_ref, f32[9,128,256]{2,1,0:T(8,128)S(1)} %collective-permute-done.3.theirs_ref, f32[2,128,256]{2,1,0:T(8,128)S(1)} %get-tuple-element.16.part_ref), custom_call_target="tpu_custom_call" | custom-call | flops 1006632960 | bytes 4194304 | tf_op jit(solution)/shard_map/reflection/pallas_call | solution.py:426
  34.2 0.4 collective-permute-done.7.theirs_ref
  34.6 0.0 copy-done.1
  34.6 1.5 %project.2.rest_0_ = f32[5,1024]{1,0:T(8,128)S(1)} custom-call(s32[8]{0:T(128)S(1)} %copy-done.1, bf16[4,128,1024]{2,1,0:T(8,128)(2,1)S(1)} %get-tuple-element.17.hi_ref, bf16[4,128,1024]{2,1,0:T(8,128)(2,1)S(1)} %get-tuple-element.18.lo_ref, f32[328,128]{1,0:T(8,128)S(1)} %add.7.mine_ref, f32[328,128]{1,0:T(8,128)S(1)} %collective-permute-done.7.theirs_ref), custom_call_target="tpu_custom_call" | custom-call | flops 402653184 | bytes 4194304 | tf_op jit(solution)/shard_map/project/pallas_call | solution.py:426
  36.1 0.0 collective-permute-done.5.theirs_ref
  36.2 1.8 %project.3 = f32[8,1024]{1,0:T(8,128)} custom-call(s32[8]{0:T(128)S(1)} %copy-done.1, bf16[4,128,1024]{2,1,0:T(8,128)(2,1)S(1)} %get-tuple-element.17.hi_ref, bf16[4,128,1024]{2,1,0:T(8,128)(2,1)S(1)} %get-tuple-element.18.lo_ref, f32[200,128]{1,0:T(8,128)S(1)} %add.6.mine_ref, f32[200,128]{1,0:T(8,128)S(1)} %collective-permute-done.5.theirs_ref, ...), custom_call_target="tpu_custom_call" | custom-call | flops 402653184 | bytes 4194304 | tf_op jit(solution)/shard_map/project/pallas_call | solution.py:426
  (10 shorter events, 0.1 us)
Async XLA Ops:
  1.3 5.1 %copy-start.2 = (f32[8,3,2,128,128]{4,3,2,1,0:T(8,128)S(1)}, f32[8,3,2,128,128]{4,3,2,1,0:T(8,128)}, u32[]{:S(2)}) copy-start(f32[8,3,2,128,128]{4,3,2,1,0:T(8,128)} %lib_ref.3) | copy-start | bytes 9437188
  1.3 5.1 %copy-start.4 = (f32[4,128]{1,0:T(4,128)S(1)}, f32[4,128]{1,0:T(4,128)}, u32[]{:S(2)}) copy-start(f32[4,128]{1,0:T(4,128)} %loss_ref.1) | copy-start | bytes 6148
  1.3 5.1 %copy-start.5 = (f32[4,1,128]{2,1,0:T(1,128)S(1)}, f32[4,1,128]{2,1,0:T(1,128)}, u32[]{:S(2)}) copy-start(f32[4,1,128]{2,1,0:T(1,128)} %param.11) | copy-start | bytes 6148
  1.3 7.9 %collective-permute-start.2 = (s32[1,8]{1,0:T(1,128)S(1)}, s32[1,8]{1,0:T(1,128)S(1)}, u32[]{:S(2)}, u32[]{:S(2)}) collective-permute-start(s32[1,8]{1,0:T(1,128)S(1)} %codes.1.code_ref), channel_id=1, source_target_pairs={{2,0},{5,1},{4,2},{1,3},{6,4},{7,5},{0,6},{3,7},{10,8},{13,9},{12,... | collective-permute-start | bytes 104 | tf_op jit(solution)/shard_map/ppermute | solution.py:464
  6.4 3.0 %collective-permute-start.1 = (s32[1,8]{1,0:T(1,128)S(1)}, s32[1,8]{1,0:T(1,128)S(1)}, u32[]{:S(2)}, u32[]{:S(2)}) collective-permute-start(s32[1,8]{1,0:T(1,128)S(1)} %codes.1.code_ref), channel_id=1, source_target_pairs={{3,0},{6,1},{5,2},{7,3},{0,4},{2,5},{1,6},{4,7},{11,8},{14,9},{13,... | collective-permute-start | bytes 104 | tf_op jit(solution)/shard_map/ppermute | solution.py:464
  6.4 4.4 %collective-permute-start = (s32[1,8]{1,0:T(1,128)S(1)}, s32[1,8]{1,0:T(1,128)S(1)}, u32[]{:S(2)}, u32[]{:S(2)}) collective-permute-start(s32[1,8]{1,0:T(1,128)S(1)} %codes.1.code_ref), channel_id=1, source_target_pairs={{4,0},{7,1},{0,2},{6,3},{1,4},{3,5},{2,6},{5,7},{12,8},{15,9},{8,1... | collective-permute-start | bytes 104 | tf_op jit(solution)/shard_map/ppermute | solution.py:464
  17.7 3.0 %collective-permute-start.3 = (f32[9,128,256]{2,1,0:T(8,128)S(1)}, f32[9,128,256]{2,1,0:T(8,128)S(1)}, u32[]{:S(2)}, u32[]{:S(2)}) collective-permute-start(f32[9,128,256]{2,1,0:T(8,128)S(1)} %far_trees.1.mine_ref), channel_id=1, source_target_pairs={{0,1},{1,0},{2,3},{3,2},{4,5},{5,4},{6,7},{7,6},{8,9},{9,8},{10,11... | collective-permute-start | bytes 3538952 | tf_op jit(solution)/shard_map/ppermute | solution.py:487
  18.0 2.6 %copy-start.3 = (f32[1,2,128,128]{3,2,1,0:T(8,128)S(1)}, f32[1,2,128,128]{3,2,1,0:T(8,128)}, u32[]{:S(2)}) copy-start(f32[1,2,128,128]{3,2,1,0:T(8,128)} %param.13) | copy-start | bytes 393220
  23.7 7.1 %copy-start = (f32[4,128,1024]{2,1,0:T(8,128)S(1)}, f32[4,128,1024]{2,1,0:T(8,128)}, u32[]{:S(2)}) copy-start(f32[4,128,1024]{2,1,0:T(8,128)} %field_ref.1) | copy-start | bytes 6291460
  23.7 5.4 %collective-permute-start.6 = (f32[328,128]{1,0:T(8,128)S(1)}, f32[328,128]{1,0:T(8,128)S(1)}, u32[]{:S(2)}, u32[]{:S(2)}) collective-permute-start(f32[328,128]{1,0:T(8,128)S(1)} %couplings.3), channel_id=1, source_target_pairs={{0,8},{1,17},{2,10},{3,19},{4,12},{5,21},{6,14},{7,23},{8,0},{9,25... | collective-permute-start | bytes 503816 | tf_op jit(solution)/shard_map/ppermute | solution.py:528
  26.4 4.8 %collective-permute-start.4 = (f32[200,128]{1,0:T(8,128)S(1)}, f32[200,128]{1,0:T(8,128)S(1)}, u32[]{:S(2)}, u32[]{:S(2)}) collective-permute-start(f32[200,128]{1,0:T(8,128)S(1)} %couplings.2), channel_id=1, source_target_pairs={{0,8},{1,17},{2,10},{3,19},{4,12},{5,21},{6,14},{7,23},{8,0},{9,25... | collective-permute-start | bytes 307208 | tf_op jit(solution)/shard_map/ppermute | solution.py:528
  29.2 5.4 %collective-permute-start.7 = (f32[328,128]{1,0:T(8,128)S(1)}, f32[328,128]{1,0:T(8,128)S(1)}, u32[]{:S(2)}, u32[]{:S(2)}) collective-permute-start(f32[328,128]{1,0:T(8,128)S(1)} %add.7.mine_ref), channel_id=1, source_target_pairs={{0,16},{1,9},{2,18},{3,11},{4,20},{5,13},{6,22},{7,15},{8,24},{9,1... | collective-permute-start | bytes 503816 | tf_op jit(solution)/shard_map/ppermute | solution.py:528
  31.1 3.5 %copy-start.1 = (s32[8]{0:T(128)S(1)}, s32[8]{0:T(128)}, u32[]{:S(2)}) copy-start(s32[8]{0:T(128)} %prof_ref.3) | copy-start | bytes 100
  31.2 5.0 %collective-permute-start.5 = (f32[200,128]{1,0:T(8,128)S(1)}, f32[200,128]{1,0:T(8,128)S(1)}, u32[]{:S(2)}, u32[]{:S(2)}) collective-permute-start(f32[200,128]{1,0:T(8,128)S(1)} %add.6.mine_ref), channel_id=1, source_target_pairs={{0,16},{1,9},{2,18},{3,11},{4,20},{5,13},{6,22},{7,15},{8,24},{9,1... | collective-permute-start | bytes 307208 | tf_op jit(solution)/shard_map/ppermute | solution.py:528

commit v10 on v9

--- a/solution.py
+++ b/solution.py
@@ -410,8 +410,9 @@
         ch, cl = split(c)
         q = prof_ref[start + j]
         fh, fl = hi_ref[q], lo_ref[q]
-        w = dot(jnp.concatenate([ch, cl], axis=1), jnp.concatenate([fh, fh], axis=0))
-        w = w + dot(ch, fl)
+        w = dot(
+            jnp.concatenate([ch, cl, ch], axis=1), jnp.concatenate([fh, fh, fl], axis=0)
+        )
         i = start + j
         out_ref[i : i + 1] = jnp.sum(
             (fh.astype(F32) + fl.astype(F32)) * w, axis=0, keepdims=True

time: 38.2 us -> 38.1 us (level)
  no operation moved by 1% of the time
where the time goes in v10:
time: 38.1 us; the launch traced here: 37.9 us
  Pallas kernels  21.5 us (56%)
  starting transfers between devices  10.7 us (28%)
  waiting for transfers between devices  4.2 us (11%)
  between operations  0.78 us (2%)
  other arithmetic  0.71 us (2%)
    pallas_call x11, Pallas kernels, call(): pl.pallas_call(kernel, out_shape=outs, in_specs=[spec(kind) for kind in k...  21.5 us
    ppermute x4, starting transfers between devices, exchange(): return lax.ppermute(part, ('wl', 'cell'), pairs_of)  5.25 us
    ppermute x3, starting transfers between devices, body(): lax.ppermute(codes, 'cell', [(block, device) for device, block in enumera...  5.11 us
    ppermute x4, waiting for transfers between devices, exchange(): return lax.ppermute(part, ('wl', 'cell'), pairs_of)  2.53 us
    ppermute x3, waiting for transfers between devices, body(): lax.ppermute(codes, 'cell', [(block, device) for device, block in enumera...  1.66 us
  transfers between devices with their start and end apart: 8, of which 4 were waited for; matrix products, arithmetic and copies ran while one was open for 0% of the time, Pallas kernels for 26%

profile of v10, /device:TPU:0, one launch (start us, length us, event | category | flops | bytes accessed | tf_op | source)
XLA Modules:
  0.0 37.9 jit_solution(13181146623501475035)
XLA Ops:
  0.6 0.7 %or_bitcast_fusion.code_ref = s32[1,8]{1,0:T(1,128)S(1)} fusion(s32[8]{0:T(128)} %param.9, s32[8]{0:T(128)} %prof_ref.3), kind=kLoop, calls=%fused_computation | loop fusion | flops 16 | bytes 96 | tf_op jit(solution)/shard_map/reshape | solution.py:460
  1.3 5.1 %collective-permute-start.2 = (s32[1,8]{1,0:T(1,128)S(1)}, s32[1,8]{1,0:T(1,128)S(1)}, u32[]{:S(2)}, u32[]{:S(2)}) collective-permute-start(s32[1,8]{1,0:T(1,128)S(1)} %codes.1.code_ref), channel_id=1, source_target_pairs={{2,0},{5,1},{4,2},{1,3},{6,4},{7,5},{0,6},{3,7},{10,8},{13,9},{12,... | collective-permute-start | bytes 104 | tf_op jit(solution)/shard_map/ppermute | solution.py:465
  6.4 0.0 collective-permute-start.1
  6.4 0.0 collective-permute-start
  6.4 0.0 copy-done.4
  6.4 0.0 copy-done.5
  6.5 2.7 %own_tree.1 = (bf16[6,3,2,128,256]{4,3,2,1,0:T(8,128)(2,1)S(1)}, f32[3,128,256]{2,1,0:T(8,128)S(1)}, f32[4,2,8,128]{3,2,1,0:T(8,128)S(1)}, f32[4,2,128,128]{3,2,1,0:T(8,128)S(1)}) custom-call(s32[1,8]{1,0:T(1,128)S(1)} %codes.1.code_ref, f32[8,3,2,128,128]{4,3,2,1,0:T(8,128)S(1)} %copy-done.2, f32[4,128]{1,0:T(4,128)S(1)} %copy-done.4, f32[4,128]{1,0:T(4,128)S(1)} %bitcast.7), custom_call_target="tpu_custom_call" | custom-call | flops 2818572288 | bytes 4194304 | tf_op jit(solution)/shard_map/own_tree/pallas_call | solution.py:427
  9.2 0.0 collective-permute-done.2.refs_3_
  9.2 0.2 collective-permute-done.1.refs_2_
  9.4 1.5 %collective-permute-done.refs_1_ = s32[1,8]{1,0:T(1,128)S(1)} collective-permute-done((s32[1,8]{1,0:T(1,128)S(1)}, s32[1,8]{1,0:T(1,128)S(1)}, u32[]{:S(2)}, u32[]{:S(2)}) %collective-permute-start) | collective-permute-done | bytes 64 | tf_op jit(solution)/shard_map/ppermute | solution.py:465
  10.9 6.8 %far_trees.1.mine_ref = f32[9,128,256]{2,1,0:T(8,128)S(1)} custom-call(s32[1]{0:T(128)} %bitcast.refs_0_.me_ref, s32[1,8]{1,0:T(1,128)S(1)} %collective-permute-done.refs_1_, s32[1,8]{1,0:T(1,128)S(1)} %collective-permute-done.1.refs_2_, s32[1,8]{1,0:T(1,128)S(1)} %collective-permute-done.2.refs_3_, f32[8,3,2,128,128]{4,3,2,1,0:T(8,128)S(1)} %copy-done.2, ...), custom_call_target="tpu_custom_call" | custom-call | flops 9663676416 | bytes 4194304 | tf_op jit(solution)/shard_map/far_trees/pallas_call | solution.py:427
  17.7 0.4 collective-permute-start.3
  18.0 2.6 %own_scan.1 = (bf16[2,8,128,256]{3,2,1,0:T(8,128)(2,1)S(1)}, bf16[2,8,128,256]{3,2,1,0:T(8,128)(2,1)S(1)}, bf16[2,8,128,256]{3,2,1,0:T(8,128)(2,1)S(1)}) custom-call(s32[1,8]{1,0:T(1,128)S(1)} %codes.1.code_ref, f32[8,3,2,128,128]{4,3,2,1,0:T(8,128)S(1)} %copy-done.2, f32[4,2,8,128]{3,2,1,0:T(8,128)S(1)} %get-tuple-element.13.refs_5_.row_ref, ...), custom_call_target="tpu_custom_call" | custom-call | flops 2717908992 | bytes 4194304 | tf_op jit(solution)/shard_map/own_scan/pallas_call | solution.py:427
  20.6 0.0 collective-permute-done.3.theirs_ref
  20.7 0.0 copy-done.3
  20.7 1.5 %chain.1 = (bf16[2,2,256,256]{3,2,1,0:T(8,128)(2,1)S(1)}, f32[2,128,256]{2,1,0:T(8,128)S(1)}) custom-call(s32[1]{0:T(128)} %bitcast.refs_0_.me_ref, f32[2,128,128]{2,1,0:T(8,128)S(1)} %bitcast.6, f32[9,128,256]{2,1,0:T(8,128)S(1)} %far_trees.1.mine_ref, f32[9,128,256]{2,1,0:T(8,128)S(1)} %collective-permute-done.3.theirs_ref), custom_call_target="tpu_custom_call" | custom-call | flops 2013265920 | bytes 4194304 | tf_op jit(solution)/shard_map/chain/pallas_call | solution.py:427
  22.2 1.5 %couplings.3 = f32[328,128]{1,0:T(8,128)S(1)} custom-call(bf16[2,2,256,256]{3,2,1,0:T(8,128)(2,1)S(1)} %get-tuple-element.19.x_ref, bf16[2,8,128,256]{3,2,1,0:T(8,128)(2,1)S(1)} %get-tuple-element.21.grown_ref, bf16[2,8,128,256]{3,2,1,0:T(8,128)(2,1)S(1)} %get-tuple-element.22.back_ref, bf16[2,8,128,256]{3,2,1,0:T(8,128)(2,1)S(1)} %get-tuple-element.23.trans_ref), custom_call_target="tpu_custom_call" | custom-call | flops 1006632960 | bytes 4194304 | tf_op jit(solution)/shard_map/couplings/pallas_call | solution.py:427
  23.7 0.0 copy-start
  23.7 1.6 %collective-permute-start.6 = (f32[328,128]{1,0:T(8,128)S(1)}, f32[328,128]{1,0:T(8,128)S(1)}, u32[]{:S(2)}, u32[]{:S(2)}) collective-permute-start(f32[328,128]{1,0:T(8,128)S(1)} %couplings.3), channel_id=1, source_target_pairs={{0,8},{1,17},{2,10},{3,19},{4,12},{5,21},{6,14},{7,23},{8,0},{9,25... | collective-permute-start | bytes 503816 | tf_op jit(solution)/shard_map/ppermute | solution.py:529
  25.3 1.1 %couplings.2 = f32[200,128]{1,0:T(8,128)S(1)} custom-call(bf16[2,2,256,256]{3,2,1,0:T(8,128)(2,1)S(1)} %get-tuple-element.19.x_ref, bf16[2,8,128,256]{3,2,1,0:T(8,128)(2,1)S(1)} %get-tuple-element.21.grown_ref, bf16[2,8,128,256]{3,2,1,0:T(8,128)(2,1)S(1)} %get-tuple-element.22.back_ref, bf16[2,8,128,256]{3,2,1,0:T(8,128)(2,1)S(1)} %get-tuple-element.23.trans_ref), custom_call_target="tpu_custom_call" | custom-call | flops 1006632960 | bytes 4194304 | tf_op jit(solution)/shard_map/couplings/pallas_call | solution.py:427
  26.4 0.6 %collective-permute-start.4 = (f32[200,128]{1,0:T(8,128)S(1)}, f32[200,128]{1,0:T(8,128)S(1)}, u32[]{:S(2)}, u32[]{:S(2)}) collective-permute-start(f32[200,128]{1,0:T(8,128)S(1)} %couplings.2), channel_id=1, source_target_pairs={{0,8},{1,17},{2,10},{3,19},{4,12},{5,21},{6,14},{7,23},{8,0},{9,25... | collective-permute-start | bytes 307208 | tf_op jit(solution)/shard_map/ppermute | solution.py:529
  27.0 2.2 %collective-permute-done.6 = f32[328,128]{1,0:T(8,128)S(1)} collective-permute-done((f32[328,128]{1,0:T(8,128)S(1)}, f32[328,128]{1,0:T(8,128)S(1)}, u32[]{:S(2)}, u32[]{:S(2)}) %collective-permute-start.6) | collective-permute-done | bytes 167968 | tf_op jit(solution)/shard_map/ppermute | solution.py:529
  29.2 1.6 %collective-permute-start.7 = (f32[328,128]{1,0:T(8,128)S(1)}, f32[328,128]{1,0:T(8,128)S(1)}, u32[]{:S(2)}, u32[]{:S(2)}) collective-permute-start(f32[328,128]{1,0:T(8,128)S(1)} %add.7.mine_ref), channel_id=1, source_target_pairs={{0,16},{1,9},{2,18},{3,11},{4,20},{5,13},{6,22},{7,15},{8,24},{9,1... | collective-permute-start | bytes 503816 | tf_op jit(solution)/shard_map/ppermute | solution.py:529
  30.8 0.4 field_parts.1
  31.1 0.0 copy-start.1
  31.2 0.0 collective-permute-done.4
  31.2 1.5 %collective-permute-start.5 = (f32[200,128]{1,0:T(8,128)S(1)}, f32[200,128]{1,0:T(8,128)S(1)}, u32[]{:S(2)}, u32[]{:S(2)}) collective-permute-start(f32[200,128]{1,0:T(8,128)S(1)} %add.6.mine_ref), channel_id=1, source_target_pairs={{0,16},{1,9},{2,18},{3,11},{4,20},{5,13},{6,22},{7,15},{8,24},{9,1... | collective-permute-start | bytes 307208 | tf_op jit(solution)/shard_map/ppermute | solution.py:529
  32.7 1.5 %reflection.1 = f32[2,16,128]{2,1,0:T(8,128)} custom-call(s32[1]{0:T(128)} %bitcast.refs_0_.me_ref, f32[9,128,256]{2,1,0:T(8,128)S(1)} %far_trees.1.mine_ref, f32[9,128,256]{2,1,0:T(8,128)S(1)} %collective-permute-done.3.theirs_ref, f32[2,128,256]{2,1,0:T(8,128)S(1)} %get-tuple-element.16.part_ref), custom_call_target="tpu_custom_call" | custom-call | flops 1006632960 | bytes 4194304 | tf_op jit(solution)/shard_map/reflection/pallas_call | solution.py:427
  34.2 0.4 collective-permute-done.7.theirs_ref
  34.6 1.5 %project.2.rest_0_ = f32[5,1024]{1,0:T(8,128)S(1)} custom-call(s32[8]{0:T(128)S(1)} %copy-done.1, bf16[4,128,1024]{2,1,0:T(8,128)(2,1)S(1)} %get-tuple-element.17.hi_ref, bf16[4,128,1024]{2,1,0:T(8,128)(2,1)S(1)} %get-tuple-element.18.lo_ref, f32[328,128]{1,0:T(8,128)S(1)} %add.7.mine_ref, f32[328,128]{1,0:T(8,128)S(1)} %collective-permute-done.7.theirs_ref), custom_call_target="tpu_custom_call" | custom-call | flops 402653184 | bytes 4194304 | tf_op jit(solution)/shard_map/project/pallas_call | solution.py:427
  36.1 0.0 collective-permute-done.5.theirs_ref
  36.1 1.8 %project.3 = f32[8,1024]{1,0:T(8,128)} custom-call(s32[8]{0:T(128)S(1)} %copy-done.1, bf16[4,128,1024]{2,1,0:T(8,128)(2,1)S(1)} %get-tuple-element.17.hi_ref, bf16[4,128,1024]{2,1,0:T(8,128)(2,1)S(1)} %get-tuple-element.18.lo_ref, f32[200,128]{1,0:T(8,128)S(1)} %add.6.mine_ref, f32[200,128]{1,0:T(8,128)S(1)} %collective-permute-done.5.theirs_ref, ...), custom_call_target="tpu_custom_call" | custom-call | flops 402653184 | bytes 4194304 | tf_op jit(solution)/shard_map/project/pallas_call | solution.py:427
  (10 shorter events, 0.1 us)
Async XLA Ops:
  1.3 5.1 %copy-start.2 = (f32[8,3,2,128,128]{4,3,2,1,0:T(8,128)S(1)}, f32[8,3,2,128,128]{4,3,2,1,0:T(8,128)}, u32[]{:S(2)}) copy-start(f32[8,3,2,128,128]{4,3,2,1,0:T(8,128)} %lib_ref.3) | copy-start | bytes 9437188
  1.3 5.1 %copy-start.4 = (f32[4,128]{1,0:T(4,128)S(1)}, f32[4,128]{1,0:T(4,128)}, u32[]{:S(2)}) copy-start(f32[4,128]{1,0:T(4,128)} %loss_ref.1) | copy-start | bytes 6148
  1.3 5.1 %copy-start.5 = (f32[4,1,128]{2,1,0:T(1,128)S(1)}, f32[4,1,128]{2,1,0:T(1,128)}, u32[]{:S(2)}) copy-start(f32[4,1,128]{2,1,0:T(1,128)} %param.11) | copy-start | bytes 6148
  1.3 7.9 %collective-permute-start.2 = (s32[1,8]{1,0:T(1,128)S(1)}, s32[1,8]{1,0:T(1,128)S(1)}, u32[]{:S(2)}, u32[]{:S(2)}) collective-permute-start(s32[1,8]{1,0:T(1,128)S(1)} %codes.1.code_ref), channel_id=1, source_target_pairs={{2,0},{5,1},{4,2},{1,3},{6,4},{7,5},{0,6},{3,7},{10,8},{13,9},{12,... | collective-permute-start | bytes 104 | tf_op jit(solution)/shard_map/ppermute | solution.py:465
  6.4 3.0 %collective-permute-start.1 = (s32[1,8]{1,0:T(1,128)S(1)}, s32[1,8]{1,0:T(1,128)S(1)}, u32[]{:S(2)}, u32[]{:S(2)}) collective-permute-start(s32[1,8]{1,0:T(1,128)S(1)} %codes.1.code_ref), channel_id=1, source_target_pairs={{3,0},{6,1},{5,2},{7,3},{0,4},{2,5},{1,6},{4,7},{11,8},{14,9},{13,... | collective-permute-start | bytes 104 | tf_op jit(solution)/shard_map/ppermute | solution.py:465
  6.4 4.4 %collective-permute-start = (s32[1,8]{1,0:T(1,128)S(1)}, s32[1,8]{1,0:T(1,128)S(1)}, u32[]{:S(2)}, u32[]{:S(2)}) collective-permute-start(s32[1,8]{1,0:T(1,128)S(1)} %codes.1.code_ref), channel_id=1, source_target_pairs={{4,0},{7,1},{0,2},{6,3},{1,4},{3,5},{2,6},{5,7},{12,8},{15,9},{8,1... | collective-permute-start | bytes 104 | tf_op jit(solution)/shard_map/ppermute | solution.py:465
  17.7 3.0 %collective-permute-start.3 = (f32[9,128,256]{2,1,0:T(8,128)S(1)}, f32[9,128,256]{2,1,0:T(8,128)S(1)}, u32[]{:S(2)}, u32[]{:S(2)}) collective-permute-start(f32[9,128,256]{2,1,0:T(8,128)S(1)} %far_trees.1.mine_ref), channel_id=1, source_target_pairs={{0,1},{1,0},{2,3},{3,2},{4,5},{5,4},{6,7},{7,6},{8,9},{9,8},{10,11... | collective-permute-start | bytes 3538952 | tf_op jit(solution)/shard_map/ppermute | solution.py:488
  18.0 2.6 %copy-start.3 = (f32[1,2,128,128]{3,2,1,0:T(8,128)S(1)}, f32[1,2,128,128]{3,2,1,0:T(8,128)}, u32[]{:S(2)}) copy-start(f32[1,2,128,128]{3,2,1,0:T(8,128)} %param.13) | copy-start | bytes 393220
  23.7 7.1 %copy-start = (f32[4,128,1024]{2,1,0:T(8,128)S(1)}, f32[4,128,1024]{2,1,0:T(8,128)}, u32[]{:S(2)}) copy-start(f32[4,128,1024]{2,1,0:T(8,128)} %field_ref.1) | copy-start | bytes 6291460
  23.7 5.4 %collective-permute-start.6 = (f32[328,128]{1,0:T(8,128)S(1)}, f32[328,128]{1,0:T(8,128)S(1)}, u32[]{:S(2)}, u32[]{:S(2)}) collective-permute-start(f32[328,128]{1,0:T(8,128)S(1)} %couplings.3), channel_id=1, source_target_pairs={{0,8},{1,17},{2,10},{3,19},{4,12},{5,21},{6,14},{7,23},{8,0},{9,25... | collective-permute-start | bytes 503816 | tf_op jit(solution)/shard_map/ppermute | solution.py:529
  26.4 4.8 %collective-permute-start.4 = (f32[200,128]{1,0:T(8,128)S(1)}, f32[200,128]{1,0:T(8,128)S(1)}, u32[]{:S(2)}, u32[]{:S(2)}) collective-permute-start(f32[200,128]{1,0:T(8,128)S(1)} %couplings.2), channel_id=1, source_target_pairs={{0,8},{1,17},{2,10},{3,19},{4,12},{5,21},{6,14},{7,23},{8,0},{9,25... | collective-permute-start | bytes 307208 | tf_op jit(solution)/shard_map/ppermute | solution.py:529
  29.2 5.4 %collective-permute-start.7 = (f32[328,128]{1,0:T(8,128)S(1)}, f32[328,128]{1,0:T(8,128)S(1)}, u32[]{:S(2)}, u32[]{:S(2)}) collective-permute-start(f32[328,128]{1,0:T(8,128)S(1)} %add.7.mine_ref), channel_id=1, source_target_pairs={{0,16},{1,9},{2,18},{3,11},{4,20},{5,13},{6,22},{7,15},{8,24},{9,1... | collective-permute-start | bytes 503816 | tf_op jit(solution)/shard_map/ppermute | solution.py:529
  31.1 3.5 %copy-start.1 = (s32[8]{0:T(128)S(1)}, s32[8]{0:T(128)}, u32[]{:S(2)}) copy-start(s32[8]{0:T(128)} %prof_ref.3) | copy-start | bytes 100
  31.2 4.9 %collective-permute-start.5 = (f32[200,128]{1,0:T(8,128)S(1)}, f32[200,128]{1,0:T(8,128)S(1)}, u32[]{:S(2)}, u32[]{:S(2)}) collective-permute-start(f32[200,128]{1,0:T(8,128)S(1)} %add.6.mine_ref), channel_id=1, source_target_pairs={{0,16},{1,9},{2,18},{3,11},{4,20},{5,13},{6,22},{7,15},{8,24},{9,1... | collective-permute-start | bytes 307208 | tf_op jit(solution)/shard_map/ppermute | solution.py:529

commit v11 on v9

--- a/solution.py
+++ b/solution.py
@@ -218,7 +218,7 @@
         for device, block in enumerate(source):
             wanted[block].discard(device)
         found.append(source)
-    return found
+    return found[::-1]
 
 
 def far_kernel(*refs):

time: 38.2 us -> 39 us (1.021)
  starting transfers between devices: 10.7 us -> 13 us
  waiting for transfers between devices: 4.19 us -> 2.76 us
    ppermute x3, starting transfers between devices: 5.11 us -> 7.64 us  [body(): lax.ppermute(codes, 'cell', [(block, device) for device, block in enumera...]
    ppermute x3, waiting for transfers between devices: 1.66 us -> 0.01 us  [body(): lax.ppermute(codes, 'cell', [(block, device) for device, block in enumera...]
  transfers between devices with their start and end apart: 8 -> 8, of which waited for: 4 -> 3; matrix products, arithmetic and copies ran while one was open for 0% -> 0% of each run, Pallas kernels for 26% -> 25%
where the time goes in v11:
time: 39 us; the launch traced here: 38.8 us
  Pallas kernels  21.5 us (55%)
  starting transfers between devices  13 us (33%)
  waiting for transfers between devices  2.76 us (7%)
  between operations  0.78 us (2%)
  other arithmetic  0.71 us (2%)
    pallas_call x11, Pallas kernels, call(): pl.pallas_call(kernel, out_shape=outs, in_specs=[spec(kind) for kind in k...  21.5 us
    ppermute x3, starting transfers between devices, body(): lax.ppermute(codes, 'cell', [(block, device) for device, block in enumera...  7.64 us
    ppermute x4, starting transfers between devices, exchange(): return lax.ppermute(part, ('wl', 'cell'), pairs_of)  5.25 us
    ppermute x4, waiting for transfers between devices, exchange(): return lax.ppermute(part, ('wl', 'cell'), pairs_of)  2.53 us
  transfers between devices with their start and end apart: 8, of which 3 were waited for; matrix products, arithmetic and copies ran while one was open for 0% of the time, Pallas kernels for 25%

profile of v11, /device:TPU:0, one launch (start us, length us, event | category | flops | bytes accessed | tf_op | source)
XLA Modules:
  0.0 38.8 jit_solution(7060872619236342255)
XLA Ops:
  0.6 0.7 %or_bitcast_fusion.code_ref = s32[1,8]{1,0:T(1,128)S(1)} fusion(s32[8]{0:T(128)} %param.9, s32[8]{0:T(128)} %prof_ref.3), kind=kLoop, calls=%fused_computation | loop fusion | flops 16 | bytes 96 | tf_op jit(solution)/shard_map/reshape | solution.py:459
  1.3 3.1 %collective-permute-start.2 = (s32[1,8]{1,0:T(1,128)S(1)}, s32[1,8]{1,0:T(1,128)S(1)}, u32[]{:S(2)}, u32[]{:S(2)}) collective-permute-start(s32[1,8]{1,0:T(1,128)S(1)} %codes.1.code_ref), channel_id=1, source_target_pairs={{4,0},{7,1},{0,2},{6,3},{1,4},{3,5},{2,6},{5,7},{12,8},{15,9},{8,1... | collective-permute-start | bytes 104 | tf_op jit(solution)/shard_map/ppermute | solution.py:464
  4.4 1.1 %collective-permute-start.1 = (s32[1,8]{1,0:T(1,128)S(1)}, s32[1,8]{1,0:T(1,128)S(1)}, u32[]{:S(2)}, u32[]{:S(2)}) collective-permute-start(s32[1,8]{1,0:T(1,128)S(1)} %codes.1.code_ref), channel_id=1, source_target_pairs={{3,0},{6,1},{5,2},{7,3},{0,4},{2,5},{1,6},{4,7},{11,8},{14,9},{13,... | collective-permute-start | bytes 104 | tf_op jit(solution)/shard_map/ppermute | solution.py:464
  5.5 3.5 %collective-permute-start = (s32[1,8]{1,0:T(1,128)S(1)}, s32[1,8]{1,0:T(1,128)S(1)}, u32[]{:S(2)}, u32[]{:S(2)}) collective-permute-start(s32[1,8]{1,0:T(1,128)S(1)} %codes.1.code_ref), channel_id=1, source_target_pairs={{2,0},{5,1},{4,2},{1,3},{6,4},{7,5},{0,6},{3,7},{10,8},{13,9},{12,... | collective-permute-start | bytes 104 | tf_op jit(solution)/shard_map/ppermute | solution.py:464
  9.0 0.0 copy-done.2
  9.0 2.7 %own_tree.1 = (bf16[6,3,2,128,256]{4,3,2,1,0:T(8,128)(2,1)S(1)}, f32[3,128,256]{2,1,0:T(8,128)S(1)}, f32[4,2,8,128]{3,2,1,0:T(8,128)S(1)}, f32[4,2,128,128]{3,2,1,0:T(8,128)S(1)}) custom-call(s32[1,8]{1,0:T(1,128)S(1)} %codes.1.code_ref, f32[8,3,2,128,128]{4,3,2,1,0:T(8,128)S(1)} %copy-done.2, f32[4,128]{1,0:T(4,128)S(1)} %copy-done.4, f32[4,128]{1,0:T(4,128)S(1)} %bitcast.7), custom_call_target="tpu_custom_call" | custom-call | flops 2818572288 | bytes 4194304 | tf_op jit(solution)/shard_map/own_tree/pallas_call | solution.py:426
  11.7 0.0 collective-permute-done.2.refs_3_
  11.7 0.0 collective-permute-done.1.refs_2_
  11.7 0.0 collective-permute-done.refs_1_
  11.8 6.8 %far_trees.1.mine_ref = f32[9,128,256]{2,1,0:T(8,128)S(1)} custom-call(s32[1]{0:T(128)} %bitcast.refs_0_.me_ref, s32[1,8]{1,0:T(1,128)S(1)} %collective-permute-done.refs_1_, s32[1,8]{1,0:T(1,128)S(1)} %collective-permute-done.1.refs_2_, s32[1,8]{1,0:T(1,128)S(1)} %collective-permute-done.2.refs_3_, f32[8,3,2,128,128]{4,3,2,1,0:T(8,128)S(1)} %copy-done.2, ...), custom_call_target="tpu_custom_call" | custom-call | flops 9663676416 | bytes 4194304 | tf_op jit(solution)/shard_map/far_trees/pallas_call | solution.py:426
  18.6 0.1 collective-permute-start.3
  18.6 0.0 copy-start.3
  18.6 2.6 %own_scan.1 = (bf16[2,8,128,256]{3,2,1,0:T(8,128)(2,1)S(1)}, bf16[2,8,128,256]{3,2,1,0:T(8,128)(2,1)S(1)}, bf16[2,8,128,256]{3,2,1,0:T(8,128)(2,1)S(1)}) custom-call(s32[1,8]{1,0:T(1,128)S(1)} %codes.1.code_ref, f32[8,3,2,128,128]{4,3,2,1,0:T(8,128)S(1)} %copy-done.2, f32[4,2,8,128]{3,2,1,0:T(8,128)S(1)} %get-tuple-element.13.refs_5_.row_ref, ...), custom_call_target="tpu_custom_call" | custom-call | flops 2717908992 | bytes 4194304 | tf_op jit(solution)/shard_map/own_scan/pallas_call | solution.py:426
  21.3 0.2 collective-permute-done.3.theirs_ref
  21.5 1.5 %chain.1 = (bf16[2,2,256,256]{3,2,1,0:T(8,128)(2,1)S(1)}, f32[2,128,256]{2,1,0:T(8,128)S(1)}) custom-call(s32[1]{0:T(128)} %bitcast.refs_0_.me_ref, f32[2,128,128]{2,1,0:T(8,128)S(1)} %bitcast.6, f32[9,128,256]{2,1,0:T(8,128)S(1)} %far_trees.1.mine_ref, f32[9,128,256]{2,1,0:T(8,128)S(1)} %collective-permute-done.3.theirs_ref), custom_call_target="tpu_custom_call" | custom-call | flops 2013265920 | bytes 4194304 | tf_op jit(solution)/shard_map/chain/pallas_call | solution.py:426
  23.0 1.5 %couplings.3 = f32[328,128]{1,0:T(8,128)S(1)} custom-call(bf16[2,2,256,256]{3,2,1,0:T(8,128)(2,1)S(1)} %get-tuple-element.19.x_ref, bf16[2,8,128,256]{3,2,1,0:T(8,128)(2,1)S(1)} %get-tuple-element.21.grown_ref, bf16[2,8,128,256]{3,2,1,0:T(8,128)(2,1)S(1)} %get-tuple-element.22.back_ref, bf16[2,8,128,256]{3,2,1,0:T(8,128)(2,1)S(1)} %get-tuple-element.23.trans_ref), custom_call_target="tpu_custom_call" | custom-call | flops 1006632960 | bytes 4194304 | tf_op jit(solution)/shard_map/couplings/pallas_call | solution.py:426
  24.5 0.0 copy-start
  24.5 1.6 %collective-permute-start.6 = (f32[328,128]{1,0:T(8,128)S(1)}, f32[328,128]{1,0:T(8,128)S(1)}, u32[]{:S(2)}, u32[]{:S(2)}) collective-permute-start(f32[328,128]{1,0:T(8,128)S(1)} %couplings.3), channel_id=1, source_target_pairs={{0,8},{1,17},{2,10},{3,19},{4,12},{5,21},{6,14},{7,23},{8,0},{9,25... | collective-permute-start | bytes 503816 | tf_op jit(solution)/shard_map/ppermute | solution.py:528
  26.1 1.1 %couplings.2 = f32[200,128]{1,0:T(8,128)S(1)} custom-call(bf16[2,2,256,256]{3,2,1,0:T(8,128)(2,1)S(1)} %get-tuple-element.19.x_ref, bf16[2,8,128,256]{3,2,1,0:T(8,128)(2,1)S(1)} %get-tuple-element.21.grown_ref, bf16[2,8,128,256]{3,2,1,0:T(8,128)(2,1)S(1)} %get-tuple-element.22.back_ref, bf16[2,8,128,256]{3,2,1,0:T(8,128)(2,1)S(1)} %get-tuple-element.23.trans_ref), custom_call_target="tpu_custom_call" | custom-call | flops 1006632960 | bytes 4194304 | tf_op jit(solution)/shard_map/couplings/pallas_call | solution.py:426
  27.2 0.6 %collective-permute-start.4 = (f32[200,128]{1,0:T(8,128)S(1)}, f32[200,128]{1,0:T(8,128)S(1)}, u32[]{:S(2)}, u32[]{:S(2)}) collective-permute-start(f32[200,128]{1,0:T(8,128)S(1)} %couplings.2), channel_id=1, source_target_pairs={{0,8},{1,17},{2,10},{3,19},{4,12},{5,21},{6,14},{7,23},{8,0},{9,25... | collective-permute-start | bytes 307208 | tf_op jit(solution)/shard_map/ppermute | solution.py:528
  27.8 2.2 %collective-permute-done.6 = f32[328,128]{1,0:T(8,128)S(1)} collective-permute-done((f32[328,128]{1,0:T(8,128)S(1)}, f32[328,128]{1,0:T(8,128)S(1)}, u32[]{:S(2)}, u32[]{:S(2)}) %collective-permute-start.6) | collective-permute-done | bytes 167968 | tf_op jit(solution)/shard_map/ppermute | solution.py:528
  30.0 1.6 %collective-permute-start.7 = (f32[328,128]{1,0:T(8,128)S(1)}, f32[328,128]{1,0:T(8,128)S(1)}, u32[]{:S(2)}, u32[]{:S(2)}) collective-permute-start(f32[328,128]{1,0:T(8,128)S(1)} %add.7.mine_ref), channel_id=1, source_target_pairs={{0,16},{1,9},{2,18},{3,11},{4,20},{5,13},{6,22},{7,15},{8,24},{9,1... | collective-permute-start | bytes 503816 | tf_op jit(solution)/shard_map/ppermute | solution.py:528
  31.6 0.0 copy-done
  31.6 0.4 field_parts.1
  31.9 0.0 copy-start.1
  32.0 0.0 collective-permute-done.4
  32.0 1.5 %collective-permute-start.5 = (f32[200,128]{1,0:T(8,128)S(1)}, f32[200,128]{1,0:T(8,128)S(1)}, u32[]{:S(2)}, u32[]{:S(2)}) collective-permute-start(f32[200,128]{1,0:T(8,128)S(1)} %add.6.mine_ref), channel_id=1, source_target_pairs={{0,16},{1,9},{2,18},{3,11},{4,20},{5,13},{6,22},{7,15},{8,24},{9,1... | collective-permute-start | bytes 307208 | tf_op jit(solution)/shard_map/ppermute | solution.py:528
  33.5 1.5 %reflection.1 = f32[2,16,128]{2,1,0:T(8,128)} custom-call(s32[1]{0:T(128)} %bitcast.refs_0_.me_ref, f32[9,128,256]{2,1,0:T(8,128)S(1)} %far_trees.1.mine_ref, f32[9,128,256]{2,1,0:T(8,128)S(1)} %collective-permute-done.3.theirs_ref, f32[2,128,256]{2,1,0:T(8,128)S(1)} %get-tuple-element.16.part_ref), custom_call_target="tpu_custom_call" | custom-call | flops 1006632960 | bytes 4194304 | tf_op jit(solution)/shard_map/reflection/pallas_call | solution.py:426
  35.0 0.4 collective-permute-done.7.theirs_ref
  35.4 1.5 %project.2.rest_0_ = f32[5,1024]{1,0:T(8,128)S(1)} custom-call(s32[8]{0:T(128)S(1)} %copy-done.1, bf16[4,128,1024]{2,1,0:T(8,128)(2,1)S(1)} %get-tuple-element.17.hi_ref, bf16[4,128,1024]{2,1,0:T(8,128)(2,1)S(1)} %get-tuple-element.18.lo_ref, f32[328,128]{1,0:T(8,128)S(1)} %add.7.mine_ref, f32[328,128]{1,0:T(8,128)S(1)} %collective-permute-done.7.theirs_ref), custom_call_target="tpu_custom_call" | custom-call | flops 402653184 | bytes 4194304 | tf_op jit(solution)/shard_map/project/pallas_call | solution.py:426
  36.9 0.0 collective-permute-done.5.theirs_ref
  37.0 1.8 %project.3 = f32[8,1024]{1,0:T(8,128)} custom-call(s32[8]{0:T(128)S(1)} %copy-done.1, bf16[4,128,1024]{2,1,0:T(8,128)(2,1)S(1)} %get-tuple-element.17.hi_ref, bf16[4,128,1024]{2,1,0:T(8,128)(2,1)S(1)} %get-tuple-element.18.lo_ref, f32[200,128]{1,0:T(8,128)S(1)} %add.6.mine_ref, f32[200,128]{1,0:T(8,128)S(1)} %collective-permute-done.5.theirs_ref, ...), custom_call_target="tpu_custom_call" | custom-call | flops 402653184 | bytes 4194304 | tf_op jit(solution)/shard_map/project/pallas_call | solution.py:426
  (10 shorter events, 0.1 us)
Async XLA Ops:
  1.3 7.7 %copy-start.2 = (f32[8,3,2,128,128]{4,3,2,1,0:T(8,128)S(1)}, f32[8,3,2,128,128]{4,3,2,1,0:T(8,128)}, u32[]{:S(2)}) copy-start(f32[8,3,2,128,128]{4,3,2,1,0:T(8,128)} %lib_ref.3) | copy-start | bytes 9437188
  1.3 7.7 %copy-start.4 = (f32[4,128]{1,0:T(4,128)S(1)}, f32[4,128]{1,0:T(4,128)}, u32[]{:S(2)}) copy-start(f32[4,128]{1,0:T(4,128)} %loss_ref.1) | copy-start | bytes 6148
  1.3 7.7 %copy-start.5 = (f32[4,1,128]{2,1,0:T(1,128)S(1)}, f32[4,1,128]{2,1,0:T(1,128)}, u32[]{:S(2)}) copy-start(f32[4,1,128]{2,1,0:T(1,128)} %param.11) | copy-start | bytes 6148
  1.3 10.4 %collective-permute-start.2 = (s32[1,8]{1,0:T(1,128)S(1)}, s32[1,8]{1,0:T(1,128)S(1)}, u32[]{:S(2)}, u32[]{:S(2)}) collective-permute-start(s32[1,8]{1,0:T(1,128)S(1)} %codes.1.code_ref), channel_id=1, source_target_pairs={{4,0},{7,1},{0,2},{6,3},{1,4},{3,5},{2,6},{5,7},{12,8},{15,9},{8,1... | collective-permute-start | bytes 104 | tf_op jit(solution)/shard_map/ppermute | solution.py:464
  4.4 7.3 %collective-permute-start.1 = (s32[1,8]{1,0:T(1,128)S(1)}, s32[1,8]{1,0:T(1,128)S(1)}, u32[]{:S(2)}, u32[]{:S(2)}) collective-permute-start(s32[1,8]{1,0:T(1,128)S(1)} %codes.1.code_ref), channel_id=1, source_target_pairs={{3,0},{6,1},{5,2},{7,3},{0,4},{2,5},{1,6},{4,7},{11,8},{14,9},{13,... | collective-permute-start | bytes 104 | tf_op jit(solution)/shard_map/ppermute | solution.py:464
  5.5 6.3 %collective-permute-start = (s32[1,8]{1,0:T(1,128)S(1)}, s32[1,8]{1,0:T(1,128)S(1)}, u32[]{:S(2)}, u32[]{:S(2)}) collective-permute-start(s32[1,8]{1,0:T(1,128)S(1)} %codes.1.code_ref), channel_id=1, source_target_pairs={{2,0},{5,1},{4,2},{1,3},{6,4},{7,5},{0,6},{3,7},{10,8},{13,9},{12,... | collective-permute-start | bytes 104 | tf_op jit(solution)/shard_map/ppermute | solution.py:464
  18.6 2.9 %collective-permute-start.3 = (f32[9,128,256]{2,1,0:T(8,128)S(1)}, f32[9,128,256]{2,1,0:T(8,128)S(1)}, u32[]{:S(2)}, u32[]{:S(2)}) collective-permute-start(f32[9,128,256]{2,1,0:T(8,128)S(1)} %far_trees.1.mine_ref), channel_id=1, source_target_pairs={{0,1},{1,0},{2,3},{3,2},{4,5},{5,4},{6,7},{7,6},{8,9},{9,8},{10,11... | collective-permute-start | bytes 3538952 | tf_op jit(solution)/shard_map/ppermute | solution.py:487
  18.6 2.8 %copy-start.3 = (f32[1,2,128,128]{3,2,1,0:T(8,128)S(1)}, f32[1,2,128,128]{3,2,1,0:T(8,128)}, u32[]{:S(2)}) copy-start(f32[1,2,128,128]{3,2,1,0:T(8,128)} %param.13) | copy-start | bytes 393220
  24.5 7.1 %copy-start = (f32[4,128,1024]{2,1,0:T(8,128)S(1)}, f32[4,128,1024]{2,1,0:T(8,128)}, u32[]{:S(2)}) copy-start(f32[4,128,1024]{2,1,0:T(8,128)} %field_ref.1) | copy-start | bytes 6291460
  24.5 5.4 %collective-permute-start.6 = (f32[328,128]{1,0:T(8,128)S(1)}, f32[328,128]{1,0:T(8,128)S(1)}, u32[]{:S(2)}, u32[]{:S(2)}) collective-permute-start(f32[328,128]{1,0:T(8,128)S(1)} %couplings.3), channel_id=1, source_target_pairs={{0,8},{1,17},{2,10},{3,19},{4,12},{5,21},{6,14},{7,23},{8,0},{9,25... | collective-permute-start | bytes 503816 | tf_op jit(solution)/shard_map/ppermute | solution.py:528
  27.2 4.8 %collective-permute-start.4 = (f32[200,128]{1,0:T(8,128)S(1)}, f32[200,128]{1,0:T(8,128)S(1)}, u32[]{:S(2)}, u32[]{:S(2)}) collective-permute-start(f32[200,128]{1,0:T(8,128)S(1)} %couplings.2), channel_id=1, source_target_pairs={{0,8},{1,17},{2,10},{3,19},{4,12},{5,21},{6,14},{7,23},{8,0},{9,25... | collective-permute-start | bytes 307208 | tf_op jit(solution)/shard_map/ppermute | solution.py:528
  30.0 5.4 %collective-permute-start.7 = (f32[328,128]{1,0:T(8,128)S(1)}, f32[328,128]{1,0:T(8,128)S(1)}, u32[]{:S(2)}, u32[]{:S(2)}) collective-permute-start(f32[328,128]{1,0:T(8,128)S(1)} %add.7.mine_ref), channel_id=1, source_target_pairs={{0,16},{1,9},{2,18},{3,11},{4,20},{5,13},{6,22},{7,15},{8,24},{9,1... | collective-permute-start | bytes 503816 | tf_op jit(solution)/shard_map/ppermute | solution.py:528
  31.9 3.5 %copy-start.1 = (s32[8]{0:T(128)S(1)}, s32[8]{0:T(128)}, u32[]{:S(2)}) copy-start(s32[8]{0:T(128)} %prof_ref.3) | copy-start | bytes 100
  32.0 5.0 %collective-permute-start.5 = (f32[200,128]{1,0:T(8,128)S(1)}, f32[200,128]{1,0:T(8,128)S(1)}, u32[]{:S(2)}, u32[]{:S(2)}) collective-permute-start(f32[200,128]{1,0:T(8,128)S(1)} %add.6.mine_ref), channel_id=1, source_target_pairs={{0,16},{1,9},{2,18},{3,11},{4,20},{5,13},{6,22},{7,15},{8,24},{9,1... | collective-permute-start | bytes 307208 | tf_op jit(solution)/shard_map/ppermute | solution.py:528
